TPU v7x, 32 devices: a whole 2x2x4 slice. The times are simulated.
32 devices in a mesh: groups: 2 (over x), gx: 16 (over z, y, core).
Axes of the slice: x: 2, y: 2, z: 4, core: 2. Of those that a mesh axis runs over, the one named last changes fastest.
Arguments:
- volume: bfloat16 [32, 256, 6, 128], P('groups', 'gx'), parts along dimension 0, may hold values from -6 to 6
- conv_weight: bfloat16 [256, 27, 128], P('gx'), may hold values from -0.078125 to 0.078125
- conv_bias: float32 [128], replicated, may hold values from -3 to 3
- tconv_weight: bfloat16 [27, 64, 128], replicated, may hold values from -0.25 to 0.25
Outputs:
- decoded: bfloat16 [64, 64, 12, 256], P(('groups', 'gx')), parts along dimension 0
There are 2 independent parts, one for each index of `groups`. A program takes and returns all parts, laid end to end along the dimension named above; an argument that names none is the same for every part. Nothing has to cross between parts.
All inputs are finite; a program needn't handle non-finite values.
Results may differ from a plain program's by a relative error of at most 0.005.
Values may be sent and summed in bfloat16 or wider, within the bound.
No kernel may reach another device: no remote copies, remote signals or barrier semaphores. Data moves between devices by JAX's collectives and lax.ppermute only.
A program may use at most 64 MiB of HBM per device.

v0:
```python
import jax
import jax.numpy as jnp
from jax import lax
from jax.sharding import PartitionSpec as P


def extended(block, sides, width):
    for axis, dim in sides:
        count = lax.axis_size(axis)
        forward = [(i, i + 1) for i in range(count - 1)]
        backward = [(target, source) for source, target in forward]
        low = lax.ppermute(
            lax.slice_in_dim(block, block.shape[dim] - width, None, axis=dim), axis, forward
        )
        high = lax.ppermute(lax.slice_in_dim(block, 0, width, axis=dim), axis, backward)
        block = jnp.concatenate([low, block, high], axis=dim)
    return block


def from_behind(block, axis, distance):
    devices = range(lax.axis_size(axis))
    route = [(i - distance, i) for i in devices if i - distance in devices]
    return lax.ppermute(block, axis, route)


def next_cell(field, axis):
    size = field.shape[axis]
    rest = lax.slice_in_dim(field, 1, size, axis=axis)
    zero_shape = list(field.shape)
    zero_shape[axis] = 1
    return jnp.concatenate([rest, jnp.zeros(zero_shape, field.dtype)], axis=axis)


def yz_classes(products, tap_x):
    layout_options = (((1, False),), ((2, False), (0, True)))
    parity_classes = []
    for par_y in range(2):
        for par_z in range(2):
            total = jnp.zeros(products.shape[:1] + products.shape[4:], jnp.float32)
            for tap_y, shift_y in layout_options[par_y]:
                for tap_z, shift_z in layout_options[par_z]:
                    term = products[:, tap_x, tap_y, tap_z]
                    if shift_y:
                        term = next_cell(term, 2)
                    if shift_z:
                        term = next_cell(term, 3)
                    total = total + term
            parity_classes.append(total)
    return jnp.stack(parity_classes, axis=0)


def alternate(even, odd):
    both = jnp.stack([even, odd], axis=0)
    rows, chans, wide_y, wide_z = (both.shape[2], both.shape[3], both.shape[4], both.shape[5])
    both = both.reshape(2, 2, 2, rows, chans, wide_y, wide_z)
    both = jnp.transpose(both, (3, 0, 4, 5, 1, 6, 2))
    return both.reshape(2 * rows, chans, 2 * wide_y, 2 * wide_z)


def conv_rows(block, weight, count):
    chans, wide_y, wide_z = (block.shape[1], block.shape[2] - 2, block.shape[3] - 2)
    taps = []
    for tap_x in range(3):
        for tap_y in range(3):
            for tap_z in range(3):
                taps.append(
                    block[tap_x : tap_x + count, :, tap_y : tap_y + wide_y, tap_z : tap_z + wide_z]
                )
    patch_columns = jnp.stack(taps, axis=2).reshape(count, chans * 27, wide_y * wide_z)
    flattened_patches = weight.reshape(chans * 27, weight.shape[2])
    output_volume = jnp.einsum(
        "fwh,wb->fbh", patch_columns, flattened_patches, preferred_element_type=jnp.float32
    )
    return output_volume.reshape(count, weight.shape[2], wide_y, wide_z)


def tap_products(hidden, flattened_patches, cup):
    rows, wide_y, wide_z = (hidden.shape[0], hidden.shape[2], hidden.shape[3])
    products = jnp.einsum(
        "oc,ncyz->noyz", flattened_patches, hidden, preferred_element_type=jnp.float32
    )
    return products.reshape(rows, 3, 3, 3, cup, wide_y, wide_z)


def per_device(volume, conv_weight, conv_bias, tconv_weight):
    wide_x, wide_y, wide_z = (volume.shape[0], volume.shape[2], volume.shape[3])
    rows = wide_x // lax.axis_size("gx")
    cout = conv_weight.shape[2]
    local = lax.all_to_all(volume, "gx", split_axis=0, concat_axis=1, tiled=True)
    widened_volume = extended(local, (("gx", 0),), 1)
    padded_volume = jnp.pad(widened_volume, ((0, 0), (0, 0), (1, 1), (1, 1)))
    summed = conv_rows(padded_volume, lax.all_gather(conv_weight, "gx", axis=0, tiled=True), rows)
    hidden = jnp.maximum(summed + conv_bias[None, :, None, None], 0.0).astype(jnp.bfloat16)
    cup = tconv_weight.shape[1]
    flattened_patches = tconv_weight.reshape(27 * cup, cout)
    products = tap_products(hidden, flattened_patches, cup)
    first = yz_classes(products, 0)
    middle = yz_classes(products, 1)
    last = yz_classes(products, 2)
    edge = from_behind(hidden, "gx", -1)
    leading_edge = yz_classes(tap_products(edge, flattened_patches, cup), 0)
    following = jnp.concatenate([first[:, 1:], leading_edge], axis=1)
    odd = last + following
    return alternate(middle, odd).astype(jnp.bfloat16)


def solution(mesh):
    return jax.shard_map(
        per_device,
        mesh=mesh,
        in_specs=(P("groups", "gx", None, None), P("gx", None, None), P(), P()),
        out_specs=P(("groups", "gx"), None, None, None),
        check_vma=False,
    )
```

profile of v0, /device:TPU:5, one launch (start us, length us, event | category | flops | bytes accessed | tf_op | source)
XLA Modules:
  0.0 140.1 jit_solution(13895225849409607237)
XLA Ops:
  6.5 17.9 %all_to_all.12 = bf16[16,16,6,128]{3,1,2,0:T(8,128)(2,1)S(1)} all-to-all(bf16[16,16,6,128]{3,1,2,0:T(8,128)(2,1)} %param.4), channel_id=1, replica_groups=mesh['groups'=2,'gx'=16] {'gx'}, dimensions={0} | all-to-all | bytes 786432 | tf_op jit(solution)/shard_map/all_to_all | solution.py:89
  24.4 3.2 %collective-permute-start = (bf16[1,256,6,128]{3,1,2,0:T(8,128)(2,1)S(1)}, bf16[1,256,6,128]{3,1,2,0:T(8,128)(2,1)S(1)}, u32[]{:S(2)}, u32[]{:S(2)}) collective-permute-start(bf16[1,256,6,128]{3,1,2,0:T(8,128)(2,1)S(1)} %bitcast.296), channel_id=1, source_target_pairs={{0,1},{1,2},{2,3},{3,4},{4,5},{5,6},{6,7},{7,8},{8,9},{9,10},{10,1... | collective-permute-start | bytes 1179656 | tf_op jit(solution)/shard_map/ppermute | solution.py:12
  27.7 1.9 %collective-permute-start.1 = (bf16[1,256,6,128]{3,1,2,0:T(8,128)(2,1)S(1)}, bf16[1,256,6,128]{3,1,2,0:T(8,128)(2,1)S(1)}, u32[]{:S(2)}, u32[]{:S(2)}) collective-permute-start(bf16[1,256,6,128]{3,1,2,0:T(8,128)(2,1)S(1)} %bitcast.297), channel_id=1, source_target_pairs={{1,0},{2,1},{3,2},{4,3},{5,4},{6,5},{7,6},{8,7},{9,8},{10,9},{11,1... | collective-permute-start | bytes 1179656 | tf_op jit(solution)/shard_map/ppermute | solution.py:15
  29.6 2.8 %collective-permute-done = bf16[1,256,6,128]{3,1,2,0:T(8,128)(2,1)S(1)} collective-permute-done((bf16[1,256,6,128]{3,1,2,0:T(8,128)(2,1)S(1)}, bf16[1,256,6,128]{3,1,2,0:T(8,128)(2,1)S(1)}, u32[]{:S(2)}, u32[]{:S(2)}) %collective-permute-start) | collective-permute-done | bytes 393248 | tf_op jit(solution)/shard_map/ppermute | solution.py:12
  32.4 5.3 %collective-permute-done.1 = bf16[1,256,6,128]{3,1,2,0:T(8,128)(2,1)S(1)} collective-permute-done((bf16[1,256,6,128]{3,1,2,0:T(8,128)(2,1)S(1)}, bf16[1,256,6,128]{3,1,2,0:T(8,128)(2,1)S(1)}, u32[]{:S(2)}, u32[]{:S(2)}) %collective-permute-start.1) | collective-permute-done | bytes 393248 | tf_op jit(solution)/shard_map/ppermute | solution.py:15
  37.7 1.7 %select_maximum_fusion = bf16[3,256,8,130]{3,1,2,0:T(8,128)(2,1)S(1)} fusion(bf16[1,256,6,128]{3,1,2,0:T(8,128)(2,1)S(1)} %collective-permute-done.1, bf16[1,256,6,128]{3,1,2,0:T(8,128)(2,1)S(1)} %bitcast.298, bf16[1,256,6,128]{3,1,2,0:T(8,128)(2,1)S(1)} %collective-permute-done), kind=kLoop, calls=%fused_computation.8 | loop fusion | flops 15175680 | bytes 2777088 | tf_op jit(solution)/shard_map/concatenate | solution.py:16
  39.7 0.2 fusion.30
  40.5 0.2 fusion.26
  40.7 0.2 fusion.25
  42.3 0.2 fusion.17
  42.9 0.2 fusion.14
  44.2 43.2 %copy.129 = bf16[1,256,27,6,128]{4,3,2,1,0:T(8,128)(2,1)S(1)} copy(bf16[1,256,27,6,128]{4,1,3,2,0:T(8,128)(2,1)S(1)} %fusion.9) | data formatting | bytes 21233664 | tf_op jit(solution)/shard_map/stack | solution.py:69
  87.3 6.4 %copy.252 = bf16[864,8,6,128]{3,1,2,0:T(8,128)(2,1)} copy(bf16[864,8,6,128]{3,2,1,0:T(8,128)(2,1)S(1)} %bitcast.288) | data formatting | bytes 21233664
  93.8 13.9 %copy.130 = bf16[768,6912]{1,0:T(8,128)(2,1)} copy(bf16[768,6912]{0,1:T(8,128)(2,1)} %bitcast.289) | data formatting | bytes 21233664 | tf_op jit(solution)/shard_map/fwh,wb->fbh/dot_general | solution.py:71
  107.7 2.7 %copy.131 = bf16[256,27,128]{2,1,0:T(8,128)(2,1)S(1)} copy(bf16[256,27,128]{2,0,1:T(8,128)(2,1)} %all-gather.2.cloned.1.call-done) | data formatting | bytes 3538944 | tf_op jit(solution)/shard_map/all_gather | solution.py:92
  110.3 1.6 %reshape.119 = bf16[6912,128,1]{1,0,2:T(8,128)(2,1)} reshape(bf16[256,27,128]{2,1,0:T(8,128)(2,1)S(1)} %copy.131) | data formatting | bytes 3538944 | tf_op jit(solution)/shard_map/reshape | solution.py:70
  111.9 7.4 %fusion.7 = bf16[6,128,128]{2,1,0:T(8,128)(2,1)S(1)} fusion(bf16[6,128,6912]{2,1,0:T(8,128)(2,1)} %bitcast.292, bf16[6912,128,1]{1,0,2:T(8,128)(2,1)} %reshape.119, f32[128]{0:T(128)S(1)} %copy-done.1), kind=kOutput, calls=%fused_computation.15 | convolution fusion | flops 1359249408 | bytes 12583424 | tf_op jit(solution)/shard_map/fwh,wb->fbh/dot_general | solution.py:71
  119.3 0.9 fusion.59
  120.2 0.4 fusion.65
  121.2 1.9 %collective-permute-start.2 = (bf16[1,128,6,128]{1,3,2,0:T(8,128)(2,1)S(1)}, bf16[1,128,6,128]{1,3,2,0:T(8,128)(2,1)S(1)}, u32[]{:S(2)}, u32[]{:S(2)}) collective-permute-start(bf16[1,128,6,128]{1,3,2,0:T(8,128)(2,1)S(1)} %bitcast.303), channel_id=1, source_target_pairs={{1,0},{2,1},{3,2},{4,3},{5,4},{6,5},{7,6},{8,7},{9,8},{10,9},{11,1... | collective-permute-start | bytes 589832 | tf_op jit(solution)/shard_map/ppermute | solution.py:23
  123.9 5.2 %collective-permute-done.2 = bf16[1,128,6,128]{1,3,2,0:T(8,128)(2,1)S(1)} collective-permute-done((bf16[1,128,6,128]{1,3,2,0:T(8,128)(2,1)S(1)}, bf16[1,128,6,128]{1,3,2,0:T(8,128)(2,1)S(1)}, u32[]{:S(2)}, u32[]{:S(2)}) %collective-permute-start.2) | collective-permute-done | bytes 196640 | tf_op jit(solution)/shard_map/ppermute | solution.py:23
  129.0 0.9 fusion.57
  130.7 1.2 copy.161
  131.9 1.4 %copy.162 = bf16[2,64,12,256]{3,1,2,0:T(8,128)(2,1)} copy(bf16[2,64,12,256]{1,3,2,0:T(8,128)(2,1)S(1)} %bitcast.295) | data formatting | bytes 1572864 | tf_op jit(solution)/shard_map/convert_element_type | solution.py:104
  (66 shorter events, 5.3 us)
Async XLA Ops:
  6.5 112.8 %copy-start = (bf16[27,64,128]{2,1,0:T(8,128)(2,1)S(1)}, bf16[27,64,128]{2,1,0:T(8,128)(2,1)}, u32[]{:S(2)}) copy-start(bf16[27,64,128]{2,1,0:T(8,128)(2,1)} %param.7) | copy-start | bytes 1327108
  6.5 101.1 %all-gather.2.cloned.1.call-start = ((), (), s32[]{:S(2)}) async-start(), calls=%async_computation.1 | async-start | bytes 1880064 | tf_op jit(solution)/shard_map/all_gather | solution.py:92
  24.4 8.0 %collective-permute-start = (bf16[1,256,6,128]{3,1,2,0:T(8,128)(2,1)S(1)}, bf16[1,256,6,128]{3,1,2,0:T(8,128)(2,1)S(1)}, u32[]{:S(2)}, u32[]{:S(2)}) collective-permute-start(bf16[1,256,6,128]{3,1,2,0:T(8,128)(2,1)S(1)} %bitcast.296), channel_id=1, source_target_pairs={{0,1},{1,2},{2,3},{3,4},{4,5},{5,6},{6,7},{7,8},{8,9},{9,10},{10,1... | collective-permute-start | bytes 1179656 | tf_op jit(solution)/shard_map/ppermute | solution.py:12
  27.7 10.0 %collective-permute-start.1 = (bf16[1,256,6,128]{3,1,2,0:T(8,128)(2,1)S(1)}, bf16[1,256,6,128]{3,1,2,0:T(8,128)(2,1)S(1)}, u32[]{:S(2)}, u32[]{:S(2)}) collective-permute-start(bf16[1,256,6,128]{3,1,2,0:T(8,128)(2,1)S(1)} %bitcast.297), channel_id=1, source_target_pairs={{1,0},{2,1},{3,2},{4,3},{5,4},{6,5},{7,6},{8,7},{9,8},{10,9},{11,1... | collective-permute-start | bytes 1179656 | tf_op jit(solution)/shard_map/ppermute | solution.py:15
  93.8 18.1 %copy-start.1 = (f32[128]{0:T(128)S(1)}, f32[128]{0:T(128)}, u32[]{:S(2)}) copy-start(f32[128]{0:T(128)} %param.6) | copy-start | bytes 1540
  121.2 7.9 %collective-permute-start.2 = (bf16[1,128,6,128]{1,3,2,0:T(8,128)(2,1)S(1)}, bf16[1,128,6,128]{1,3,2,0:T(8,128)(2,1)S(1)}, u32[]{:S(2)}, u32[]{:S(2)}) collective-permute-start(bf16[1,128,6,128]{1,3,2,0:T(8,128)(2,1)S(1)} %bitcast.303), channel_id=1, source_target_pairs={{1,0},{2,1},{3,2},{4,3},{5,4},{6,5},{7,6},{8,7},{9,8},{10,9},{11,1... | collective-permute-start | bytes 589832 | tf_op jit(solution)/shard_map/ppermute | solution.py:23
Sparse Core Ops, SparseCore 0:
  29.8 39.9 all-gather.1
where the time goes:
time: 141 us; the launch traced here: 140 us
  local copies, waits for them, and re-layouts  76.6 us (54%)
  blocking collectives  17.9 us (13%)
  between operations  13.9 us (10%)
  waiting for transfers between devices  13.2 us (9%)
  matrix products  9.13 us (6%)
  starting transfers between devices  7.09 us (5%)
  other arithmetic  2.26 us (2%)
    another operation x2, local copies, waits for them, and re-layouts, conv_rows(): jnp.stack(taps, axis=2).reshape(count, chans * 27, wide_y * wide_z)  43.4 us
    all_to_all x1, blocking collectives, per_device(): lax.all_to_all(volume, 'gx', split_axis=0, concat_axis=1, tiled=True)  17.9 us
    dot_general x1, local copies, waits for them, and re-layouts, conv_rows(): jnp.einsum('fwh,wb->fbh', patch_columns, flattened_patches, preferred_ele...  13.9 us
    unnamed x32, local copies, waits for them, and re-layouts  10.8 us
    dot_general x1, matrix products, conv_rows(): jnp.einsum('fwh,wb->fbh', patch_columns, flattened_patches, preferred_ele...  7.43 us
    ppermute x1, waiting for transfers between devices, extended(): lax.ppermute(lax.slice_in_dim(block, 0, width, axis=dim), axis, backward)  5.28 us
    ppermute x1, waiting for transfers between devices, from_behind(): return lax.ppermute(block, axis, route)  5.16 us
    ppermute x1, starting transfers between devices, extended(): lax.ppermute(lax.slice_in_dim(block, block.shape[dim] - width, None, axis...  3.24 us
  transfers between devices with their start and end apart: 4, of which 3 were waited for; matrix products, arithmetic and copies ran while one was open for 50% of the time, Pallas kernels for 0%

commit v1 on v0

v1 whole, which is shorter than its diff:
```python
import functools

import jax
import jax.numpy as jnp
from jax import lax
from jax.experimental import pallas as pl
from jax.experimental.pallas import tpu as pltpu
from jax.sharding import PartitionSpec as P

TILE = 4


def window(first, count, total):
    return jnp.clip(first, 0, total - count)


def body(parts, total, scalars, *refs):
    vols, weights = refs[:parts], refs[parts : 2 * parts]
    bias_ref, up_ref, out_ref, cells, taps, upper = refs[2 * parts :]
    slots, cin = cells.shape[0], cells.shape[2]
    wide_y, wide_z = cells.shape[1] - 2, cells.shape[3]
    cout = taps.shape[1] // 3
    cup = up_ref.shape[1]
    plane = scalars[0]
    blank = jnp.zeros((slots, cin, wide_z), cells.dtype)
    cells[:, 0] = blank
    cells[:, wide_y + 1] = blank
    row = 0
    for part in range(parts):
        vol, weight = vols[part], weights[part]
        chans = vol.shape[2]
        for slot in range(slots):
            at = plane - 1 + slot
            inside = jnp.logical_and(at >= 0, at < total)
            held = vol[jnp.clip(at - scalars[1 + part], 0, vol.shape[0] - 1)]
            cells[slot, 1 : wide_y + 1, row : row + chans] = jnp.where(inside, held, jnp.zeros_like(held))
        row += chans
    for tap in range(27):
        column = jnp.concatenate([weight[tap] for weight in weights], axis=0)
        at = tap % 3 * cout
        taps[tap // 3, at : at + cout] = column.T
    eye = lax.broadcasted_iota(jnp.int32, (cout, cout), 0) == lax.broadcasted_iota(jnp.int32, (cout, cout), 1)
    bias = jnp.sum(jnp.where(eye, bias_ref[...], 0.0), axis=1, keepdims=True)
    lane = lax.broadcasted_iota(jnp.int32, (cout, wide_z), 1)
    hidden = []
    for ahead in range(2):
        rows = []
        for pair in range(wide_y // 2):
            acc = jnp.zeros((3 * cout, 2 * wide_z), jnp.float32)
            for tap_x in range(3):
                for tap_y in range(3):
                    at = 2 * pair + tap_y
                    block = jnp.concatenate([cells[ahead + tap_x, at], cells[ahead + tap_x, at + 1]], axis=1)
                    acc += jnp.dot(taps[3 * tap_x + tap_y], block, preferred_element_type=jnp.float32)
            for side in range(2):
                cut = acc[:, side * wide_z : (side + 1) * wide_z]
                low = jnp.where(lane == 0, 0.0, pltpu.roll(cut[:cout], 1, 1))
                high = jnp.where(lane == wide_z - 1, 0.0, pltpu.roll(cut[2 * cout :], wide_z - 1, 1))
                summed = cut[cout : 2 * cout] + low + high
                value = jnp.maximum(summed + bias, 0.0)
                if ahead:
                    value = jnp.where(plane + 1 < total, value, 0.0)
                rows.append(value.astype(jnp.bfloat16))
        hidden.append(jnp.concatenate(rows, axis=1))
    upper[:cout] = hidden[0]
    upper[cout:] = hidden[1]
    shape = (2 * wide_z, 2 * wide_z)
    source, target = (lax.broadcasted_iota(jnp.int32, shape, axis) for axis in range(2))
    weave = (target == 2 * (source % wide_z) + source // wide_z).astype(jnp.bfloat16)
    edge = lax.broadcasted_iota(jnp.int32, (cup, wide_z), 1) == wide_z - 1

    def later(value):
        return jnp.where(edge, 0.0, pltpu.roll(value, wide_z - 1, 1))

    for odd in range(2):
        if odd:
            left = jnp.concatenate([up_ref[18:27].reshape(9 * cup, cout), up_ref[0:9].reshape(9 * cup, cout)], axis=1)
            right = upper[...]
        else:
            left = up_ref[9:18].reshape(9 * cup, cout)
            right = upper[:cout]
        product = jnp.dot(left, right, preferred_element_type=jnp.float32)

        def term(tap_y, tap_z, y):
            at = (3 * tap_y + tap_z) * cup
            return product[at : at + cup, y * wide_z : (y + 1) * wide_z]

        lines = []
        for y in range(wide_y):
            for par_y in range(2):
                choices = [(1, y)] if par_y == 0 else [(2, y)] + ([(0, y + 1)] if y + 1 < wide_y else [])
                even = sum(term(tap_y, 1, at) for tap_y, at in choices)
                plain = sum(term(tap_y, 2, at) for tap_y, at in choices)
                moved = sum(term(tap_y, 0, at) for tap_y, at in choices)
                lines.append(jnp.concatenate([even, plain + later(moved)], axis=1).astype(jnp.bfloat16))
        woven = jnp.dot(jnp.concatenate(lines, axis=0), weave, preferred_element_type=jnp.float32)
        out_ref[odd] = woven.astype(jnp.bfloat16).reshape(2 * wide_y, cup, 2 * wide_z)


def local_step(plane, total, vols, starts, weights, bias, up):
    cin = sum(vol.shape[2] for vol in vols)
    wide_y, wide_z = vols[0].shape[1], vols[0].shape[3]
    cup, cout = up.shape[1], up.shape[2]
    scalars = jnp.stack([plane, *starts]).astype(jnp.int32)
    vmem = pl.BlockSpec(memory_space=pltpu.VMEM)
    return pl.pallas_call(
        functools.partial(body, len(vols), total),
        out_shape=jax.ShapeDtypeStruct((2, 2 * wide_y, cup, 2 * wide_z), jnp.bfloat16),
        in_specs=[pl.BlockSpec(memory_space=pltpu.SMEM)] + [vmem] * (2 * len(vols) + 2),
        out_specs=vmem,
        scratch_shapes=[
            pltpu.VMEM((4, wide_y + 2, cin, wide_z), jnp.bfloat16),
            pltpu.VMEM((9, 3 * cout, cin), jnp.bfloat16),
            pltpu.VMEM((2 * cout, wide_y * wide_z), jnp.bfloat16),
        ],
        compiler_params=pltpu.CompilerParams(vmem_limit_bytes=40 * 2**20),
        cost_estimate=pl.CostEstimate(flops=4 * 10**9, bytes_accessed=6 * 10**6, transcendentals=0),
    )(scalars, *vols, *weights, bias[None, :], up)


def per_device(volume, conv_weight, conv_bias, tconv_weight):
    total, size = volume.shape[0], lax.axis_size("gx")
    assert total == size and size % TILE == 0
    me = lax.axis_index("gx")
    tiles = size // TILE
    tile, side, core = me // TILE, me // 2 % 2, me % 2
    vol = jnp.transpose(volume, (0, 2, 1, 3))
    weight = jnp.transpose(conv_weight, (1, 0, 2))

    def cut(block, start, first, count):
        return lax.dynamic_slice_in_dim(block, window(first, count, total) - start, count, 0)

    def first_of(tile_at):
        return TILE * tile_at - 1

    def swap(block, bit):
        return lax.ppermute(block, "gx", [(i, i ^ bit) for i in range(size)])

    wide = min(7, total)
    start = window(first_of(tile), wide, total)
    vols = [cut(vol, 0, first_of(tile), wide)]
    weights = [weight]
    for step in range(1, tiles):
        there = (tile + step) % tiles
        route = [(i, (i + TILE * step) % size) for i in range(size)]
        vols.append(lax.ppermute(cut(vol, 0, first_of(there), wide), "gx", route))
        weights.append(lax.ppermute(weight, "gx", route))
    theirs = TILE * tile + 2 * (1 - side) - 1
    own = TILE * tile + 2 * side - 1
    start5 = window(own, 5, total)
    far_vols = [swap(cut(v, start, theirs, 5), 2) for v in vols]
    far_weights = [swap(w, 2) for w in weights]
    near = [cut(v, start, own, 5) for v in vols]
    vols, weights = near + far_vols, weights + far_weights
    core_vols = [swap(cut(v, start5, (me ^ 1) - 1, 4), 1) for v in vols]
    core_weights = [swap(w, 1) for w in weights]
    starts = [start5] * len(vols) + [window(me - 1, 4, total)] * len(core_vols)
    out = local_step(me, total, vols + core_vols, starts, weights + core_weights, conv_bias, tconv_weight)
    return jnp.transpose(out, (0, 2, 1, 3))


def solution(mesh):
    return jax.shard_map(
        per_device,
        mesh=mesh,
        in_specs=(P("groups", "gx", None, None), P("gx", None, None), P(), P()),
        out_specs=P(("groups", "gx"), None, None, None),
        check_vma=False,
    )
```

time: 141 us -> 62.9 us (0.45)
  the two profiles are of different devices: /device:TPU:5 before, /device:TPU:0 now
where the time goes in v1:
time: 62.9 us; the launch traced here: 62.6 us
  waiting for transfers between devices  29.1 us (46%)
  starting transfers between devices  20.4 us (32%)
  local copies, waits for them, and re-layouts  6.91 us (11%)
  Pallas kernels  6.08 us (10%)
    ppermute x24, starting transfers between devices, swap(): return lax.ppermute(block, 'gx', [(i, i ^ bit) for i in range(size)])  16.2 us
    ppermute x24, waiting for transfers between devices, swap(): return lax.ppermute(block, 'gx', [(i, i ^ bit) for i in range(size)])  14.5 us
    ppermute x3, waiting for transfers between devices, per_device(): vols.append(lax.ppermute(cut(vol, 0, first_of(there), wide), 'gx', route))  12.3 us
    pallas_call x1, Pallas kernels, local_step(): pl.pallas_call(functools.partial(body, len(vols), total), out_shape=jax.S...  6.08 us
    unnamed x16, local copies, waits for them, and re-layouts  3.73 us
    ppermute x3, starting transfers between devices, per_device(): weights.append(lax.ppermute(weight, 'gx', route))  3.66 us
    dynamic_slice x13, local copies, waits for them, and re-layouts, cut(): lax.dynamic_slice_in_dim(block, window(first, count, total) - start, coun...  3.09 us
    ppermute x3, waiting for transfers between devices, per_device(): weights.append(lax.ppermute(weight, 'gx', route))  2.29 us
  transfers between devices with their start and end apart: 30, of which 12 were waited for; matrix products, arithmetic and copies ran while one was open for 5% of the time, Pallas kernels for 0%

profile of v1, /device:TPU:0, one launch (start us, length us, event | category | flops | bytes accessed | tf_op | source)
XLA Modules:
  0.0 62.6 jit_solution(355608794662129853)
XLA Ops:
  0.5 2.6 %collective-permute-start.18 = (bf16[27,16,128]{2,1,0:T(8,128)(2,1)}, bf16[27,16,128]{2,1,0:T(8,128)(2,1)S(1)}, u32[]{:S(2)}, u32[]{:S(2)}) collective-permute-start(bf16[27,16,128]{2,1,0:T(8,128)(2,1)} %bitcast.19), channel_id=1, source_target_pairs={{0,2},{1,3},{2,0},{3,1},{4,6},{5,7},{6,4},{7,5},{8,10},{9,11},{10,... | collective-permute-start | bytes 331784 | tf_op jit(solution)/shard_map/ppermute | solution.py:137
  3.0 3.6 %collective-permute-start.17 = (bf16[27,16,128]{2,1,0:T(8,128)(2,1)}, bf16[27,16,128]{2,1,0:T(8,128)(2,1)S(1)}, u32[]{:S(2)}, u32[]{:S(2)}) collective-permute-start(bf16[27,16,128]{2,1,0:T(8,128)(2,1)} %bitcast.20), channel_id=1, source_target_pairs={{0,12},{1,13},{2,14},{3,15},{4,0},{5,1},{6,2},{7,3},{8,4},{9,5},{1... | collective-permute-start | bytes 331784 | tf_op jit(solution)/shard_map/ppermute | solution.py:147
  6.6 1.0 %dynamic-slice_bitcast_fusion.3 = (bf16[5,6,16,128]{3,2,1,0:T(8,128)(2,1)S(1)}, bf16[5,6,16,128]{3,2,1,0:T(8,128)(2,1)S(1)}) fusion(bf16[16,16,6,128]{3,1,2,0:T(8,128)(2,1)} %param.4, s32[]{:T(128)S(6)} %add.106, s32[]{:T(128)S(6)} %add.97), kind=kLoop, calls=%fused_computation.3 | loop fusion | bytes 491528 | tf_op jit(solution)/shard_map/dynamic_slice | solution.py:131
  8.8 4.0 %collective-permute-done.3.refs_4_ = bf16[5,6,16,128]{3,2,1,0:T(8,128)(2,1)S(1)} collective-permute-done((bf16[5,6,16,128]{3,2,1,0:T(8,128)(2,1)S(1)}, bf16[5,6,16,128]{3,2,1,0:T(8,128)(2,1)S(1)}, u32[]{:S(2)}, u32[]{:S(2)}) %collective-permute-start.3) | collective-permute-done | bytes 122912 | tf_op jit(solution)/shard_map/ppermute | solution.py:137
  12.8 1.4 %collective-permute-done.2 = bf16[7,6,16,128]{3,2,1,0:T(8,128)(2,1)S(1)} collective-permute-done((bf16[7,6,16,128]{3,2,1,0:T(8,128)(2,1)S(1)}, bf16[7,6,16,128]{3,2,1,0:T(8,128)(2,1)S(1)}, u32[]{:S(2)}, u32[]{:S(2)}) %collective-permute-start.2) | collective-permute-done | bytes 172064 | tf_op jit(solution)/shard_map/ppermute | solution.py:146
  14.2 10.9 %collective-permute-done.1 = bf16[7,6,16,128]{3,2,1,0:T(8,128)(2,1)S(1)} collective-permute-done((bf16[7,6,16,128]{3,2,1,0:T(8,128)(2,1)S(1)}, bf16[7,6,16,128]{3,2,1,0:T(8,128)(2,1)S(1)}, u32[]{:S(2)}, u32[]{:S(2)}) %collective-permute-start.1) | collective-permute-done | bytes 172064 | tf_op jit(solution)/shard_map/ppermute | solution.py:146
  25.3 1.2 %collective-permute-done.7.refs_8_ = bf16[4,6,16,128]{3,2,1,0:T(8,128)(2,1)S(1)} collective-permute-done((bf16[4,6,16,128]{3,2,1,0:T(8,128)(2,1)S(1)}, bf16[4,6,16,128]{3,2,1,0:T(8,128)(2,1)S(1)}, u32[]{:S(2)}, u32[]{:S(2)}) %collective-permute-start.7) | collective-permute-done | bytes 98336 | tf_op jit(solution)/shard_map/ppermute | solution.py:137
  26.6 3.7 %collective-permute-start.6 = (bf16[5,6,16,128]{3,2,1,0:T(8,128)(2,1)S(1)}, bf16[5,6,16,128]{3,2,1,0:T(8,128)(2,1)S(1)}, u32[]{:S(2)}, u32[]{:S(2)}) collective-permute-start(bf16[5,6,16,128]{3,2,1,0:T(8,128)(2,1)S(1)} %get-tuple-element.10), channel_id=1, source_target_pairs={{0,2},{1,3},{2,0},{3,1},{4,6},{5,7},{6,4},{7,5},{8,10},{9,11},{10,... | collective-permute-start | bytes 368648 | tf_op jit(solution)/shard_map/ppermute | solution.py:137
  31.0 3.7 %collective-permute-start.5 = (bf16[5,6,16,128]{3,2,1,0:T(8,128)(2,1)S(1)}, bf16[5,6,16,128]{3,2,1,0:T(8,128)(2,1)S(1)}, u32[]{:S(2)}, u32[]{:S(2)}) collective-permute-start(bf16[5,6,16,128]{3,2,1,0:T(8,128)(2,1)S(1)} %get-tuple-element.12), channel_id=1, source_target_pairs={{0,2},{1,3},{2,0},{3,1},{4,6},{5,7},{6,4},{7,5},{8,10},{9,11},{10,... | collective-permute-start | bytes 368648 | tf_op jit(solution)/shard_map/ppermute | solution.py:137
  34.8 2.2 %collective-permute-done.15.refs_17_ = bf16[27,16,128]{2,1,0:T(8,128)(2,1)S(1)} collective-permute-done((bf16[27,16,128]{2,1,0:T(8,128)(2,1)S(1)}, bf16[27,16,128]{2,1,0:T(8,128)(2,1)S(1)}, u32[]{:S(2)}, u32[]{:S(2)}) %collective-permute-start.15) | collective-permute-done | bytes 110624 | tf_op jit(solution)/shard_map/ppermute | solution.py:147
  37.3 1.8 %collective-permute-start.20 = (bf16[27,16,128]{2,1,0:T(8,128)(2,1)S(1)}, bf16[27,16,128]{2,1,0:T(8,128)(2,1)S(1)}, u32[]{:S(2)}, u32[]{:S(2)}) collective-permute-start(bf16[27,16,128]{2,1,0:T(8,128)(2,1)S(1)} %collective-permute-done.16.refs_18_), channel_id=1, source_target_pairs={{0,2},{1,3},{2,0},{3,1},{4,6},{5,7},{6,4},{7,5},{8,10},{9,11},{10,... | collective-permute-start | bytes 331784 | tf_op jit(solution)/shard_map/ppermute | solution.py:137
  39.4 0.6 %constant_dynamic-slice_fusion = bf16[4,6,16,128]{3,2,1,0:T(8,128)(2,1)} fusion(bf16[5,6,16,128]{3,2,1,0:T(8,128)(2,1)S(1)} %collective-permute-done.6.refs_7_, s32[]{:T(128)S(6)} %select_n.68), kind=kLoop, calls=%fused_computation.6 | loop fusion | bytes 196612 | tf_op jit(solution)/shard_map/dynamic_slice | solution.py:131
  40.1 2.9 %collective-permute-done.21.refs_23_ = bf16[27,16,128]{2,1,0:T(8,128)(2,1)S(1)} collective-permute-done((bf16[27,16,128]{2,1,0:T(8,128)(2,1)S(1)}, bf16[27,16,128]{2,1,0:T(8,128)(2,1)S(1)}, u32[]{:S(2)}, u32[]{:S(2)}) %collective-permute-start.21) | collective-permute-done | bytes 110624 | tf_op jit(solution)/shard_map/ppermute | solution.py:137
  43.0 2.3 %collective-permute-done.20.refs_22_ = bf16[27,16,128]{2,1,0:T(8,128)(2,1)S(1)} collective-permute-done((bf16[27,16,128]{2,1,0:T(8,128)(2,1)S(1)}, bf16[27,16,128]{2,1,0:T(8,128)(2,1)S(1)}, u32[]{:S(2)}, u32[]{:S(2)}) %collective-permute-start.20) | collective-permute-done | bytes 110624 | tf_op jit(solution)/shard_map/ppermute | solution.py:137
  45.8 0.6 %constant_dynamic-slice_fusion.1 = bf16[4,6,16,128]{3,2,1,0:T(8,128)(2,1)} fusion(bf16[5,6,16,128]{3,2,1,0:T(8,128)(2,1)S(1)} %collective-permute-done.5.refs_6_, s32[]{:T(128)S(6)} %select_n.68), kind=kLoop, calls=%fused_computation.7 | loop fusion | bytes 196612 | tf_op jit(solution)/shard_map/dynamic_slice | solution.py:131
  46.4 2.5 %collective-permute-done.19.refs_21_ = bf16[27,16,128]{2,1,0:T(8,128)(2,1)S(1)} collective-permute-done((bf16[27,16,128]{2,1,0:T(8,128)(2,1)S(1)}, bf16[27,16,128]{2,1,0:T(8,128)(2,1)S(1)}, u32[]{:S(2)}, u32[]{:S(2)}) %collective-permute-start.19) | collective-permute-done | bytes 110624 | tf_op jit(solution)/shard_map/ppermute | solution.py:137
  50.0 0.6 %constant_dynamic-slice_fusion.2 = bf16[4,6,16,128]{3,2,1,0:T(8,128)(2,1)} fusion(bf16[5,6,16,128]{3,2,1,0:T(8,128)(2,1)S(1)} %collective-permute-done.4.refs_5_, s32[]{:T(128)S(6)} %select_n.68), kind=kLoop, calls=%fused_computation.8 | loop fusion | bytes 196612 | tf_op jit(solution)/shard_map/dynamic_slice | solution.py:131
  50.7 0.6 %copy-done.2 = bf16[4,6,16,128]{3,2,1,0:T(8,128)(2,1)} copy-done((bf16[4,6,16,128]{3,2,1,0:T(8,128)(2,1)}, bf16[4,6,16,128]{3,2,1,0:T(8,128)(2,1)S(1)}, u32[]{:S(2)}) %copy-start.2) | copy-done | bytes 98328
  51.4 0.6 %copy-done.4 = bf16[4,6,16,128]{3,2,1,0:T(8,128)(2,1)} copy-done((bf16[4,6,16,128]{3,2,1,0:T(8,128)(2,1)}, bf16[4,6,16,128]{3,2,1,0:T(8,128)(2,1)S(1)}, u32[]{:S(2)}) %copy-start.4) | copy-done | bytes 98328
  52.9 0.8 %collective-permute-done.13.refs_14_ = bf16[4,6,16,128]{3,2,1,0:T(8,128)(2,1)} collective-permute-done((bf16[4,6,16,128]{3,2,1,0:T(8,128)(2,1)}, bf16[4,6,16,128]{3,2,1,0:T(8,128)(2,1)}, u32[]{:S(2)}, u32[]{:S(2)}) %collective-permute-start.13) | collective-permute-done | bytes 98336 | tf_op jit(solution)/shard_map/ppermute | solution.py:137
  54.1 0.7 %copy-done.6 = f32[128]{0:T(128)S(1)} copy-done((f32[128]{0:T(128)S(1)}, f32[128]{0:T(128)}, u32[]{:S(2)}) %copy-start.6) | copy-done | bytes 536
  54.8 0.9 %copy-done.3 = bf16[4,6,16,128]{3,2,1,0:T(8,128)(2,1)S(1)} copy-done((bf16[4,6,16,128]{3,2,1,0:T(8,128)(2,1)S(1)}, bf16[4,6,16,128]{3,2,1,0:T(8,128)(2,1)}, u32[]{:S(2)}) %copy-start.3) | copy-done | bytes 98328
  55.6 0.9 %copy-done.5 = bf16[4,6,16,128]{3,2,1,0:T(8,128)(2,1)S(1)} copy-done((bf16[4,6,16,128]{3,2,1,0:T(8,128)(2,1)S(1)}, bf16[4,6,16,128]{3,2,1,0:T(8,128)(2,1)}, u32[]{:S(2)}) %copy-start.5) | copy-done | bytes 98328
  56.5 6.1 %shard_map.46 = bf16[2,12,64,256]{3,2,1,0:T(8,128)(2,1)} custom-call(s32[17]{0:T(128)S(1)} %stack.11.scalars, bf16[5,6,16,128]{3,2,1,0:T(8,128)(2,1)S(1)} %get-tuple-element.6.refs_0_, bf16[5,6,16,128]{3,2,1,0:T(8,128)(2,1)S(1)} %get-tuple-element.15.refs_1_, bf16[5,6,16,128]{3,2,1,0:T(8,128)(2,1)S(1)} %get-tuple-element.13.refs_2_, ...), custom_call_target="tpu_custom_call" | custom-call | flops 4000000000 | bytes 6000000 | tf_op jit(solution)/shard_map/pallas_call | solution.py:106
  (67 shorter events, 6.0 us)
Async XLA Ops:
  0.0 30.3 %collective-permute-start.22 = (bf16[27,16,128]{2,1,0:T(8,128)(2,1)}, bf16[27,16,128]{2,1,0:T(8,128)(2,1)S(1)}, u32[]{:S(2)}, u32[]{:S(2)}) collective-permute-start(bf16[27,16,128]{2,1,0:T(8,128)(2,1)} %bitcast.18), channel_id=1, source_target_pairs={{0,1},{1,0},{2,3},{3,2},{4,5},{5,4},{6,7},{7,6},{8,9},{9,8},{10,11... | collective-permute-start | bytes 331784 | tf_op jit(solution)/shard_map/ppermute | solution.py:137
  0.5 29.9 %collective-permute-start.18 = (bf16[27,16,128]{2,1,0:T(8,128)(2,1)}, bf16[27,16,128]{2,1,0:T(8,128)(2,1)S(1)}, u32[]{:S(2)}, u32[]{:S(2)}) collective-permute-start(bf16[27,16,128]{2,1,0:T(8,128)(2,1)} %bitcast.19), channel_id=1, source_target_pairs={{0,2},{1,3},{2,0},{3,1},{4,6},{5,7},{6,4},{7,5},{8,10},{9,11},{10,... | collective-permute-start | bytes 331784 | tf_op jit(solution)/shard_map/ppermute | solution.py:137
  3.0 27.4 %collective-permute-start.17 = (bf16[27,16,128]{2,1,0:T(8,128)(2,1)}, bf16[27,16,128]{2,1,0:T(8,128)(2,1)S(1)}, u32[]{:S(2)}, u32[]{:S(2)}) collective-permute-start(bf16[27,16,128]{2,1,0:T(8,128)(2,1)} %bitcast.20), channel_id=1, source_target_pairs={{0,12},{1,13},{2,14},{3,15},{4,0},{5,1},{6,2},{7,3},{8,4},{9,5},{1... | collective-permute-start | bytes 331784 | tf_op jit(solution)/shard_map/ppermute | solution.py:147
  7.6 5.2 %collective-permute-start.3 = (bf16[5,6,16,128]{3,2,1,0:T(8,128)(2,1)S(1)}, bf16[5,6,16,128]{3,2,1,0:T(8,128)(2,1)S(1)}, u32[]{:S(2)}, u32[]{:S(2)}) collective-permute-start(bf16[5,6,16,128]{3,2,1,0:T(8,128)(2,1)S(1)} %get-tuple-element.5), channel_id=1, source_target_pairs={{0,2},{1,3},{2,0},{3,1},{4,6},{5,7},{6,4},{7,5},{8,10},{9,11},{10,... | collective-permute-start | bytes 368648 | tf_op jit(solution)/shard_map/ppermute | solution.py:137
  8.2 5.9 %collective-permute-start.2 = (bf16[7,6,16,128]{3,2,1,0:T(8,128)(2,1)S(1)}, bf16[7,6,16,128]{3,2,1,0:T(8,128)(2,1)S(1)}, u32[]{:S(2)}, u32[]{:S(2)}) collective-permute-start(bf16[7,6,16,128]{3,2,1,0:T(8,128)(2,1)S(1)} %get-tuple-element.7), channel_id=1, source_target_pairs={{0,12},{1,13},{2,14},{3,15},{4,0},{5,1},{6,2},{7,3},{8,4},{9,5},{1... | collective-permute-start | bytes 516104 | tf_op jit(solution)/shard_map/ppermute | solution.py:146
  12.8 12.3 %collective-permute-start.1 = (bf16[7,6,16,128]{3,2,1,0:T(8,128)(2,1)S(1)}, bf16[7,6,16,128]{3,2,1,0:T(8,128)(2,1)S(1)}, u32[]{:S(2)}, u32[]{:S(2)}) collective-permute-start(bf16[7,6,16,128]{3,2,1,0:T(8,128)(2,1)S(1)} %get-tuple-element.8), channel_id=1, source_target_pairs={{0,8},{1,9},{2,10},{3,11},{4,12},{5,13},{6,14},{7,15},{8,0},{9,1},... | collective-permute-start | bytes 516104 | tf_op jit(solution)/shard_map/ppermute | solution.py:146
  14.2 11.0 %collective-permute-start = (bf16[7,6,16,128]{3,2,1,0:T(8,128)(2,1)S(1)}, bf16[7,6,16,128]{3,2,1,0:T(8,128)(2,1)S(1)}, u32[]{:S(2)}, u32[]{:S(2)}) collective-permute-start(bf16[7,6,16,128]{3,2,1,0:T(8,128)(2,1)S(1)} %get-tuple-element.9), channel_id=1, source_target_pairs={{0,4},{1,5},{2,6},{3,7},{4,8},{5,9},{6,10},{7,11},{8,12},{9,13},{1... | collective-permute-start | bytes 516104 | tf_op jit(solution)/shard_map/ppermute | solution.py:146
  25.1 5.9 %collective-permute-start.16 = (bf16[27,16,128]{2,1,0:T(8,128)(2,1)S(1)}, bf16[27,16,128]{2,1,0:T(8,128)(2,1)S(1)}, u32[]{:S(2)}, u32[]{:S(2)}) collective-permute-start(bf16[27,16,128]{2,1,0:T(8,128)(2,1)S(1)} %bitcast.21), channel_id=1, source_target_pairs={{0,8},{1,9},{2,10},{3,11},{4,12},{5,13},{6,14},{7,15},{8,0},{9,1},... | collective-permute-start | bytes 331784 | tf_op jit(solution)/shard_map/ppermute | solution.py:147
  26.6 12.6 %collective-permute-start.6 = (bf16[5,6,16,128]{3,2,1,0:T(8,128)(2,1)S(1)}, bf16[5,6,16,128]{3,2,1,0:T(8,128)(2,1)S(1)}, u32[]{:S(2)}, u32[]{:S(2)}) collective-permute-start(bf16[5,6,16,128]{3,2,1,0:T(8,128)(2,1)S(1)} %get-tuple-element.10), channel_id=1, source_target_pairs={{0,2},{1,3},{2,0},{3,1},{4,6},{5,7},{6,4},{7,5},{8,10},{9,11},{10,... | collective-permute-start | bytes 368648 | tf_op jit(solution)/shard_map/ppermute | solution.py:137
  30.3 6.7 %collective-permute-start.15 = (bf16[27,16,128]{2,1,0:T(8,128)(2,1)S(1)}, bf16[27,16,128]{2,1,0:T(8,128)(2,1)S(1)}, u32[]{:S(2)}, u32[]{:S(2)}) collective-permute-start(bf16[27,16,128]{2,1,0:T(8,128)(2,1)S(1)} %bitcast.22), channel_id=1, source_target_pairs={{0,4},{1,5},{2,6},{3,7},{4,8},{5,9},{6,10},{7,11},{8,12},{9,13},{1... | collective-permute-start | bytes 331784 | tf_op jit(solution)/shard_map/ppermute | solution.py:147
  30.4 6.9 %collective-permute-start.26 = (bf16[27,16,128]{2,1,0:T(8,128)(2,1)S(1)}, bf16[27,16,128]{2,1,0:T(8,128)(2,1)S(1)}, u32[]{:S(2)}, u32[]{:S(2)}) collective-permute-start(bf16[27,16,128]{2,1,0:T(8,128)(2,1)S(1)} %collective-permute-done.18.refs_20_), channel_id=1, source_target_pairs={{0,1},{1,0},{2,3},{3,2},{4,5},{5,4},{6,7},{7,6},{8,9},{9,8},{10,11... | collective-permute-start | bytes 331784 | tf_op jit(solution)/shard_map/ppermute | solution.py:137
  30.5 6.8 %collective-permute-start.25 = (bf16[27,16,128]{2,1,0:T(8,128)(2,1)S(1)}, bf16[27,16,128]{2,1,0:T(8,128)(2,1)S(1)}, u32[]{:S(2)}, u32[]{:S(2)}) collective-permute-start(bf16[27,16,128]{2,1,0:T(8,128)(2,1)S(1)} %collective-permute-done.17.refs_19_), channel_id=1, source_target_pairs={{0,1},{1,0},{2,3},{3,2},{4,5},{5,4},{6,7},{7,6},{8,9},{9,8},{10,11... | collective-permute-start | bytes 331784 | tf_op jit(solution)/shard_map/ppermute | solution.py:137
  31.0 14.3 %collective-permute-start.5 = (bf16[5,6,16,128]{3,2,1,0:T(8,128)(2,1)S(1)}, bf16[5,6,16,128]{3,2,1,0:T(8,128)(2,1)S(1)}, u32[]{:S(2)}, u32[]{:S(2)}) collective-permute-start(bf16[5,6,16,128]{3,2,1,0:T(8,128)(2,1)S(1)} %get-tuple-element.12), channel_id=1, source_target_pairs={{0,2},{1,3},{2,0},{3,1},{4,6},{5,7},{6,4},{7,5},{8,10},{9,11},{10,... | collective-permute-start | bytes 368648 | tf_op jit(solution)/shard_map/ppermute | solution.py:137
  37.0 5.9 %collective-permute-start.21 = (bf16[27,16,128]{2,1,0:T(8,128)(2,1)S(1)}, bf16[27,16,128]{2,1,0:T(8,128)(2,1)S(1)}, u32[]{:S(2)}, u32[]{:S(2)}) collective-permute-start(bf16[27,16,128]{2,1,0:T(8,128)(2,1)S(1)} %collective-permute-done.17.refs_19_), channel_id=1, source_target_pairs={{0,2},{1,3},{2,0},{3,1},{4,6},{5,7},{6,4},{7,5},{8,10},{9,11},{10,... | collective-permute-start | bytes 331784 | tf_op jit(solution)/shard_map/ppermute | solution.py:137
  37.3 5.6 %collective-permute-start.24 = (bf16[27,16,128]{2,1,0:T(8,128)(2,1)S(1)}, bf16[27,16,128]{2,1,0:T(8,128)(2,1)S(1)}, u32[]{:S(2)}, u32[]{:S(2)}) collective-permute-start(bf16[27,16,128]{2,1,0:T(8,128)(2,1)S(1)} %collective-permute-done.16.refs_18_), channel_id=1, source_target_pairs={{0,1},{1,0},{2,3},{3,2},{4,5},{5,4},{6,7},{7,6},{8,9},{9,8},{10,11... | collective-permute-start | bytes 331784 | tf_op jit(solution)/shard_map/ppermute | solution.py:137
  37.3 8.0 %collective-permute-start.20 = (bf16[27,16,128]{2,1,0:T(8,128)(2,1)S(1)}, bf16[27,16,128]{2,1,0:T(8,128)(2,1)S(1)}, u32[]{:S(2)}, u32[]{:S(2)}) collective-permute-start(bf16[27,16,128]{2,1,0:T(8,128)(2,1)S(1)} %collective-permute-done.16.refs_18_), channel_id=1, source_target_pairs={{0,2},{1,3},{2,0},{3,1},{4,6},{5,7},{6,4},{7,5},{8,10},{9,11},{10,... | collective-permute-start | bytes 331784 | tf_op jit(solution)/shard_map/ppermute | solution.py:137
  39.1 10.4 %collective-permute-start.4 = (bf16[5,6,16,128]{3,2,1,0:T(8,128)(2,1)S(1)}, bf16[5,6,16,128]{3,2,1,0:T(8,128)(2,1)S(1)}, u32[]{:S(2)}, u32[]{:S(2)}) collective-permute-start(bf16[5,6,16,128]{3,2,1,0:T(8,128)(2,1)S(1)} %get-tuple-element.14), channel_id=1, source_target_pairs={{0,2},{1,3},{2,0},{3,1},{4,6},{5,7},{6,4},{7,5},{8,10},{9,11},{10,... | collective-permute-start | bytes 368648 | tf_op jit(solution)/shard_map/ppermute | solution.py:137
  42.9 3.5 %collective-permute-start.23 = (bf16[27,16,128]{2,1,0:T(8,128)(2,1)S(1)}, bf16[27,16,128]{2,1,0:T(8,128)(2,1)S(1)}, u32[]{:S(2)}, u32[]{:S(2)}) collective-permute-start(bf16[27,16,128]{2,1,0:T(8,128)(2,1)S(1)} %collective-permute-done.15.refs_17_), channel_id=1, source_target_pairs={{0,1},{1,0},{2,3},{3,2},{4,5},{5,4},{6,7},{7,6},{8,9},{9,8},{10,11... | collective-permute-start | bytes 331784 | tf_op jit(solution)/shard_map/ppermute | solution.py:137
  42.9 6.0 %collective-permute-start.19 = (bf16[27,16,128]{2,1,0:T(8,128)(2,1)S(1)}, bf16[27,16,128]{2,1,0:T(8,128)(2,1)S(1)}, u32[]{:S(2)}, u32[]{:S(2)}) collective-permute-start(bf16[27,16,128]{2,1,0:T(8,128)(2,1)S(1)} %collective-permute-done.15.refs_17_), channel_id=1, source_target_pairs={{0,2},{1,3},{2,0},{3,1},{4,6},{5,7},{6,4},{7,5},{8,10},{9,11},{10,... | collective-permute-start | bytes 331784 | tf_op jit(solution)/shard_map/ppermute | solution.py:137
  45.3 3.7 %collective-permute-start.11 = (bf16[4,6,16,128]{3,2,1,0:T(8,128)(2,1)S(1)}, bf16[4,6,16,128]{3,2,1,0:T(8,128)(2,1)S(1)}, u32[]{:S(2)}, u32[]{:S(2)}) collective-permute-start(bf16[4,6,16,128]{3,2,1,0:T(8,128)(2,1)S(1)} %constant_dynamic-slice_fusion.3), channel_id=1, source_target_pairs={{0,1},{1,0},{2,3},{3,2},{4,5},{5,4},{6,7},{7,6},{8,9},{9,8},{10,11... | collective-permute-start | bytes 294920 | tf_op jit(solution)/shard_map/ppermute | solution.py:137
  45.3 4.2 %collective-permute-start.10 = (bf16[4,6,16,128]{3,2,1,0:T(8,128)(2,1)S(1)}, bf16[4,6,16,128]{3,2,1,0:T(8,128)(2,1)S(1)}, u32[]{:S(2)}, u32[]{:S(2)}) collective-permute-start(bf16[4,6,16,128]{3,2,1,0:T(8,128)(2,1)S(1)} %constant_dynamic-slice_fusion.4), channel_id=1, source_target_pairs={{0,1},{1,0},{2,3},{3,2},{4,5},{5,4},{6,7},{7,6},{8,9},{9,8},{10,11... | collective-permute-start | bytes 294920 | tf_op jit(solution)/shard_map/ppermute | solution.py:137
  46.4 4.2 %collective-permute-start.9 = (bf16[4,6,16,128]{3,2,1,0:T(8,128)(2,1)S(1)}, bf16[4,6,16,128]{3,2,1,0:T(8,128)(2,1)S(1)}, u32[]{:S(2)}, u32[]{:S(2)}) collective-permute-start(bf16[4,6,16,128]{3,2,1,0:T(8,128)(2,1)S(1)} %constant_dynamic-slice_fusion.5), channel_id=1, source_target_pairs={{0,1},{1,0},{2,3},{3,2},{4,5},{5,4},{6,7},{7,6},{8,9},{9,8},{10,11... | collective-permute-start | bytes 294920 | tf_op jit(solution)/shard_map/ppermute | solution.py:137
  49.0 3.5 %collective-permute-start.29 = (bf16[27,16,128]{2,1,0:T(8,128)(2,1)S(1)}, bf16[27,16,128]{2,1,0:T(8,128)(2,1)S(1)}, u32[]{:S(2)}, u32[]{:S(2)}) collective-permute-start(bf16[27,16,128]{2,1,0:T(8,128)(2,1)S(1)} %collective-permute-done.21.refs_23_), channel_id=1, source_target_pairs={{0,1},{1,0},{2,3},{3,2},{4,5},{5,4},{6,7},{7,6},{8,9},{9,8},{10,11... | collective-permute-start | bytes 331784 | tf_op jit(solution)/shard_map/ppermute | solution.py:137
  49.5 3.1 %collective-permute-start.28 = (bf16[27,16,128]{2,1,0:T(8,128)(2,1)S(1)}, bf16[27,16,128]{2,1,0:T(8,128)(2,1)S(1)}, u32[]{:S(2)}, u32[]{:S(2)}) collective-permute-start(bf16[27,16,128]{2,1,0:T(8,128)(2,1)S(1)} %collective-permute-done.20.refs_22_), channel_id=1, source_target_pairs={{0,1},{1,0},{2,3},{3,2},{4,5},{5,4},{6,7},{7,6},{8,9},{9,8},{10,11... | collective-permute-start | bytes 331784 | tf_op jit(solution)/shard_map/ppermute | solution.py:137
  (14 other events, 58.5 us)

commit v2 on v1

v2 whole, which is shorter than its diff:
```python
import functools

import jax
import jax.numpy as jnp
from jax import lax
from jax.experimental import pallas as pl
from jax.experimental.pallas import tpu as pltpu
from jax.sharding import PartitionSpec as P

TILE = 4
VMEM = pl.BlockSpec(memory_space=pltpu.VMEM)
SMEM = pl.BlockSpec(memory_space=pltpu.SMEM)


def window(first, count, total):
    return jnp.clip(first, 0, total - count)


def conv_body(order, span, total, scalars, *refs):
    steps = len(order)
    vols, fars, weights = refs[:steps], refs[steps : steps + 2], refs[steps + 2 : -4]
    keep_ref, send_ref, cells, taps = refs[-4:]
    core, group, first = scalars[0], scalars[1], scalars[2]
    slots, wide_y, wide_z = cells.shape[0], cells.shape[1] - 2, cells.shape[3]
    chans = vols[0].shape[2]
    cout, cin = taps.shape[0] // 3, cells.shape[2]
    blank = jnp.zeros((slots, cin, wide_z), cells.dtype)
    cells[:, 0] = blank
    cells[:, wide_y + 1] = blank
    half = steps // 2
    for slot in range(slots):
        at = first + slot
        inside = jnp.logical_and(at >= 0, at < total)
        for place, step in enumerate(order):
            near = vols[place]
            far = fars[step // half].at[step % half]
            for base, ref, start in ((0, near, scalars[3 + place]), (steps, far, scalars[3 + steps])):
                held = ref[jnp.clip(at - start, 0, ref.shape[0] - 1)]
                row = (base + place) * chans
                cells[slot, 1 : wide_y + 1, row : row + chans] = jnp.where(inside, held, jnp.zeros_like(held))
    for tap in range(27):
        part = tap // span
        start = min(part * span, 27 - span)
        pieces = []
        for column in range(2):
            for place in range(steps):
                pieces.append(weights[column][group ^ part, place, tap - start])
        block = jnp.concatenate(pieces, axis=0)
        at = tap // 3 * cin
        taps[tap % 3 * cout : (tap % 3 + 1) * cout, at : at + cin] = block.T
    lane = lax.broadcasted_iota(jnp.int32, (cout, wide_z), 1)
    for which in range(3):
        if which == 0:
            base, targets = 1, ((keep_ref, 1 - core), (send_ref, core))
        elif which == 1:
            base, targets = 2 * (1 - core), ((send_ref, 1 - core),)
        else:
            base, targets = 2 * core, ((keep_ref, core),)
        for pair in range(wide_y // 2):
            blocks = []
            for tap_x in range(3):
                for tap_y in range(3):
                    at = 2 * pair + tap_y
                    blocks.append(jnp.concatenate([cells[base + tap_x, at], cells[base + tap_x, at + 1]], axis=1))
            acc = jnp.dot(taps[...], jnp.concatenate(blocks, axis=0), preferred_element_type=jnp.float32)
            for side in range(2):
                cut = acc[:, side * wide_z : (side + 1) * wide_z]
                low = jnp.where(lane == 0, 0.0, pltpu.roll(cut[:cout], 1, 1))
                high = jnp.where(lane == wide_z - 1, 0.0, pltpu.roll(cut[2 * cout :], wide_z - 1, 1))
                summed = cut[cout : 2 * cout] + low + high
                for ref, index in targets:
                    ref[index, 2 * pair + side] = summed


def up_body(total, scalars, keep_ref, came_ref, bias_ref, up_ref, out_ref):
    plane = scalars[0]
    wide_y, cout, wide_z = keep_ref.shape[1:]
    cup = up_ref.shape[1]
    eye = lax.broadcasted_iota(jnp.int32, (cout, cout), 0) == lax.broadcasted_iota(jnp.int32, (cout, cout), 1)
    bias = jnp.sum(jnp.where(eye, bias_ref[...], 0.0), axis=1, keepdims=True)
    hidden = []
    for ahead in range(2):
        rows = []
        for y in range(wide_y):
            value = jnp.maximum(keep_ref[ahead, y] + came_ref[ahead, y] + bias, 0.0)
            if ahead:
                value = jnp.where(plane + 1 < total, value, 0.0)
            rows.append(value.astype(jnp.bfloat16))
        hidden.append(jnp.concatenate(rows, axis=1))
    shape = (2 * wide_z, 2 * wide_z)
    source, target = (lax.broadcasted_iota(jnp.int32, shape, axis) for axis in range(2))
    weave = (target == 2 * (source % wide_z) + source // wide_z).astype(jnp.bfloat16)
    edge = lax.broadcasted_iota(jnp.int32, (cup, wide_z), 1) == wide_z - 1

    def later(value):
        return jnp.where(edge, 0.0, pltpu.roll(value, wide_z - 1, 1))

    for odd in range(2):
        if odd:
            left = jnp.concatenate([up_ref[18:27].reshape(9 * cup, cout), up_ref[0:9].reshape(9 * cup, cout)], axis=1)
            right = jnp.concatenate(hidden, axis=0)
        else:
            left = up_ref[9:18].reshape(9 * cup, cout)
            right = hidden[0]
        product = jnp.dot(left, right, preferred_element_type=jnp.float32)

        def term(tap_y, tap_z, y):
            at = (3 * tap_y + tap_z) * cup
            return product[at : at + cup, y * wide_z : (y + 1) * wide_z]

        lines = []
        for y in range(wide_y):
            for par_y in range(2):
                choices = [(1, y)] if par_y == 0 else [(2, y)] + ([(0, y + 1)] if y + 1 < wide_y else [])
                even = sum(term(tap_y, 1, at) for tap_y, at in choices)
                plain = sum(term(tap_y, 2, at) for tap_y, at in choices)
                moved = sum(term(tap_y, 0, at) for tap_y, at in choices)
                lines.append(jnp.concatenate([even, plain + later(moved)], axis=1).astype(jnp.bfloat16))
        woven = jnp.dot(jnp.concatenate(lines, axis=0), weave, preferred_element_type=jnp.float32)
        out_ref[odd] = woven.astype(jnp.bfloat16).reshape(2 * wide_y, cup, 2 * wide_z)


def partial_sums(order, span, total, scalars, vols, fars, weights, cout):
    _, wide_y, chans, wide_z = vols[0].shape
    cin = 2 * len(order) * chans
    shape = jax.ShapeDtypeStruct((2, wide_y, cout, wide_z), jnp.float32)
    return pl.pallas_call(
        functools.partial(conv_body, order, span, total),
        out_shape=(shape, shape),
        in_specs=[SMEM] + [VMEM] * (len(vols) + len(fars) + len(weights)),
        out_specs=(VMEM, VMEM),
        scratch_shapes=[
            pltpu.VMEM((5, wide_y + 2, cin, wide_z), jnp.bfloat16),
            pltpu.VMEM((3 * cout, 9 * cin), jnp.bfloat16),
        ],
        compiler_params=pltpu.CompilerParams(vmem_limit_bytes=24 * 2**20),
        cost_estimate=pl.CostEstimate(flops=2 * 10**9, bytes_accessed=4 * 10**6, transcendentals=0),
    )(scalars, *vols, *fars, *weights)


def upsample(total, plane, keep, came, bias, up):
    _, wide_y, _, wide_z = keep.shape
    return pl.pallas_call(
        functools.partial(up_body, total),
        out_shape=jax.ShapeDtypeStruct((2, 2 * wide_y, up.shape[1], 2 * wide_z), jnp.bfloat16),
        in_specs=[SMEM] + [VMEM] * 4,
        out_specs=VMEM,
        compiler_params=pltpu.CompilerParams(vmem_limit_bytes=24 * 2**20),
        cost_estimate=pl.CostEstimate(flops=10**9, bytes_accessed=3 * 10**6, transcendentals=0),
    )(jnp.reshape(plane, (1,)).astype(jnp.int32), keep, came, bias[None, :], up)


def per_device(volume, conv_weight, conv_bias, tconv_weight):
    total, size, groups = volume.shape[0], lax.axis_size("gx"), lax.axis_size("groups")
    tiles = size // TILE
    assert total == size and size % TILE == 0 and tiles & (tiles - 1) == 0 and groups & (groups - 1) == 0
    me, group = lax.axis_index("gx"), lax.axis_index("groups")
    tile, side, core = me // TILE, me // 2 % 2, me % 2
    vol = jnp.transpose(volume, (0, 2, 1, 3))
    weight = jnp.transpose(conv_weight, (1, 0, 2))
    cout = weight.shape[2]

    def cut(block, start, first, count):
        return lax.dynamic_slice_in_dim(block, window(first, count, total) - start, count, 0)

    def swap(block, mask):
        return lax.ppermute(block, "gx", [(i, i ^ mask) for i in range(size)])

    def cross(block, mask):
        return lax.ppermute(block, "groups", [(i, i ^ mask) for i in range(groups)])

    span = -(-27 // groups)
    held = lax.dynamic_slice_in_dim(weight, jnp.minimum(group * span, 27 - span), span, 0)[None]
    order, bit = [0], tiles // 2
    wide = min(7, total)
    came = {}

    def fetch(step):
        there = TILE * (tile ^ step) - 1
        came[step] = swap(cut(vol, 0, there, wide), TILE * step)

    while bit:
        held = jnp.concatenate([held, swap(held, TILE * bit)], axis=0)
        order = order + [place ^ bit for place in order]
        bit //= 2
    for step in reversed(range(1, tiles)):
        fetch(step)
    far = swap(held, 2)
    columns = [[held], [far]]
    for mask in range(1, groups):
        for column in columns:
            column.append(cross(column[0], mask))
    weights = [jnp.stack(column, axis=0) for column in columns]
    start = window(TILE * tile - 1, wide, total)
    theirs = TILE * tile + 2 * (1 - side) - 1
    own = TILE * tile + 2 * side - 1
    half = tiles // 2
    fars = []
    for steps in (range(half), range(half, tiles)):
        pieces = [cut(came[step], start, theirs, 5) if step else cut(vol, 0, theirs, 5) for step in steps]
        fars.append(swap(jnp.stack(pieces, axis=0), 2))
    vols = [came[step] if step else vol for step in order]
    starts = [start if step else jnp.zeros_like(start) for step in order]
    scalars = jnp.stack([core, group, own, *starts, window(own, 5, total)]).astype(jnp.int32)
    keep, send = partial_sums(tuple(order), span, total, scalars, vols, fars, weights, cout)
    out = upsample(total, me, keep, swap(send, 1), conv_bias, tconv_weight)
    return jnp.transpose(out, (0, 2, 1, 3))


def solution(mesh):
    return jax.shard_map(
        per_device,
        mesh=mesh,
        in_specs=(P("groups", "gx", None, None), P("gx", None, None), P(), P()),
        out_specs=P(("groups", "gx"), None, None, None),
        check_vma=False,
    )
```

time: 62.9 us -> 47.5 us (0.76)
  waiting for transfers between devices: 29.1 us -> 22.5 us
  starting transfers between devices: 20.4 us -> 16.3 us
  local copies, waits for them, and re-layouts: 6.91 us -> 2.86 us
  Pallas kernels: 6.08 us -> 5.38 us
    ppermute x30 -> x11, waiting for transfers between devices: 29.1 us -> 22.5 us  [the longest x9 18.1 us: swap(): return lax.ppermute(block, 'gx', [(i, i ^ mask) for i in range(size)])]
    ppermute x30 -> x11, starting transfers between devices: 20.4 us -> 16.3 us  [the longest x9 14.7 us: swap(): return lax.ppermute(block, 'gx', [(i, i ^ mask) for i in range(size)])]
    unnamed x16 -> x8, local copies, waits for them, and re-layouts: 3.73 us -> 1.56 us
    dynamic_slice x13 -> x1, local copies, waits for them, and re-layouts: 3.09 us -> 1.17 us  [cut(): lax.dynamic_slice_in_dim(block, window(first, count, total) - start, coun...]
    pallas_call x1 -> x2, Pallas kernels: 6.08 us -> 5.38 us  [the longest x1 3.26 us: partial_sums(): pl.pallas_call(functools.partial(conv_body, order, span, total), out_shap...]
  transfers between devices with their start and end apart: 30 -> 11, of which waited for: 12 -> 6; matrix products, arithmetic and copies ran while one was open for 5% -> 3% of each run, Pallas kernels for 0% -> 0%
where the time goes in v2:
time: 47.5 us; the launch traced here: 47.3 us
  waiting for transfers between devices  22.5 us (47%)
  starting transfers between devices  16.3 us (34%)
  Pallas kernels  5.38 us (11%)
  local copies, waits for them, and re-layouts  2.86 us (6%)
    ppermute x9, waiting for transfers between devices, swap(): return lax.ppermute(block, 'gx', [(i, i ^ mask) for i in range(size)])  18.1 us
    ppermute x9, starting transfers between devices, swap(): return lax.ppermute(block, 'gx', [(i, i ^ mask) for i in range(size)])  14.7 us
    ppermute x2, waiting for transfers between devices, cross(): return lax.ppermute(block, 'groups', [(i, i ^ mask) for i in range(groups)])  4.36 us
    pallas_call x1, Pallas kernels, partial_sums(): pl.pallas_call(functools.partial(conv_body, order, span, total), out_shap...  3.26 us
    pallas_call x1, Pallas kernels, upsample(): pl.pallas_call(functools.partial(up_body, total), out_shape=jax.ShapeDtyp...  2.11 us
    ppermute x2, starting transfers between devices, cross(): return lax.ppermute(block, 'groups', [(i, i ^ mask) for i in range(groups)])  1.56 us
    unnamed x8, local copies, waits for them, and re-layouts  1.56 us
    dynamic_slice x1, local copies, waits for them, and re-layouts, cut(): lax.dynamic_slice_in_dim(block, window(first, count, total) - start, coun...  1.17 us
  transfers between devices with their start and end apart: 11, of which 6 were waited for; matrix products, arithmetic and copies ran while one was open for 3% of the time, Pallas kernels for 0%

profile of v2, /device:TPU:0, one launch (start us, length us, event | category | flops | bytes accessed | tf_op | source)
XLA Modules:
  0.0 47.3 jit_solution(4904930699542989482)
XLA Ops:
  0.0 0.9 %copy-done = bf16[16,27,128]{2,0,1:T(8,128)(2,1)S(1)} copy-done((bf16[16,27,128]{2,0,1:T(8,128)(2,1)S(1)}, bf16[16,27,128]{2,0,1:T(8,128)(2,1)}, u32[]{:S(2)}) %copy-start) | copy-done | bytes 110616
  0.9 4.0 %collective-permute-start.5 = (bf16[1,14,16,128]{3,2,1,0:T(8,128)(2,1)S(1)}, bf16[1,14,16,128]{3,2,1,0:T(8,128)(2,1)S(1)}, u32[]{:S(2)}, u32[]{:S(2)}) collective-permute-start(bf16[1,14,16,128]{3,2,1,0:T(8,128)(2,1)S(1)} %dynamic-slice_bitcast_fusion.7), channel_id=1, source_target_pairs={{0,8},{1,9},{2,10},{3,11},{4,12},{5,13},{6,14},{7,15},{8,0},{9,1},... | collective-permute-start | bytes 172040 | tf_op jit(solution)/shard_map/ppermute | solution.py:167
  4.9 1.2 %dynamic-slice_bitcast_fusion = (bf16[7,6,16,128]{3,2,1,0:T(8,128)(2,1)S(1)}, bf16[7,6,16,128]{3,2,1,0:T(8,128)(2,1)S(1)}, bf16[7,6,16,128]{3,2,1,0:T(8,128)(2,1)S(1)}) fusion(bf16[16,16,6,128]{3,1,2,0:T(8,128)(2,1)} %param.4, s32[]{:T(128)S(6)} %min.29, s32[]{:T(128)S(6)} %min.28, s32[]{:T(128)S(6)} %min.27), kind=kLoop, calls=%fused_computation.5 | loop fusion | bytes 1032204 | tf_op jit(solution)/shard_map/dynamic_slice | solution.py:164
  6.1 1.4 %collective-permute-start.2 = (bf16[7,6,16,128]{3,2,1,0:T(8,128)(2,1)S(1)}, bf16[7,6,16,128]{3,2,1,0:T(8,128)(2,1)S(1)}, u32[]{:S(2)}, u32[]{:S(2)}) collective-permute-start(bf16[7,6,16,128]{3,2,1,0:T(8,128)(2,1)S(1)} %get-tuple-element.9), channel_id=1, source_target_pairs={{0,12},{1,13},{2,14},{3,15},{4,8},{5,9},{6,10},{7,11},{8,4},{9,5},... | collective-permute-start | bytes 516104 | tf_op jit(solution)/shard_map/ppermute | solution.py:167
  7.5 0.3 collective-permute-start.1
  7.8 2.7 %collective-permute-start = (bf16[7,6,16,128]{3,2,1,0:T(8,128)(2,1)S(1)}, bf16[7,6,16,128]{3,2,1,0:T(8,128)(2,1)S(1)}, u32[]{:S(2)}, u32[]{:S(2)}) collective-permute-start(bf16[7,6,16,128]{3,2,1,0:T(8,128)(2,1)S(1)} %get-tuple-element.11), channel_id=1, source_target_pairs={{0,8},{1,9},{2,10},{3,11},{4,12},{5,13},{6,14},{7,15},{8,0},{9,1},... | collective-permute-start | bytes 516104 | tf_op jit(solution)/shard_map/ppermute | solution.py:167
  10.6 0.0 collective-permute-done.5
  10.6 1.5 %collective-permute-start.6 = (bf16[2,14,16,128]{3,2,1,0:T(8,128)(2,1)S(1)}, bf16[2,14,16,128]{3,2,1,0:T(8,128)(2,1)S(1)}, u32[]{:S(2)}, u32[]{:S(2)}) collective-permute-start(bf16[2,14,16,128]{3,2,1,0:T(8,128)(2,1)S(1)} %pad_maximum_fusion.5), channel_id=1, source_target_pairs={{0,4},{1,5},{2,6},{3,7},{4,0},{5,1},{6,2},{7,3},{8,12},{9,13},{10,... | collective-permute-start | bytes 344072 | tf_op jit(solution)/shard_map/ppermute | solution.py:167
  12.1 0.1 stack.61.scalars
  12.2 8.6 %collective-permute-done.6 = bf16[2,14,16,128]{3,2,1,0:T(8,128)(2,1)S(1)} collective-permute-done((bf16[2,14,16,128]{3,2,1,0:T(8,128)(2,1)S(1)}, bf16[2,14,16,128]{3,2,1,0:T(8,128)(2,1)S(1)}, u32[]{:S(2)}, u32[]{:S(2)}) %collective-permute-start.6) | collective-permute-done | bytes 114720 | tf_op jit(solution)/shard_map/ppermute | solution.py:167
  20.8 1.6 %collective-permute-start.7 = (bf16[4,14,16,128]{3,2,1,0:T(8,128)(2,1)S(1)}, bf16[4,14,16,128]{3,2,1,0:T(8,128)(2,1)S(1)}, u32[]{:S(2)}, u32[]{:S(2)}) collective-permute-start(bf16[4,14,16,128]{3,2,1,0:T(8,128)(2,1)S(1)} %get-tuple-element.13), channel_id=1, source_target_pairs={{0,16},{16,0},{1,17},{17,1},{2,18},{18,2},{3,19},{19,3},{4,20},{20... | collective-permute-start | bytes 688136 | tf_op jit(solution)/shard_map/ppermute | solution.py:170
  22.4 1.5 %collective-permute-start.8 = (bf16[4,14,16,128]{3,2,1,0:T(8,128)(2,1)S(1)}, bf16[4,14,16,128]{3,2,1,0:T(8,128)(2,1)S(1)}, u32[]{:S(2)}, u32[]{:S(2)}) collective-permute-start(bf16[4,14,16,128]{3,2,1,0:T(8,128)(2,1)S(1)} %get-tuple-element.13), channel_id=1, source_target_pairs={{0,2},{1,3},{2,0},{3,1},{4,6},{5,7},{6,4},{7,5},{8,10},{9,11},{10,... | collective-permute-start | bytes 688136 | tf_op jit(solution)/shard_map/ppermute | solution.py:167
  23.9 0.2 collective-permute-done.refs_1_
  24.1 1.6 %collective-permute-start.4 = (bf16[2,5,6,16,128]{4,3,2,1,0:T(8,128)(2,1)S(1)}, bf16[2,5,6,16,128]{4,3,2,1,0:T(8,128)(2,1)S(1)}, u32[]{:S(2)}, u32[]{:S(2)}) collective-permute-start(bf16[2,5,6,16,128]{4,3,2,1,0:T(8,128)(2,1)S(1)} %pad_maximum_fusion.3), channel_id=1, source_target_pairs={{0,2},{1,3},{2,0},{3,1},{4,6},{5,7},{6,4},{7,5},{8,10},{9,11},{10,... | collective-permute-start | bytes 737288 | tf_op jit(solution)/shard_map/ppermute | solution.py:167
  25.7 0.0 collective-permute-done.1.refs_2_
  25.7 5.1 %collective-permute-done.8 = bf16[4,14,16,128]{3,2,1,0:T(8,128)(2,1)S(1)} collective-permute-done((bf16[4,14,16,128]{3,2,1,0:T(8,128)(2,1)S(1)}, bf16[4,14,16,128]{3,2,1,0:T(8,128)(2,1)S(1)}, u32[]{:S(2)}, u32[]{:S(2)}) %collective-permute-start.8) | collective-permute-done | bytes 229408 | tf_op jit(solution)/shard_map/ppermute | solution.py:167
  30.8 1.6 %collective-permute-start.3 = (bf16[2,5,6,16,128]{4,3,2,1,0:T(8,128)(2,1)S(1)}, bf16[2,5,6,16,128]{4,3,2,1,0:T(8,128)(2,1)S(1)}, u32[]{:S(2)}, u32[]{:S(2)}) collective-permute-start(bf16[2,5,6,16,128]{4,3,2,1,0:T(8,128)(2,1)S(1)} %pad_maximum_fusion.2), channel_id=1, source_target_pairs={{0,2},{1,3},{2,0},{3,1},{4,6},{5,7},{6,4},{7,5},{8,10},{9,11},{10,... | collective-permute-start | bytes 737288 | tf_op jit(solution)/shard_map/ppermute | solution.py:167
  32.5 4.4 %collective-permute-done.9 = bf16[4,14,16,128]{3,2,1,0:T(8,128)(2,1)S(1)} collective-permute-done((bf16[4,14,16,128]{3,2,1,0:T(8,128)(2,1)S(1)}, bf16[4,14,16,128]{3,2,1,0:T(8,128)(2,1)S(1)}, u32[]{:S(2)}, u32[]{:S(2)}) %collective-permute-start.9) | collective-permute-done | bytes 229408 | tf_op jit(solution)/shard_map/ppermute | solution.py:170
  36.9 2.0 %collective-permute-done.3.refs_4_ = bf16[2,5,6,16,128]{4,3,2,1,0:T(8,128)(2,1)S(1)} collective-permute-done((bf16[2,5,6,16,128]{4,3,2,1,0:T(8,128)(2,1)S(1)}, bf16[2,5,6,16,128]{4,3,2,1,0:T(8,128)(2,1)S(1)}, u32[]{:S(2)}, u32[]{:S(2)}) %collective-permute-start.3) | collective-permute-done | bytes 245792 | tf_op jit(solution)/shard_map/ppermute | solution.py:167
  38.9 3.3 %shard_map.46 = (f32[2,6,128,128]{3,2,1,0:T(8,128)S(1)}, f32[2,6,128,128]{3,2,1,0:T(8,128)S(1)}) custom-call(s32[8]{0:T(128)S(1)} %stack.61.scalars, bf16[16,6,16,128]{3,2,1,0:T(8,128)(2,1)S(1)} %bitcast.34, bf16[7,6,16,128]{3,2,1,0:T(8,128)(2,1)S(1)} %collective-permute-done.refs_1_, bf16[7,6,16,128]{3,2,1,0:T(8,128)(2,1)S(1)} %collective-permute-done.1.refs_2_, ...), custom_call_target="tpu_custom_call" | custom-call | flops 2000000000 | bytes 4000000 | tf_op jit(solution)/shard_map/pallas_call | solution.py:127
  42.2 0.1 collective-permute-start.10
  42.3 2.3 %collective-permute-done.10.came_ref = f32[2,6,128,128]{3,2,1,0:T(8,128)S(1)} collective-permute-done((f32[2,6,128,128]{3,2,1,0:T(8,128)S(1)}, f32[2,6,128,128]{3,2,1,0:T(8,128)S(1)}, u32[]{:S(2)}, u32[]{:S(2)}) %collective-permute-start.10) | collective-permute-done | bytes 786464 | tf_op jit(solution)/shard_map/ppermute | solution.py:167
  44.5 0.7 %copy-done.3 = f32[128]{0:T(128)S(1)} copy-done((f32[128]{0:T(128)S(1)}, f32[128]{0:T(128)}, u32[]{:S(2)}) %copy-start.3) | copy-done | bytes 536
  45.2 2.1 %shard_map.47 = bf16[2,12,64,256]{3,2,1,0:T(8,128)(2,1)} custom-call(s32[1]{0:T(128)} %bitcast.scalars, f32[2,6,128,128]{3,2,1,0:T(8,128)S(1)} %get-tuple-element.7.keep_ref, f32[2,6,128,128]{3,2,1,0:T(8,128)S(1)} %collective-permute-done.10.came_ref, f32[1,128]{1,0:T(1,128)S(1)} %bitcast.35, bf16[27,64,128]{2,1,0:T(8,128)(2,1)S(1)} %copy-done.2), custom_call_target="tpu_custom_call" | custom-call | flops 1000000000 | bytes 3000000 | tf_op jit(solution)/shard_map/pallas_call | solution.py:143
  (21 shorter events, 0.2 us)
Async XLA Ops:
  0.0 0.9 %copy-start = (bf16[16,27,128]{2,0,1:T(8,128)(2,1)S(1)}, bf16[16,27,128]{2,0,1:T(8,128)(2,1)}, u32[]{:S(2)}) copy-start(bf16[16,27,128]{2,0,1:T(8,128)(2,1)} %param.5) | copy-start | bytes 331780
  0.9 9.7 %collective-permute-start.5 = (bf16[1,14,16,128]{3,2,1,0:T(8,128)(2,1)S(1)}, bf16[1,14,16,128]{3,2,1,0:T(8,128)(2,1)S(1)}, u32[]{:S(2)}, u32[]{:S(2)}) collective-permute-start(bf16[1,14,16,128]{3,2,1,0:T(8,128)(2,1)S(1)} %dynamic-slice_bitcast_fusion.7), channel_id=1, source_target_pairs={{0,8},{1,9},{2,10},{3,11},{4,12},{5,13},{6,14},{7,15},{8,0},{9,1},... | collective-permute-start | bytes 172040 | tf_op jit(solution)/shard_map/ppermute | solution.py:167
  4.9 7.1 %copy-start.1 = (bf16[16,16,6,128]{3,1,2,0:T(8,128)(2,1)S(1)}, bf16[16,16,6,128]{3,1,2,0:T(8,128)(2,1)}, u32[]{:S(2)}) copy-start(bf16[16,16,6,128]{3,1,2,0:T(8,128)(2,1)} %param.4) | copy-start | bytes 1179652
  6.1 17.8 %collective-permute-start.2 = (bf16[7,6,16,128]{3,2,1,0:T(8,128)(2,1)S(1)}, bf16[7,6,16,128]{3,2,1,0:T(8,128)(2,1)S(1)}, u32[]{:S(2)}, u32[]{:S(2)}) collective-permute-start(bf16[7,6,16,128]{3,2,1,0:T(8,128)(2,1)S(1)} %get-tuple-element.9), channel_id=1, source_target_pairs={{0,12},{1,13},{2,14},{3,15},{4,8},{5,9},{6,10},{7,11},{8,4},{9,5},... | collective-permute-start | bytes 516104 | tf_op jit(solution)/shard_map/ppermute | solution.py:167
  7.5 18.2 %collective-permute-start.1 = (bf16[7,6,16,128]{3,2,1,0:T(8,128)(2,1)S(1)}, bf16[7,6,16,128]{3,2,1,0:T(8,128)(2,1)S(1)}, u32[]{:S(2)}, u32[]{:S(2)}) collective-permute-start(bf16[7,6,16,128]{3,2,1,0:T(8,128)(2,1)S(1)} %get-tuple-element.10), channel_id=1, source_target_pairs={{0,4},{1,5},{2,6},{3,7},{4,0},{5,1},{6,2},{7,3},{8,12},{9,13},{10,... | collective-permute-start | bytes 516104 | tf_op jit(solution)/shard_map/ppermute | solution.py:167
  7.8 16.3 %collective-permute-start = (bf16[7,6,16,128]{3,2,1,0:T(8,128)(2,1)S(1)}, bf16[7,6,16,128]{3,2,1,0:T(8,128)(2,1)S(1)}, u32[]{:S(2)}, u32[]{:S(2)}) collective-permute-start(bf16[7,6,16,128]{3,2,1,0:T(8,128)(2,1)S(1)} %get-tuple-element.11), channel_id=1, source_target_pairs={{0,8},{1,9},{2,10},{3,11},{4,12},{5,13},{6,14},{7,15},{8,0},{9,1},... | collective-permute-start | bytes 516104 | tf_op jit(solution)/shard_map/ppermute | solution.py:167
  10.6 10.2 %collective-permute-start.6 = (bf16[2,14,16,128]{3,2,1,0:T(8,128)(2,1)S(1)}, bf16[2,14,16,128]{3,2,1,0:T(8,128)(2,1)S(1)}, u32[]{:S(2)}, u32[]{:S(2)}) collective-permute-start(bf16[2,14,16,128]{3,2,1,0:T(8,128)(2,1)S(1)} %pad_maximum_fusion.5), channel_id=1, source_target_pairs={{0,4},{1,5},{2,6},{3,7},{4,0},{5,1},{6,2},{7,3},{8,12},{9,13},{10,... | collective-permute-start | bytes 344072 | tf_op jit(solution)/shard_map/ppermute | solution.py:167
  20.8 11.6 %collective-permute-start.7 = (bf16[4,14,16,128]{3,2,1,0:T(8,128)(2,1)S(1)}, bf16[4,14,16,128]{3,2,1,0:T(8,128)(2,1)S(1)}, u32[]{:S(2)}, u32[]{:S(2)}) collective-permute-start(bf16[4,14,16,128]{3,2,1,0:T(8,128)(2,1)S(1)} %get-tuple-element.13), channel_id=1, source_target_pairs={{0,16},{16,0},{1,17},{17,1},{2,18},{18,2},{3,19},{19,3},{4,20},{20... | collective-permute-start | bytes 688136 | tf_op jit(solution)/shard_map/ppermute | solution.py:170
  22.4 8.4 %collective-permute-start.8 = (bf16[4,14,16,128]{3,2,1,0:T(8,128)(2,1)S(1)}, bf16[4,14,16,128]{3,2,1,0:T(8,128)(2,1)S(1)}, u32[]{:S(2)}, u32[]{:S(2)}) collective-permute-start(bf16[4,14,16,128]{3,2,1,0:T(8,128)(2,1)S(1)} %get-tuple-element.13), channel_id=1, source_target_pairs={{0,2},{1,3},{2,0},{3,1},{4,6},{5,7},{6,4},{7,5},{8,10},{9,11},{10,... | collective-permute-start | bytes 688136 | tf_op jit(solution)/shard_map/ppermute | solution.py:167
  24.1 12.7 %collective-permute-start.4 = (bf16[2,5,6,16,128]{4,3,2,1,0:T(8,128)(2,1)S(1)}, bf16[2,5,6,16,128]{4,3,2,1,0:T(8,128)(2,1)S(1)}, u32[]{:S(2)}, u32[]{:S(2)}) collective-permute-start(bf16[2,5,6,16,128]{4,3,2,1,0:T(8,128)(2,1)S(1)} %pad_maximum_fusion.3), channel_id=1, source_target_pairs={{0,2},{1,3},{2,0},{3,1},{4,6},{5,7},{6,4},{7,5},{8,10},{9,11},{10,... | collective-permute-start | bytes 737288 | tf_op jit(solution)/shard_map/ppermute | solution.py:167
  30.8 6.0 %collective-permute-start.9 = (bf16[4,14,16,128]{3,2,1,0:T(8,128)(2,1)S(1)}, bf16[4,14,16,128]{3,2,1,0:T(8,128)(2,1)S(1)}, u32[]{:S(2)}, u32[]{:S(2)}) collective-permute-start(bf16[4,14,16,128]{3,2,1,0:T(8,128)(2,1)S(1)} %collective-permute-done.8), channel_id=1, source_target_pairs={{0,16},{16,0},{1,17},{17,1},{2,18},{18,2},{3,19},{19,3},{4,20},{20... | collective-permute-start | bytes 688136 | tf_op jit(solution)/shard_map/ppermute | solution.py:170
  30.8 8.1 %collective-permute-start.3 = (bf16[2,5,6,16,128]{4,3,2,1,0:T(8,128)(2,1)S(1)}, bf16[2,5,6,16,128]{4,3,2,1,0:T(8,128)(2,1)S(1)}, u32[]{:S(2)}, u32[]{:S(2)}) collective-permute-start(bf16[2,5,6,16,128]{4,3,2,1,0:T(8,128)(2,1)S(1)} %pad_maximum_fusion.2), channel_id=1, source_target_pairs={{0,2},{1,3},{2,0},{3,1},{4,6},{5,7},{6,4},{7,5},{8,10},{9,11},{10,... | collective-permute-start | bytes 737288 | tf_op jit(solution)/shard_map/ppermute | solution.py:167
  38.9 5.6 %copy-start.2 = (bf16[27,64,128]{2,1,0:T(8,128)(2,1)S(1)}, bf16[27,64,128]{2,1,0:T(8,128)(2,1)}, u32[]{:S(2)}) copy-start(bf16[27,64,128]{2,1,0:T(8,128)(2,1)} %up_ref.1) | copy-start | bytes 1327108
  42.2 2.4 %collective-permute-start.10 = (f32[2,6,128,128]{3,2,1,0:T(8,128)S(1)}, f32[2,6,128,128]{3,2,1,0:T(8,128)S(1)}, u32[]{:S(2)}, u32[]{:S(2)}) collective-permute-start(f32[2,6,128,128]{3,2,1,0:T(8,128)S(1)} %get-tuple-element.8), channel_id=1, source_target_pairs={{0,1},{1,0},{2,3},{3,2},{4,5},{5,4},{6,7},{7,6},{8,9},{9,8},{10,11... | collective-permute-start | bytes 2359304 | tf_op jit(solution)/shard_map/ppermute | solution.py:167
  44.5 0.7 %copy-start.3 = (f32[128]{0:T(128)S(1)}, f32[128]{0:T(128)}, u32[]{:S(2)}) copy-start(f32[128]{0:T(128)} %param.6) | copy-start | bytes 1540

commit v3 on v1

v3 whole, which is shorter than its diff:
```python
import functools

import jax
import jax.numpy as jnp
from jax import lax
from jax.experimental import pallas as pl
from jax.experimental.pallas import tpu as pltpu
from jax.sharding import PartitionSpec as P

TILE = 4
VMEM = pl.BlockSpec(memory_space=pltpu.VMEM)
SMEM = pl.BlockSpec(memory_space=pltpu.SMEM)
PARAMS = pltpu.CompilerParams(vmem_limit_bytes=16 * 2**20)


def window(first, count, total):
    return jnp.clip(first, 0, total - count)


def after(value, *earlier):
    return lax.optimization_barrier((value, *earlier))[0]


def cut_body(counts, scalars, vol_ref, *outs):
    for at, (out_ref, count) in enumerate(zip(outs, counts)):
        out_ref[...] = vol_ref[pl.ds(scalars[at], count)]


def cuts(vol, starts, counts):
    return pl.pallas_call(
        functools.partial(cut_body, counts),
        out_shape=[jax.ShapeDtypeStruct((count, *vol.shape[1:]), vol.dtype) for count in counts],
        in_specs=[SMEM, VMEM],
        out_specs=[VMEM] * len(counts),
        compiler_params=PARAMS,
    )(jnp.stack(starts).astype(jnp.int32), vol)


def taps_body(near_order, far_order, span, scalars, *refs):
    weights, out_ref = refs[:-1], refs[-1]
    group = scalars[0]
    cout = out_ref.shape[0] // 3
    for tap_z in range(3):
        pieces = []
        for tap in range(tap_z, 27, 3):
            part = tap // span
            start = min(part * span, 27 - span)
            for weight, order in zip(weights, (near_order, far_order)):
                pieces += [weight[group ^ part, place, tap - start] for place in order]
        out_ref[tap_z * cout : (tap_z + 1) * cout] = jnp.concatenate(pieces, axis=0).T


def taps_of(near_order, far_order, span, group, weights):
    cout, chans = weights[0].shape[-1], weights[0].shape[-2]
    columns = 9 * chans * (len(near_order) + len(far_order))
    return pl.pallas_call(
        functools.partial(taps_body, near_order, far_order, span),
        out_shape=jax.ShapeDtypeStruct((3 * cout, columns), jnp.bfloat16),
        in_specs=[SMEM] + [VMEM] * len(weights),
        out_specs=VMEM,
        compiler_params=PARAMS,
        cost_estimate=pl.CostEstimate(flops=0, bytes_accessed=3 * 10**6, transcendentals=0),
    )(jnp.reshape(group, (1,)).astype(jnp.int32), *weights)


def conv_rows(total, steps, scalars, refs, taps, plane, store):
    near, far = refs[:steps], [ref.at[at] for ref in refs[steps:] for at in range(ref.shape[0])]
    parts = [*near, *far]
    _, wide_y, chans, wide_z = near[0].shape
    cout = taps.shape[0] // 3
    lane = lax.broadcasted_iota(jnp.int32, (cout, wide_z), 1)
    zeros = jnp.zeros((len(parts) * chans, wide_z), taps.dtype)

    def row(at, y):
        if not 0 <= y < wide_y:
            return zeros
        held = [ref[jnp.clip(at - scalars[2 + place], 0, ref.shape[0] - 1), y] for place, ref in enumerate(parts)]
        return jnp.where(jnp.logical_and(at >= 0, at < total), jnp.concatenate(held, axis=0), zeros)

    for pair in range(0, wide_y, 2):
        blocks = []
        for tap_x in range(3):
            for tap_y in range(3):
                y = pair + tap_y - 1
                blocks.append(jnp.concatenate([row(plane + tap_x - 1, y), row(plane + tap_x - 1, y + 1)], axis=1))
        acc = jnp.dot(taps[...], jnp.concatenate(blocks, axis=0), preferred_element_type=jnp.float32)
        for side in range(2):
            part = acc[:, side * wide_z : (side + 1) * wide_z]
            low = jnp.where(lane == 0, 0.0, pltpu.roll(part[:cout], 1, 1))
            high = jnp.where(lane == wide_z - 1, 0.0, pltpu.roll(part[2 * cout :], wide_z - 1, 1))
            store(pair + side, part[cout : 2 * cout] + low + high)


def send_body(total, steps, scalars, *refs):
    *parts, taps, out_ref = refs
    core, first = scalars[0], scalars[1]
    for at, plane in enumerate((first + 1, first + 2 * (1 - core))):

        def store(y, value, at=at):
            out_ref[at, y] = value

        conv_rows(total, steps, scalars, parts, taps, plane, store)


def keep_body(total, steps, scalars, *refs):
    *parts, taps, shared_ref, bias_ref, out_ref = refs
    core, first = scalars[0], scalars[1]
    bias = bias_ref[...]
    plane = first + 2 * core
    inside = plane < total

    def store(y, value):
        out_ref[core, y] = jnp.where(inside, value + bias, -jnp.inf)
        out_ref[1 - core, y] = shared_ref[0, y] + bias

    conv_rows(total, steps, scalars, parts, taps, plane, store)


def conv_call(body, total, steps, scalars, parts, taps, *more):
    _, wide_y, _, wide_z = parts[0].shape
    cout = taps.shape[0] // 3
    return pl.pallas_call(
        functools.partial(body, total, steps),
        out_shape=jax.ShapeDtypeStruct((2, wide_y, cout, wide_z), jnp.float32),
        in_specs=[SMEM] + [VMEM] * (len(parts) + 1 + len(more)),
        out_specs=VMEM,
        compiler_params=PARAMS,
        cost_estimate=pl.CostEstimate(flops=10**9, bytes_accessed=4 * 10**6, transcendentals=0),
    )(scalars, *parts, taps, *more)


def up_body(scalars, keep_ref, came_ref, up_ref, out_ref):
    core = scalars[0]
    _, wide_y, cout, wide_z = keep_ref.shape
    cup = up_ref.shape[1]
    hidden = []
    for ahead in range(2):
        at = jnp.where(core == ahead, 1, 0)
        rows = [jnp.maximum(keep_ref[ahead, y] + came_ref[at, y], 0.0).astype(jnp.bfloat16) for y in range(wide_y)]
        hidden.append(jnp.concatenate(rows, axis=1))
    shape = (2 * wide_z, 2 * wide_z)
    source, target = (lax.broadcasted_iota(jnp.int32, shape, axis) for axis in range(2))
    weave = (target == 2 * (source % wide_z) + source // wide_z).astype(jnp.bfloat16)
    edge = lax.broadcasted_iota(jnp.int32, (cup, wide_z), 1) == wide_z - 1

    def later(value):
        return jnp.where(edge, 0.0, pltpu.roll(value, wide_z - 1, 1))

    for odd in range(2):
        if odd:
            left = jnp.concatenate([up_ref[18:27].reshape(9 * cup, cout), up_ref[0:9].reshape(9 * cup, cout)], axis=1)
            right = jnp.concatenate(hidden, axis=0)
        else:
            left = up_ref[9:18].reshape(9 * cup, cout)
            right = hidden[0]
        product = jnp.dot(left, right, preferred_element_type=jnp.float32)

        def term(tap_y, tap_z, y):
            at = (3 * tap_y + tap_z) * cup
            return product[at : at + cup, y * wide_z : (y + 1) * wide_z]

        lines = []
        for y in range(wide_y):
            for par_y in range(2):
                choices = [(1, y)] if par_y == 0 else [(2, y)] + ([(0, y + 1)] if y + 1 < wide_y else [])
                even = sum(term(tap_y, 1, at) for tap_y, at in choices)
                plain = sum(term(tap_y, 2, at) for tap_y, at in choices)
                moved = sum(term(tap_y, 0, at) for tap_y, at in choices)
                lines.append(jnp.concatenate([even, plain + later(moved)], axis=1).astype(jnp.bfloat16))
        woven = jnp.dot(jnp.concatenate(lines, axis=0), weave, preferred_element_type=jnp.float32)
        out_ref[odd] = woven.astype(jnp.bfloat16).reshape(2 * wide_y, cup, 2 * wide_z)


def upsample(scalars, keep, came, up):
    _, wide_y, _, wide_z = keep.shape
    return pl.pallas_call(
        up_body,
        out_shape=jax.ShapeDtypeStruct((2, 2 * wide_y, up.shape[1], 2 * wide_z), jnp.bfloat16),
        in_specs=[SMEM] + [VMEM] * 3,
        out_specs=VMEM,
        compiler_params=PARAMS,
        cost_estimate=pl.CostEstimate(flops=10**9, bytes_accessed=3 * 10**6, transcendentals=0),
    )(scalars, keep, came, up)


def per_device(volume, conv_weight, conv_bias, tconv_weight):
    total, size, groups = volume.shape[0], lax.axis_size("gx"), lax.axis_size("groups")
    tiles = size // TILE
    assert total == size and size % TILE == 0 and tiles & (tiles - 1) == 0 and groups & (groups - 1) == 0
    me, group = lax.axis_index("gx"), lax.axis_index("groups")
    tile, side, core = me // TILE, me // 2 % 2, me % 2
    vol = jnp.transpose(volume, (0, 2, 1, 3))
    weight = jnp.transpose(conv_weight, (1, 0, 2))

    def swap(block, mask):
        return lax.ppermute(block, "gx", [(i, i ^ mask) for i in range(size)])

    def cross(block, mask):
        return lax.ppermute(block, "groups", [(i, i ^ mask) for i in range(groups)])

    wide = min(7, total)
    start = window(TILE * tile - 1, wide, total)
    theirs = window(TILE * tile + 2 * (1 - side) - 1, 5, total)
    own = TILE * tile + 2 * side
    steps = range(tiles)
    firsts = [window(TILE * (tile ^ step) - 1, wide, total) for step in steps[1:]]
    far_own, *pieces = cuts(vol, [theirs, *firsts], [5] + [wide] * (tiles - 1))
    span = -(-27 // groups)
    held = lax.dynamic_slice_in_dim(weight, jnp.minimum(group * span, 27 - span), span, 0)
    held, bias, *pieces = lax.optimization_barrier(
        (held, jnp.broadcast_to(conv_bias[:, None], (weight.shape[2], vol.shape[3])), *pieces)
    )
    held = jnp.stack([held] + [swap(held, TILE * step) for step in steps[1:]], axis=0)
    near = [vol]
    for step, piece in zip(steps[1:], pieces):
        near.append(swap(after(piece, held) if step % 4 == 2 else piece, TILE * step))
    far_held = swap(held, 2)
    columns = [jnp.stack([part] + [cross(part, mask) for mask in range(1, groups)], axis=0) for part in (held, far_held)]
    far_order = [[0, 1]] + [[step] for step in steps[2:]]
    far = []
    for chosen in far_order:
        cut = [lax.dynamic_slice_in_dim(near[step], theirs - start, 5, 0) if step else far_own for step in chosen]
        far.append(swap(jnp.stack(cut, axis=0), 2))
    taps = taps_of(tuple(steps), tuple(step for chosen in far_order for step in chosen), span, group, columns)
    starts = [jnp.zeros_like(start)] + [start] * (tiles - 1) + [window(own - 1, 5, total)] * tiles
    scalars = jnp.stack([core, own, *starts]).astype(jnp.int32)
    parts = near + far
    shared = conv_call(send_body, total, tiles, scalars, parts, taps)
    came = swap(shared, 1)
    keep = conv_call(keep_body, total, tiles, scalars, parts, taps, shared, bias)
    out = upsample(scalars[:1], keep, came, tconv_weight)
    return jnp.transpose(out, (0, 2, 1, 3))


def solution(mesh):
    return jax.shard_map(
        per_device,
        mesh=mesh,
        in_specs=(P("groups", "gx", None, None), P("gx", None, None), P(), P()),
        out_specs=P(("groups", "gx"), None, None, None),
        check_vma=False,
    )
```

time: 62.9 us -> 39.5 us (0.63)
  waiting for transfers between devices: 29.1 us -> 12.7 us
  local copies, waits for them, and re-layouts: 6.91 us -> 2.16 us
  starting transfers between devices: 20.4 us -> 17.4 us
  Pallas kernels: 6.08 us -> 6.78 us
    ppermute x30 -> x13, waiting for transfers between devices: 29.1 us -> 12.7 us  [the longest x11 12.1 us: swap(): return lax.ppermute(block, 'gx', [(i, i ^ mask) for i in range(size)])]
    dynamic_slice x13 -> x1, local copies, waits for them, and re-layouts: 3.09 us -> 0.01 us  [per_device(): lax.dynamic_slice_in_dim(weight, jnp.minimum(group * span, 27 - span), sp...]
    ppermute x30 -> x13, starting transfers between devices: 20.4 us -> 17.4 us  [the longest x11 15.6 us: swap(): return lax.ppermute(block, 'gx', [(i, i ^ mask) for i in range(size)])]
    unnamed x16 -> x10, local copies, waits for them, and re-layouts: 3.73 us -> 1.97 us
    pallas_call x1 -> x5, Pallas kernels: 6.08 us -> 6.78 us  [the longest x2 3.88 us: conv_call(): pl.pallas_call(functools.partial(body, total, steps), out_shape=jax.Shape...]
  transfers between devices with their start and end apart: 30 -> 13, of which waited for: 12 -> 7; matrix products, arithmetic and copies ran while one was open for 5% -> 1% of each run, Pallas kernels for 0% -> 5%
where the time goes in v3:
time: 39.5 us; the launch traced here: 39.3 us
  starting transfers between devices  17.4 us (44%)
  waiting for transfers between devices  12.7 us (32%)
  Pallas kernels  6.78 us (17%)
  local copies, waits for them, and re-layouts  2.16 us (5%)
    ppermute x11, starting transfers between devices, swap(): return lax.ppermute(block, 'gx', [(i, i ^ mask) for i in range(size)])  15.6 us
    ppermute x11, waiting for transfers between devices, swap(): return lax.ppermute(block, 'gx', [(i, i ^ mask) for i in range(size)])  12.1 us
    pallas_call x2, Pallas kernels, conv_call(): pl.pallas_call(functools.partial(body, total, steps), out_shape=jax.Shape...  3.88 us
    pallas_call x1, Pallas kernels, upsample(): pl.pallas_call(up_body, out_shape=jax.ShapeDtypeStruct((2, 2 * wide_y, up...  2.02 us
    unnamed x10, local copies, waits for them, and re-layouts  1.97 us
    ppermute x2, starting transfers between devices, cross(): return lax.ppermute(block, 'groups', [(i, i ^ mask) for i in range(groups)])  1.72 us
  transfers between devices with their start and end apart: 13, of which 7 were waited for; matrix products, arithmetic and copies ran while one was open for 1% of the time, Pallas kernels for 5%

profile of v3, /device:TPU:0, one launch (start us, length us, event | category | flops | bytes accessed | tf_op | source)
XLA Modules:
  0.0 39.3 jit_solution(13381848179801872690)
XLA Ops:
  0.0 0.9 %copy-done = bf16[16,27,128]{2,0,1:T(8,128)(2,1)S(1)} copy-done((bf16[16,27,128]{2,0,1:T(8,128)(2,1)S(1)}, bf16[16,27,128]{2,0,1:T(8,128)(2,1)}, u32[]{:S(2)}) %copy-start) | copy-done | bytes 110616
  1.0 1.0 %copy-done.1 = bf16[16,16,6,128]{3,1,2,0:T(8,128)(2,1)S(1)} copy-done((bf16[16,16,6,128]{3,1,2,0:T(8,128)(2,1)S(1)}, bf16[16,16,6,128]{3,1,2,0:T(8,128)(2,1)}, u32[]{:S(2)}) %copy-start.1) | copy-done | bytes 393240
  2.0 0.6 %shard_map.46 = (bf16[5,6,16,128]{3,2,1,0:T(8,128)(2,1)S(1)}, bf16[7,6,16,128]{3,2,1,0:T(8,128)(2,1)S(1)}, bf16[7,6,16,128]{3,2,1,0:T(8,128)(2,1)S(1)}, bf16[7,6,16,128]{3,2,1,0:T(8,128)(2,1)S(1)}) custom-call(s32[4]{0:T(128)S(1)} %pad_add_fusion.scalars, bf16[16,6,16,128]{3,2,1,0:T(8,128)(2,1)S(1)} %bitcast.29), custom_call_target="tpu_custom_call" | custom-call | tf_op jit(solution)/shard_map/pallas_call | solution.py:30
  2.7 5.1 %collective-permute-start.3 = (bf16[14,16,128]{2,1,0:T(8,128)(2,1)S(1)}, bf16[14,16,128]{2,1,0:T(8,128)(2,1)S(1)}, u32[]{:S(2)}, u32[]{:S(2)}) collective-permute-start(bf16[14,16,128]{2,1,0:T(8,128)(2,1)S(1)} %dynamic-slice_bitcast_fusion.3), channel_id=1, source_target_pairs={{0,12},{1,13},{2,14},{3,15},{4,8},{5,9},{6,10},{7,11},{8,4},{9,5},... | collective-permute-start | bytes 172040 | tf_op jit(solution)/shard_map/ppermute | solution.py:196
  7.8 0.6 %collective-permute-start.1 = (bf16[14,16,128]{2,1,0:T(8,128)(2,1)S(1)}, bf16[14,16,128]{2,1,0:T(8,128)(2,1)S(1)}, u32[]{:S(2)}, u32[]{:S(2)}) collective-permute-start(bf16[14,16,128]{2,1,0:T(8,128)(2,1)S(1)} %dynamic-slice_bitcast_fusion.3), channel_id=1, source_target_pairs={{0,4},{1,5},{2,6},{3,7},{4,0},{5,1},{6,2},{7,3},{8,12},{9,13},{10,... | collective-permute-start | bytes 172040 | tf_op jit(solution)/shard_map/ppermute | solution.py:196
  8.4 3.7 %collective-permute-start.5 = (bf16[7,6,16,128]{3,2,1,0:T(8,128)(2,1)S(1)}, bf16[7,6,16,128]{3,2,1,0:T(8,128)(2,1)S(1)}, u32[]{:S(2)}, u32[]{:S(2)}) collective-permute-start(bf16[7,6,16,128]{3,2,1,0:T(8,128)(2,1)S(1)} %get-tuple-element.22), channel_id=1, source_target_pairs={{0,12},{1,13},{2,14},{3,15},{4,8},{5,9},{6,10},{7,11},{8,4},{9,5},... | collective-permute-start | bytes 516104 | tf_op jit(solution)/shard_map/ppermute | solution.py:196
  12.2 0.1 stack.87.scalars
  12.3 3.5 %collective-permute-done.2 = bf16[14,16,128]{2,1,0:T(8,128)(2,1)S(1)} collective-permute-done((bf16[14,16,128]{2,1,0:T(8,128)(2,1)S(1)}, bf16[14,16,128]{2,1,0:T(8,128)(2,1)S(1)}, u32[]{:S(2)}, u32[]{:S(2)}) %collective-permute-start.2) | collective-permute-done | bytes 57376 | tf_op jit(solution)/shard_map/ppermute | solution.py:196
  15.8 1.6 %collective-permute-start.9 = (bf16[4,14,16,128]{3,2,1,0:T(8,128)(2,1)S(1)}, bf16[4,14,16,128]{3,2,1,0:T(8,128)(2,1)S(1)}, u32[]{:S(2)}, u32[]{:S(2)}) collective-permute-start(bf16[4,14,16,128]{3,2,1,0:T(8,128)(2,1)S(1)} %get-tuple-element.26), channel_id=1, source_target_pairs={{0,16},{16,0},{1,17},{17,1},{2,18},{18,2},{3,19},{19,3},{4,20},{20... | collective-permute-start | bytes 688136 | tf_op jit(solution)/shard_map/ppermute | solution.py:199
  17.4 1.5 %collective-permute-start.10 = (bf16[4,14,16,128]{3,2,1,0:T(8,128)(2,1)S(1)}, bf16[4,14,16,128]{3,2,1,0:T(8,128)(2,1)S(1)}, u32[]{:S(2)}, u32[]{:S(2)}) collective-permute-start(bf16[4,14,16,128]{3,2,1,0:T(8,128)(2,1)S(1)} %get-tuple-element.26), channel_id=1, source_target_pairs={{0,2},{1,3},{2,0},{3,1},{4,6},{5,7},{6,4},{7,5},{8,10},{9,11},{10,... | collective-permute-start | bytes 688136 | tf_op jit(solution)/shard_map/ppermute | solution.py:196
  18.9 1.4 %collective-permute-start.8 = (bf16[1,5,6,16,128]{4,3,2,1,0:T(8,128)(2,1)S(1)}, bf16[1,5,6,16,128]{4,3,2,1,0:T(8,128)(2,1)S(1)}, u32[]{:S(2)}, u32[]{:S(2)}) collective-permute-start(bf16[1,5,6,16,128]{4,3,2,1,0:T(8,128)(2,1)S(1)} %dynamic-slice_bitcast_fusion), channel_id=1, source_target_pairs={{0,2},{1,3},{2,0},{3,1},{4,6},{5,7},{6,4},{7,5},{8,10},{9,11},{10,... | collective-permute-start | bytes 368648 | tf_op jit(solution)/shard_map/ppermute | solution.py:196
  20.3 0.4 %collective-permute-done.refs_1_ = bf16[7,6,16,128]{3,2,1,0:T(8,128)(2,1)S(1)} collective-permute-done((bf16[7,6,16,128]{3,2,1,0:T(8,128)(2,1)S(1)}, bf16[7,6,16,128]{3,2,1,0:T(8,128)(2,1)S(1)}, u32[]{:S(2)}, u32[]{:S(2)}) %collective-permute-start) | collective-permute-done | bytes 172064 | tf_op jit(solution)/shard_map/ppermute | solution.py:196
  20.8 1.6 %collective-permute-start.6 = (bf16[2,5,6,16,128]{4,3,2,1,0:T(8,128)(2,1)S(1)}, bf16[2,5,6,16,128]{4,3,2,1,0:T(8,128)(2,1)S(1)}, u32[]{:S(2)}, u32[]{:S(2)}) collective-permute-start(bf16[2,5,6,16,128]{4,3,2,1,0:T(8,128)(2,1)S(1)} %pad_maximum_fusion.2), channel_id=1, source_target_pairs={{0,2},{1,3},{2,0},{3,1},{4,6},{5,7},{6,4},{7,5},{8,10},{9,11},{10,... | collective-permute-start | bytes 737288 | tf_op jit(solution)/shard_map/ppermute | solution.py:196
  22.4 1.4 %collective-permute-done.10 = bf16[4,14,16,128]{3,2,1,0:T(8,128)(2,1)S(1)} collective-permute-done((bf16[4,14,16,128]{3,2,1,0:T(8,128)(2,1)S(1)}, bf16[4,14,16,128]{3,2,1,0:T(8,128)(2,1)S(1)}, u32[]{:S(2)}, u32[]{:S(2)}) %collective-permute-start.10) | collective-permute-done | bytes 229408 | tf_op jit(solution)/shard_map/ppermute | solution.py:196
  23.8 0.2 collective-permute-start.11
  23.9 3.6 %collective-permute-done.4.refs_2_ = bf16[7,6,16,128]{3,2,1,0:T(8,128)(2,1)S(1)} collective-permute-done((bf16[7,6,16,128]{3,2,1,0:T(8,128)(2,1)S(1)}, bf16[7,6,16,128]{3,2,1,0:T(8,128)(2,1)S(1)}, u32[]{:S(2)}, u32[]{:S(2)}) %collective-permute-start.4) | collective-permute-done | bytes 172064 | tf_op jit(solution)/shard_map/ppermute | solution.py:196
  27.5 1.6 %collective-permute-start.7 = (bf16[1,5,6,16,128]{4,3,2,1,0:T(8,128)(2,1)S(1)}, bf16[1,5,6,16,128]{4,3,2,1,0:T(8,128)(2,1)S(1)}, u32[]{:S(2)}, u32[]{:S(2)}) collective-permute-start(bf16[1,5,6,16,128]{4,3,2,1,0:T(8,128)(2,1)S(1)} %dynamic-slice_bitcast_fusion.1), channel_id=1, source_target_pairs={{0,2},{1,3},{2,0},{3,1},{4,6},{5,7},{6,4},{7,5},{8,10},{9,11},{10,... | collective-permute-start | bytes 368648 | tf_op jit(solution)/shard_map/ppermute | solution.py:196
  29.2 0.6 %collective-permute-done.11 = bf16[4,14,16,128]{3,2,1,0:T(8,128)(2,1)S(1)} collective-permute-done((bf16[4,14,16,128]{3,2,1,0:T(8,128)(2,1)S(1)}, bf16[4,14,16,128]{3,2,1,0:T(8,128)(2,1)S(1)}, u32[]{:S(2)}, u32[]{:S(2)}) %collective-permute-start.11) | collective-permute-done | bytes 229408 | tf_op jit(solution)/shard_map/ppermute | solution.py:199
  29.8 0.3 shard_map.47.refs_7_
  30.1 2.5 %collective-permute-done.7.refs_5_ = bf16[1,5,6,16,128]{4,3,2,1,0:T(8,128)(2,1)S(1)} collective-permute-done((bf16[1,5,6,16,128]{4,3,2,1,0:T(8,128)(2,1)S(1)}, bf16[1,5,6,16,128]{4,3,2,1,0:T(8,128)(2,1)S(1)}, u32[]{:S(2)}, u32[]{:S(2)}) %collective-permute-start.7) | collective-permute-done | bytes 122912 | tf_op jit(solution)/shard_map/ppermute | solution.py:196
  32.6 2.3 %shard_map.48.refs_8_ = f32[2,6,128,128]{3,2,1,0:T(8,128)S(1)} custom-call(s32[10]{0:T(128)S(1)} %stack.87.scalars, bf16[16,6,16,128]{3,2,1,0:T(8,128)(2,1)S(1)} %bitcast.30, bf16[7,6,16,128]{3,2,1,0:T(8,128)(2,1)S(1)} %collective-permute-done.refs_1_, bf16[7,6,16,128]{3,2,1,0:T(8,128)(2,1)S(1)} %collective-permute-done.4.refs_2_, ...), custom_call_target="tpu_custom_call" | custom-call | flops 1000000000 | bytes 4000000 | tf_op jit(solution)/shard_map/pallas_call | solution.py:122
  35.0 1.6 %shard_map.49.keep_ref = f32[2,6,128,128]{3,2,1,0:T(8,128)S(1)} custom-call(s32[10]{0:T(128)S(1)} %stack.87.scalars, bf16[16,6,16,128]{3,2,1,0:T(8,128)(2,1)S(1)} %bitcast.31, bf16[7,6,16,128]{3,2,1,0:T(8,128)(2,1)S(1)} %collective-permute-done.refs_1_, bf16[7,6,16,128]{3,2,1,0:T(8,128)(2,1)S(1)} %collective-permute-done.4.refs_2_, ...), custom_call_target="tpu_custom_call" | custom-call | flops 1000000000 | bytes 4000000 | tf_op jit(solution)/shard_map/pallas_call | solution.py:122
  36.6 0.7 %collective-permute-done.12.came_ref = f32[2,6,128,128]{3,2,1,0:T(8,128)S(1)} collective-permute-done((f32[2,6,128,128]{3,2,1,0:T(8,128)S(1)}, f32[2,6,128,128]{3,2,1,0:T(8,128)S(1)}, u32[]{:S(2)}, u32[]{:S(2)}) %collective-permute-start.12) | collective-permute-done | bytes 786464 | tf_op jit(solution)/shard_map/ppermute | solution.py:196
  37.3 2.0 %shard_map.50 = bf16[2,12,64,256]{3,2,1,0:T(8,128)(2,1)} custom-call(s32[1]{0:T(128)} %bitcast.scalars, f32[2,6,128,128]{3,2,1,0:T(8,128)S(1)} %shard_map.49.keep_ref, f32[2,6,128,128]{3,2,1,0:T(8,128)S(1)} %collective-permute-done.12.came_ref, bf16[27,64,128]{2,1,0:T(8,128)(2,1)S(1)} %copy-done.3), custom_call_target="tpu_custom_call" | custom-call | flops 1000000000 | bytes 3000000 | tf_op jit(solution)/shard_map/pallas_call | solution.py:176
  (28 shorter events, 0.5 us)
Async XLA Ops:
  0.0 0.9 %copy-start = (bf16[16,27,128]{2,0,1:T(8,128)(2,1)S(1)}, bf16[16,27,128]{2,0,1:T(8,128)(2,1)}, u32[]{:S(2)}) copy-start(bf16[16,27,128]{2,0,1:T(8,128)(2,1)} %param.5) | copy-start | bytes 331780
  1.0 1.0 %copy-start.1 = (bf16[16,16,6,128]{3,1,2,0:T(8,128)(2,1)S(1)}, bf16[16,16,6,128]{3,1,2,0:T(8,128)(2,1)}, u32[]{:S(2)}) copy-start(bf16[16,16,6,128]{3,1,2,0:T(8,128)(2,1)} %param.4) | copy-start | bytes 1179652
  2.0 0.7 %copy-start.4 = (f32[128]{0:T(128)S(1)}, f32[128]{0:T(128)}, u32[]{:S(2)}) copy-start(f32[128]{0:T(128)} %param.6) | copy-start | bytes 1540
  2.7 9.6 %collective-permute-start.3 = (bf16[14,16,128]{2,1,0:T(8,128)(2,1)S(1)}, bf16[14,16,128]{2,1,0:T(8,128)(2,1)S(1)}, u32[]{:S(2)}, u32[]{:S(2)}) collective-permute-start(bf16[14,16,128]{2,1,0:T(8,128)(2,1)S(1)} %dynamic-slice_bitcast_fusion.3), channel_id=1, source_target_pairs={{0,12},{1,13},{2,14},{3,15},{4,8},{5,9},{6,10},{7,11},{8,4},{9,5},... | collective-permute-start | bytes 172040 | tf_op jit(solution)/shard_map/ppermute | solution.py:196
  7.8 8.0 %collective-permute-start.2 = (bf16[14,16,128]{2,1,0:T(8,128)(2,1)S(1)}, bf16[14,16,128]{2,1,0:T(8,128)(2,1)S(1)}, u32[]{:S(2)}, u32[]{:S(2)}) collective-permute-start(bf16[14,16,128]{2,1,0:T(8,128)(2,1)S(1)} %dynamic-slice_bitcast_fusion.3), channel_id=1, source_target_pairs={{0,8},{1,9},{2,10},{3,11},{4,12},{5,13},{6,14},{7,15},{8,0},{9,1},... | collective-permute-start | bytes 172040 | tf_op jit(solution)/shard_map/ppermute | solution.py:196
  7.8 8.0 %collective-permute-start.1 = (bf16[14,16,128]{2,1,0:T(8,128)(2,1)S(1)}, bf16[14,16,128]{2,1,0:T(8,128)(2,1)S(1)}, u32[]{:S(2)}, u32[]{:S(2)}) collective-permute-start(bf16[14,16,128]{2,1,0:T(8,128)(2,1)S(1)} %dynamic-slice_bitcast_fusion.3), channel_id=1, source_target_pairs={{0,4},{1,5},{2,6},{3,7},{4,0},{5,1},{6,2},{7,3},{8,12},{9,13},{10,... | collective-permute-start | bytes 172040 | tf_op jit(solution)/shard_map/ppermute | solution.py:196
  8.4 10.4 %collective-permute-start.5 = (bf16[7,6,16,128]{3,2,1,0:T(8,128)(2,1)S(1)}, bf16[7,6,16,128]{3,2,1,0:T(8,128)(2,1)S(1)}, u32[]{:S(2)}, u32[]{:S(2)}) collective-permute-start(bf16[7,6,16,128]{3,2,1,0:T(8,128)(2,1)S(1)} %get-tuple-element.22), channel_id=1, source_target_pairs={{0,12},{1,13},{2,14},{3,15},{4,8},{5,9},{6,10},{7,11},{8,4},{9,5},... | collective-permute-start | bytes 516104 | tf_op jit(solution)/shard_map/ppermute | solution.py:196
  12.2 8.6 %collective-permute-start = (bf16[7,6,16,128]{3,2,1,0:T(8,128)(2,1)S(1)}, bf16[7,6,16,128]{3,2,1,0:T(8,128)(2,1)S(1)}, u32[]{:S(2)}, u32[]{:S(2)}) collective-permute-start(bf16[7,6,16,128]{3,2,1,0:T(8,128)(2,1)S(1)} %get-tuple-element.18), channel_id=1, source_target_pairs={{0,4},{1,5},{2,6},{3,7},{4,0},{5,1},{6,2},{7,3},{8,12},{9,13},{10,... | collective-permute-start | bytes 516104 | tf_op jit(solution)/shard_map/ppermute | solution.py:196
  15.8 13.3 %collective-permute-start.9 = (bf16[4,14,16,128]{3,2,1,0:T(8,128)(2,1)S(1)}, bf16[4,14,16,128]{3,2,1,0:T(8,128)(2,1)S(1)}, u32[]{:S(2)}, u32[]{:S(2)}) collective-permute-start(bf16[4,14,16,128]{3,2,1,0:T(8,128)(2,1)S(1)} %get-tuple-element.26), channel_id=1, source_target_pairs={{0,16},{16,0},{1,17},{17,1},{2,18},{18,2},{3,19},{19,3},{4,20},{20... | collective-permute-start | bytes 688136 | tf_op jit(solution)/shard_map/ppermute | solution.py:199
  17.4 6.4 %collective-permute-start.10 = (bf16[4,14,16,128]{3,2,1,0:T(8,128)(2,1)S(1)}, bf16[4,14,16,128]{3,2,1,0:T(8,128)(2,1)S(1)}, u32[]{:S(2)}, u32[]{:S(2)}) collective-permute-start(bf16[4,14,16,128]{3,2,1,0:T(8,128)(2,1)S(1)} %get-tuple-element.26), channel_id=1, source_target_pairs={{0,2},{1,3},{2,0},{3,1},{4,6},{5,7},{6,4},{7,5},{8,10},{9,11},{10,... | collective-permute-start | bytes 688136 | tf_op jit(solution)/shard_map/ppermute | solution.py:196
  18.9 8.7 %collective-permute-start.4 = (bf16[7,6,16,128]{3,2,1,0:T(8,128)(2,1)S(1)}, bf16[7,6,16,128]{3,2,1,0:T(8,128)(2,1)S(1)}, u32[]{:S(2)}, u32[]{:S(2)}) collective-permute-start(bf16[7,6,16,128]{3,2,1,0:T(8,128)(2,1)S(1)} %get-tuple-element.21), channel_id=1, source_target_pairs={{0,8},{1,9},{2,10},{3,11},{4,12},{5,13},{6,14},{7,15},{8,0},{9,1},... | collective-permute-start | bytes 516104 | tf_op jit(solution)/shard_map/ppermute | solution.py:196
  18.9 11.2 %collective-permute-start.8 = (bf16[1,5,6,16,128]{4,3,2,1,0:T(8,128)(2,1)S(1)}, bf16[1,5,6,16,128]{4,3,2,1,0:T(8,128)(2,1)S(1)}, u32[]{:S(2)}, u32[]{:S(2)}) collective-permute-start(bf16[1,5,6,16,128]{4,3,2,1,0:T(8,128)(2,1)S(1)} %dynamic-slice_bitcast_fusion), channel_id=1, source_target_pairs={{0,2},{1,3},{2,0},{3,1},{4,6},{5,7},{6,4},{7,5},{8,10},{9,11},{10,... | collective-permute-start | bytes 368648 | tf_op jit(solution)/shard_map/ppermute | solution.py:196
  20.8 11.8 %collective-permute-start.6 = (bf16[2,5,6,16,128]{4,3,2,1,0:T(8,128)(2,1)S(1)}, bf16[2,5,6,16,128]{4,3,2,1,0:T(8,128)(2,1)S(1)}, u32[]{:S(2)}, u32[]{:S(2)}) collective-permute-start(bf16[2,5,6,16,128]{4,3,2,1,0:T(8,128)(2,1)S(1)} %pad_maximum_fusion.2), channel_id=1, source_target_pairs={{0,2},{1,3},{2,0},{3,1},{4,6},{5,7},{6,4},{7,5},{8,10},{9,11},{10,... | collective-permute-start | bytes 737288 | tf_op jit(solution)/shard_map/ppermute | solution.py:196
  23.8 6.0 %collective-permute-start.11 = (bf16[4,14,16,128]{3,2,1,0:T(8,128)(2,1)S(1)}, bf16[4,14,16,128]{3,2,1,0:T(8,128)(2,1)S(1)}, u32[]{:S(2)}, u32[]{:S(2)}) collective-permute-start(bf16[4,14,16,128]{3,2,1,0:T(8,128)(2,1)S(1)} %collective-permute-done.10), channel_id=1, source_target_pairs={{0,16},{16,0},{1,17},{17,1},{2,18},{18,2},{3,19},{19,3},{4,20},{20... | collective-permute-start | bytes 688136 | tf_op jit(solution)/shard_map/ppermute | solution.py:199
  27.5 5.1 %collective-permute-start.7 = (bf16[1,5,6,16,128]{4,3,2,1,0:T(8,128)(2,1)S(1)}, bf16[1,5,6,16,128]{4,3,2,1,0:T(8,128)(2,1)S(1)}, u32[]{:S(2)}, u32[]{:S(2)}) collective-permute-start(bf16[1,5,6,16,128]{4,3,2,1,0:T(8,128)(2,1)S(1)} %dynamic-slice_bitcast_fusion.1), channel_id=1, source_target_pairs={{0,2},{1,3},{2,0},{3,1},{4,6},{5,7},{6,4},{7,5},{8,10},{9,11},{10,... | collective-permute-start | bytes 368648 | tf_op jit(solution)/shard_map/ppermute | solution.py:196
  29.8 2.8 %copy-start.2 = (bf16[16,16,6,128]{3,1,2,0:T(8,128)(2,1)S(1)}, bf16[16,16,6,128]{3,1,2,0:T(8,128)(2,1)}, u32[]{:S(2)}) copy-start(bf16[16,16,6,128]{3,1,2,0:T(8,128)(2,1)} %param.4) | copy-start | bytes 1179652
  34.9 2.4 %copy-start.3 = (bf16[27,64,128]{2,1,0:T(8,128)(2,1)S(1)}, bf16[27,64,128]{2,1,0:T(8,128)(2,1)}, u32[]{:S(2)}) copy-start(bf16[27,64,128]{2,1,0:T(8,128)(2,1)} %up_ref.1) | copy-start | bytes 1327108
  34.9 2.4 %collective-permute-start.12 = (f32[2,6,128,128]{3,2,1,0:T(8,128)S(1)}, f32[2,6,128,128]{3,2,1,0:T(8,128)S(1)}, u32[]{:S(2)}, u32[]{:S(2)}) collective-permute-start(f32[2,6,128,128]{3,2,1,0:T(8,128)S(1)} %shard_map.48.refs_8_), channel_id=1, source_target_pairs={{0,1},{1,0},{2,3},{3,2},{4,5},{5,4},{6,7},{7,6},{8,9},{9,8},{10,11... | collective-permute-start | bytes 2359304 | tf_op jit(solution)/shard_map/ppermute | solution.py:196

commit v4 on v3

v4 whole, which is shorter than its diff:
```python
import functools

import jax
import jax.numpy as jnp
from jax import lax
from jax.experimental import pallas as pl
from jax.experimental.pallas import tpu as pltpu
from jax.sharding import PartitionSpec as P

TILE = 4
VMEM = pl.BlockSpec(memory_space=pltpu.VMEM)
PARAMS = pltpu.CompilerParams(vmem_limit_bytes=16 * 2**20)


def window(first, count, total):
    return jnp.clip(first, 0, total - count)


def chip_first():
    return lax.axis_index("gx") // 2 * 2


def tile_start(total, mask=0):
    return window(TILE * (lax.axis_index("gx") // TILE ^ mask) - 1, min(7, total), total)


def chip_start(total, mask=0):
    return window((chip_first() ^ mask) - 1, 5, total)


def after(value, *earlier):
    return lax.optimization_barrier((value, *earlier))[0]


def cut_body(starts, counts, vol_ref, *outs):
    for out_ref, start, count in zip(outs, starts(), counts):
        out_ref[...] = vol_ref[pl.ds(start, count)]


def cuts(vol, starts, counts):
    return pl.pallas_call(
        functools.partial(cut_body, starts, counts),
        out_shape=[jax.ShapeDtypeStruct((count, *vol.shape[1:]), vol.dtype) for count in counts],
        in_specs=[VMEM],
        out_specs=[VMEM] * len(counts),
        compiler_params=PARAMS,
    )(vol)


def taps_body(near_order, far_order, span, *refs):
    weights, out_ref = refs[:-1], refs[-1]
    group = lax.axis_index("groups")
    cout = out_ref.shape[0] // 3
    for tap_z in range(3):
        pieces = []
        for tap in range(tap_z, 27, 3):
            part = tap // span
            start = min(part * span, 27 - span)
            for weight, order in zip(weights, (near_order, far_order)):
                pieces += [weight[group ^ part, place, tap - start] for place in order]
        out_ref[tap_z * cout : (tap_z + 1) * cout] = jnp.concatenate(pieces, axis=0).T


def taps_of(near_order, far_order, span, weights):
    cout, chans = weights[0].shape[-1], weights[0].shape[-2]
    columns = 9 * chans * (len(near_order) + len(far_order))
    return pl.pallas_call(
        functools.partial(taps_body, near_order, far_order, span),
        out_shape=jax.ShapeDtypeStruct((3 * cout, columns), jnp.bfloat16),
        in_specs=[VMEM] * len(weights),
        out_specs=VMEM,
        compiler_params=PARAMS,
        cost_estimate=pl.CostEstimate(flops=0, bytes_accessed=3 * 10**6, transcendentals=0),
    )(*weights)


def conv_planes(total, kinds, refs, taps, first, stores):
    steps = len(kinds)
    parts = [*refs[:steps], *(ref.at[at] for ref in refs[steps:] for at in range(ref.shape[0]))]
    _, wide_y, chans, wide_z = parts[0].shape
    cout = taps.shape[0] // 3
    lane = lax.broadcasted_iota(jnp.int32, (cout, wide_z), 1)
    zeros = jnp.zeros((len(parts) * chans, wide_z), taps.dtype)
    by_kind = {"all": 0, "tile": tile_start(total), "chip": chip_start(total)}
    starts = [by_kind[kind] for kind in kinds] + [by_kind["chip"]] * steps
    rows = {(slot, y): zeros for slot in range(len(stores) + 2) for y in (-1, wide_y)}
    for slot in range(len(stores) + 2):
        at = first - 1 + slot
        inside = jnp.logical_and(at >= 0, at < total)
        index = [jnp.clip(at - starts[place], 0, ref.shape[0] - 1) for place, ref in enumerate(parts)]
        for y in range(wide_y):
            held = jnp.concatenate([ref[index[place], y] for place, ref in enumerate(parts)], axis=0)
            rows[slot, y] = jnp.where(inside, held, zeros)
    for plane, store in enumerate(stores):
        for pair in range(0, wide_y, 2):
            blocks = []
            for tap_x in range(3):
                for y in range(pair - 1, pair + 2):
                    blocks.append(jnp.concatenate([rows[plane + tap_x, y], rows[plane + tap_x, y + 1]], axis=1))
            acc = jnp.dot(taps[...], jnp.concatenate(blocks, axis=0), preferred_element_type=jnp.float32)
            for side in range(2):
                part = acc[:, side * wide_z : (side + 1) * wide_z]
                low = jnp.where(lane == 0, 0.0, pltpu.roll(part[:cout], 1, 1))
                high = jnp.where(lane == wide_z - 1, 0.0, pltpu.roll(part[2 * cout :], wide_z - 1, 1))
                store(pair + side, part[cout : 2 * cout] + low + high)


def send_body(total, kinds, *refs):
    *parts, taps, out_ref = refs
    core = lax.axis_index("gx") % 2

    def lower(y, value):
        out_ref[core, y] = value

    def upper(y, value):
        out_ref[1 - core, y] = value

    conv_planes(total, kinds, parts, taps, chip_first() + 1 - core, (lower, upper))


def keep_body(total, kinds, *refs):
    *parts, taps, shared_ref, bias_ref, out_ref = refs
    core = lax.axis_index("gx") % 2
    bias = bias_ref[...]
    plane = chip_first() + 2 * core
    inside = plane < total

    def store(y, value):
        out_ref[core, y] = jnp.where(inside, value + bias, -jnp.inf)
        out_ref[1 - core, y] = shared_ref[0, y] + bias

    conv_planes(total, kinds, parts, taps, plane, (store,))


def conv_call(body, total, kinds, parts, taps, *more):
    _, wide_y, _, wide_z = parts[0].shape
    cout = taps.shape[0] // 3
    return pl.pallas_call(
        functools.partial(body, total, kinds),
        out_shape=jax.ShapeDtypeStruct((2, wide_y, cout, wide_z), jnp.float32),
        in_specs=[VMEM] * (len(parts) + 1 + len(more)),
        out_specs=VMEM,
        compiler_params=PARAMS,
        cost_estimate=pl.CostEstimate(flops=10**9, bytes_accessed=4 * 10**6, transcendentals=0),
    )(*parts, taps, *more)


def up_body(keep_ref, came_ref, up_ref, out_ref):
    core = lax.axis_index("gx") % 2
    _, wide_y, cout, wide_z = keep_ref.shape
    cup = up_ref.shape[1]
    hidden = []
    for ahead in range(2):
        at = jnp.where(core == ahead, 1, 0)
        rows = [jnp.maximum(keep_ref[ahead, y] + came_ref[at, y], 0.0).astype(jnp.bfloat16) for y in range(wide_y)]
        hidden.append(jnp.concatenate(rows, axis=1))
    shape = (2 * wide_z, 2 * wide_z)
    source, target = (lax.broadcasted_iota(jnp.int32, shape, axis) for axis in range(2))
    weave = (target == 2 * (source % wide_z) + source // wide_z).astype(jnp.bfloat16)
    edge = lax.broadcasted_iota(jnp.int32, (cup, wide_z), 1) == wide_z - 1

    def later(value):
        return jnp.where(edge, 0.0, pltpu.roll(value, wide_z - 1, 1))

    for odd in range(2):
        if odd:
            left = jnp.concatenate([up_ref[18:27].reshape(9 * cup, cout), up_ref[0:9].reshape(9 * cup, cout)], axis=1)
            right = jnp.concatenate(hidden, axis=0)
        else:
            left = up_ref[9:18].reshape(9 * cup, cout)
            right = hidden[0]
        product = jnp.dot(left, right, preferred_element_type=jnp.float32)

        def term(tap_y, tap_z, y):
            at = (3 * tap_y + tap_z) * cup
            return product[at : at + cup, y * wide_z : (y + 1) * wide_z]

        lines = []
        for y in range(wide_y):
            for par_y in range(2):
                choices = [(1, y)] if par_y == 0 else [(2, y)] + ([(0, y + 1)] if y + 1 < wide_y else [])
                even = sum(term(tap_y, 1, at) for tap_y, at in choices)
                plain = sum(term(tap_y, 2, at) for tap_y, at in choices)
                moved = sum(term(tap_y, 0, at) for tap_y, at in choices)
                lines.append(jnp.concatenate([even, plain + later(moved)], axis=1).astype(jnp.bfloat16))
        woven = jnp.dot(jnp.concatenate(lines, axis=0), weave, preferred_element_type=jnp.float32)
        out_ref[odd] = woven.astype(jnp.bfloat16).reshape(2 * wide_y, cup, 2 * wide_z)


def upsample(keep, came, up):
    _, wide_y, _, wide_z = keep.shape
    return pl.pallas_call(
        up_body,
        out_shape=jax.ShapeDtypeStruct((2, 2 * wide_y, up.shape[1], 2 * wide_z), jnp.bfloat16),
        in_specs=[VMEM] * 3,
        out_specs=VMEM,
        compiler_params=PARAMS,
        cost_estimate=pl.CostEstimate(flops=10**9, bytes_accessed=3 * 10**6, transcendentals=0),
    )(keep, came, up)


def per_device(volume, conv_weight, conv_bias, tconv_weight):
    total, size, groups = volume.shape[0], lax.axis_size("gx"), lax.axis_size("groups")
    tiles = size // TILE
    assert total == size and size % TILE == 0 and tiles & (tiles - 1) == 0 and groups & (groups - 1) == 0
    group = lax.axis_index("groups")
    vol = jnp.transpose(volume, (0, 2, 1, 3))
    weight = jnp.transpose(conv_weight, (1, 0, 2))

    def swap(block, mask):
        return lax.ppermute(block, "gx", [(i, i ^ mask) for i in range(size)])

    def cross(block, mask):
        return lax.ppermute(block, "groups", [(i, i ^ mask) for i in range(groups)])

    wide = min(7, total)
    steps = range(tiles)

    straight = {step for step in steps if step % 4 == 2}
    counts = [5] + [count for step in steps[1:] for count in ([5, 5] if step in straight else [wide])]

    def starts():
        found = [chip_start(total, 2)]
        for step in steps[1:]:
            mask = TILE * step
            found += [chip_start(total, mask), chip_start(total, mask ^ 2)] if step in straight else [tile_start(total, step)]
        return found

    pieces = cuts(vol, starts, counts)
    span = -(-27 // groups)
    held = lax.dynamic_slice_in_dim(weight, jnp.minimum(group * span, 27 - span), span, 0)
    held, *pieces = lax.optimization_barrier((held, *pieces))
    far_own, *pieces = pieces
    held = jnp.stack([held] + [swap(held, TILE * step) for step in steps[1:]], axis=0)
    near, far, far_order = {0: vol}, [], []
    for step in steps[1:]:
        if step in straight:
            near[step] = swap(after(pieces.pop(0), held), TILE * step)
            far.append(swap(after(pieces.pop(0), held), TILE * step ^ 2)[None])
            far_order.append([step])
        else:
            near[step] = swap(pieces.pop(0), TILE * step)
    far_held = swap(held, 2)
    columns = [jnp.stack([part] + [cross(part, mask) for mask in range(1, groups)], axis=0) for part in (held, far_held)]
    partner = chip_start(total, 2) - tile_start(total)
    for chosen in ([0, *steps[1::4]], [*steps[3::4]]):
        cut = [lax.dynamic_slice_in_dim(near[step], partner, 5, 0) if step else far_own for step in chosen]
        far.append(swap(jnp.stack(cut, axis=0), 2))
        far_order.append(chosen)
    kinds = tuple("all" if step == 0 else "chip" if step in straight else "tile" for step in steps)
    near = [near[step] for step in steps]
    bias = jnp.broadcast_to(conv_bias[:, None], (weight.shape[2], vol.shape[3]))
    far[-2], bias = lax.optimization_barrier((far[-2], bias))
    taps = taps_of(tuple(steps), tuple(step for chosen in far_order for step in chosen), span, columns)
    parts = near + far
    shared = conv_call(send_body, total, kinds, parts, taps)
    came = swap(shared, 1)
    keep = conv_call(keep_body, total, kinds, parts, taps, shared, bias)
    out = upsample(keep, came, tconv_weight)
    return jnp.transpose(out, (0, 2, 1, 3))


def solution(mesh):
    return jax.shard_map(
        per_device,
        mesh=mesh,
        in_specs=(P("groups", "gx", None, None), P("gx", None, None), P(), P()),
        out_specs=P(("groups", "gx"), None, None, None),
        check_vma=False,
    )
```

time: 39.5 us -> 36.8 us (0.932)
  Pallas kernels: 6.78 us -> 5.17 us
  starting transfers between devices: 17.4 us -> 18.8 us
  waiting for transfers between devices: 12.7 us -> 11.3 us
  local copies, waits for them, and re-layouts: 2.16 us -> 1.15 us
    ppermute x11, waiting for transfers between devices: 12.1 us -> 9.31 us  [swap(): return lax.ppermute(block, 'gx', [(i, i ^ mask) for i in range(size)])]
    pallas_call x3, Pallas kernels: 4.47 us -> 2.87 us  [the longest x2 2.82 us: conv_call(): pl.pallas_call(functools.partial(body, total, kinds), out_shape=jax.Shape...]
    ppermute x11, starting transfers between devices: 15.6 us -> 17.2 us  [swap(): return lax.ppermute(block, 'gx', [(i, i ^ mask) for i in range(size)])]
    ppermute x2, waiting for transfers between devices: 0.6 us -> 2 us  [cross(): return lax.ppermute(block, 'groups', [(i, i ^ mask) for i in range(groups)])]
    unnamed x10, local copies, waits for them, and re-layouts: 1.97 us -> 1.05 us
  transfers between devices with their start and end apart: 13 -> 13, of which waited for: 7 -> 8; matrix products, arithmetic and copies ran while one was open for 1% -> 1% of each run, Pallas kernels for 5% -> 4%
where the time goes in v4:
time: 36.8 us; the launch traced here: 36.7 us
  starting transfers between devices  18.8 us (51%)
  waiting for transfers between devices  11.3 us (31%)
  Pallas kernels  5.17 us (14%)
  local copies, waits for them, and re-layouts  1.15 us (3%)
    ppermute x11, starting transfers between devices, swap(): return lax.ppermute(block, 'gx', [(i, i ^ mask) for i in range(size)])  17.2 us
    ppermute x11, waiting for transfers between devices, swap(): return lax.ppermute(block, 'gx', [(i, i ^ mask) for i in range(size)])  9.31 us
    pallas_call x2, Pallas kernels, conv_call(): pl.pallas_call(functools.partial(body, total, kinds), out_shape=jax.Shape...  2.82 us
    pallas_call x1, Pallas kernels, upsample(): pl.pallas_call(up_body, out_shape=jax.ShapeDtypeStruct((2, 2 * wide_y, up...  2 us
    ppermute x2, waiting for transfers between devices, cross(): return lax.ppermute(block, 'groups', [(i, i ^ mask) for i in range(groups)])  2 us
    ppermute x2, starting transfers between devices, cross(): return lax.ppermute(block, 'groups', [(i, i ^ mask) for i in range(groups)])  1.6 us
    unnamed x10, local copies, waits for them, and re-layouts  1.05 us
  transfers between devices with their start and end apart: 13, of which 8 were waited for; matrix products, arithmetic and copies ran while one was open for 1% of the time, Pallas kernels for 4%

profile of v4, /device:TPU:0, one launch (start us, length us, event | category | flops | bytes accessed | tf_op | source)
XLA Modules:
  0.0 36.7 jit_solution(8852279612241066803)
XLA Ops:
  0.0 1.0 %copy-done.1 = bf16[16,16,6,128]{3,1,2,0:T(8,128)(2,1)S(1)} copy-done((bf16[16,16,6,128]{3,1,2,0:T(8,128)(2,1)S(1)}, bf16[16,16,6,128]{3,1,2,0:T(8,128)(2,1)}, u32[]{:S(2)}) %copy-start.1) | copy-done | bytes 393240
  1.1 5.1 %collective-permute-start.3 = (bf16[14,16,128]{2,1,0:T(8,128)(2,1)S(1)}, bf16[14,16,128]{2,1,0:T(8,128)(2,1)S(1)}, u32[]{:S(2)}, u32[]{:S(2)}) collective-permute-start(bf16[14,16,128]{2,1,0:T(8,128)(2,1)S(1)} %dynamic-slice_bitcast_fusion.2), channel_id=1, source_target_pairs={{0,12},{1,13},{2,14},{3,15},{4,8},{5,9},{6,10},{7,11},{8,4},{9,5},... | collective-permute-start | bytes 172040 | tf_op jit(solution)/shard_map/ppermute | solution.py:211
  6.2 0.6 %collective-permute-start.1 = (bf16[14,16,128]{2,1,0:T(8,128)(2,1)S(1)}, bf16[14,16,128]{2,1,0:T(8,128)(2,1)S(1)}, u32[]{:S(2)}, u32[]{:S(2)}) collective-permute-start(bf16[14,16,128]{2,1,0:T(8,128)(2,1)S(1)} %dynamic-slice_bitcast_fusion.2), channel_id=1, source_target_pairs={{0,4},{1,5},{2,6},{3,7},{4,0},{5,1},{6,2},{7,3},{8,12},{9,13},{10,... | collective-permute-start | bytes 172040 | tf_op jit(solution)/shard_map/ppermute | solution.py:211
  6.9 1.4 %collective-permute-start = (bf16[7,6,16,128]{3,2,1,0:T(8,128)(2,1)S(1)}, bf16[7,6,16,128]{3,2,1,0:T(8,128)(2,1)S(1)}, u32[]{:S(2)}, u32[]{:S(2)}) collective-permute-start(bf16[7,6,16,128]{3,2,1,0:T(8,128)(2,1)S(1)} %get-tuple-element.25), channel_id=1, source_target_pairs={{0,4},{1,5},{2,6},{3,7},{4,0},{5,1},{6,2},{7,3},{8,12},{9,13},{10,... | collective-permute-start | bytes 516104 | tf_op jit(solution)/shard_map/ppermute | solution.py:211
  8.3 2.4 %collective-permute-start.5 = (bf16[7,6,16,128]{3,2,1,0:T(8,128)(2,1)S(1)}, bf16[7,6,16,128]{3,2,1,0:T(8,128)(2,1)S(1)}, u32[]{:S(2)}, u32[]{:S(2)}) collective-permute-start(bf16[7,6,16,128]{3,2,1,0:T(8,128)(2,1)S(1)} %get-tuple-element.29), channel_id=1, source_target_pairs={{0,12},{1,13},{2,14},{3,15},{4,8},{5,9},{6,10},{7,11},{8,4},{9,5},... | collective-permute-start | bytes 516104 | tf_op jit(solution)/shard_map/ppermute | solution.py:211
  10.7 1.2 %collective-permute-done.2 = bf16[14,16,128]{2,1,0:T(8,128)(2,1)S(1)} collective-permute-done((bf16[14,16,128]{2,1,0:T(8,128)(2,1)S(1)}, bf16[14,16,128]{2,1,0:T(8,128)(2,1)S(1)}, u32[]{:S(2)}, u32[]{:S(2)}) %collective-permute-start.2) | collective-permute-done | bytes 57376 | tf_op jit(solution)/shard_map/ppermute | solution.py:211
  11.9 0.1 collective-permute-done.1
  12.0 1.6 %collective-permute-start.9 = (bf16[4,14,16,128]{3,2,1,0:T(8,128)(2,1)S(1)}, bf16[4,14,16,128]{3,2,1,0:T(8,128)(2,1)S(1)}, u32[]{:S(2)}, u32[]{:S(2)}) collective-permute-start(bf16[4,14,16,128]{3,2,1,0:T(8,128)(2,1)S(1)} %get-tuple-element.36), channel_id=1, source_target_pairs={{0,16},{16,0},{1,17},{17,1},{2,18},{18,2},{3,19},{19,3},{4,20},{20... | collective-permute-start | bytes 688136 | tf_op jit(solution)/shard_map/ppermute | solution.py:214
  13.6 1.5 %collective-permute-start.10 = (bf16[4,14,16,128]{3,2,1,0:T(8,128)(2,1)S(1)}, bf16[4,14,16,128]{3,2,1,0:T(8,128)(2,1)S(1)}, u32[]{:S(2)}, u32[]{:S(2)}) collective-permute-start(bf16[4,14,16,128]{3,2,1,0:T(8,128)(2,1)S(1)} %get-tuple-element.36), channel_id=1, source_target_pairs={{0,2},{1,3},{2,0},{3,1},{4,6},{5,7},{6,4},{7,5},{8,10},{9,11},{10,... | collective-permute-start | bytes 688136 | tf_op jit(solution)/shard_map/ppermute | solution.py:211
  15.1 0.6 %collective-permute-done.refs_1_ = bf16[7,6,16,128]{3,2,1,0:T(8,128)(2,1)S(1)} collective-permute-done((bf16[7,6,16,128]{3,2,1,0:T(8,128)(2,1)S(1)}, bf16[7,6,16,128]{3,2,1,0:T(8,128)(2,1)S(1)}, u32[]{:S(2)}, u32[]{:S(2)}) %collective-permute-start) | collective-permute-done | bytes 172064 | tf_op jit(solution)/shard_map/ppermute | solution.py:211
  15.7 1.9 %collective-permute-start.7 = (bf16[2,5,6,16,128]{4,3,2,1,0:T(8,128)(2,1)S(1)}, bf16[2,5,6,16,128]{4,3,2,1,0:T(8,128)(2,1)S(1)}, u32[]{:S(2)}, u32[]{:S(2)}) collective-permute-start(bf16[2,5,6,16,128]{4,3,2,1,0:T(8,128)(2,1)S(1)} %pad_maximum_fusion.2), channel_id=1, source_target_pairs={{0,2},{1,3},{2,0},{3,1},{4,6},{5,7},{6,4},{7,5},{8,10},{9,11},{10,... | collective-permute-start | bytes 737288 | tf_op jit(solution)/shard_map/ppermute | solution.py:211
  17.7 1.7 %collective-permute-start.4 = (bf16[5,6,16,128]{3,2,1,0:T(8,128)(2,1)S(1)}, bf16[5,6,16,128]{3,2,1,0:T(8,128)(2,1)S(1)}, u32[]{:S(2)}, u32[]{:S(2)}) collective-permute-start(bf16[5,6,16,128]{3,2,1,0:T(8,128)(2,1)S(1)} %get-tuple-element.28), channel_id=1, source_target_pairs={{0,8},{1,9},{2,10},{3,11},{4,12},{5,13},{6,14},{7,15},{8,0},{9,1},... | collective-permute-start | bytes 368648 | tf_op jit(solution)/shard_map/ppermute | solution.py:211
  19.3 0.8 %collective-permute-start.6 = (bf16[5,6,16,128]{3,2,1,0:T(8,128)(2,1)S(1)}, bf16[5,6,16,128]{3,2,1,0:T(8,128)(2,1)S(1)}, u32[]{:S(2)}, u32[]{:S(2)}) collective-permute-start(bf16[5,6,16,128]{3,2,1,0:T(8,128)(2,1)S(1)} %get-tuple-element.31), channel_id=1, source_target_pairs={{0,10},{1,11},{2,8},{3,9},{4,14},{5,15},{6,12},{7,13},{8,2},{9,3},... | collective-permute-start | bytes 368648 | tf_op jit(solution)/shard_map/ppermute | solution.py:211
  20.2 1.8 %collective-permute-done.10 = bf16[4,14,16,128]{3,2,1,0:T(8,128)(2,1)S(1)} collective-permute-done((bf16[4,14,16,128]{3,2,1,0:T(8,128)(2,1)S(1)}, bf16[4,14,16,128]{3,2,1,0:T(8,128)(2,1)S(1)}, u32[]{:S(2)}, u32[]{:S(2)}) %collective-permute-start.10) | collective-permute-done | bytes 229408 | tf_op jit(solution)/shard_map/ppermute | solution.py:211
  22.1 1.6 %collective-permute-start.8 = (bf16[1,5,6,16,128]{4,3,2,1,0:T(8,128)(2,1)S(1)}, bf16[1,5,6,16,128]{4,3,2,1,0:T(8,128)(2,1)S(1)}, u32[]{:S(2)}, u32[]{:S(2)}) collective-permute-start(bf16[1,5,6,16,128]{4,3,2,1,0:T(8,128)(2,1)S(1)} %dynamic-slice_bitcast_fusion), channel_id=1, source_target_pairs={{0,2},{1,3},{2,0},{3,1},{4,6},{5,7},{6,4},{7,5},{8,10},{9,11},{10,... | collective-permute-start | bytes 368648 | tf_op jit(solution)/shard_map/ppermute | solution.py:211
  23.7 2.2 %collective-permute-done.7.refs_5_ = bf16[2,5,6,16,128]{4,3,2,1,0:T(8,128)(2,1)S(1)} collective-permute-done((bf16[2,5,6,16,128]{4,3,2,1,0:T(8,128)(2,1)S(1)}, bf16[2,5,6,16,128]{4,3,2,1,0:T(8,128)(2,1)S(1)}, u32[]{:S(2)}, u32[]{:S(2)}) %collective-permute-start.7) | collective-permute-done | bytes 245792 | tf_op jit(solution)/shard_map/ppermute | solution.py:211
  26.0 0.1 broadcast_in_dim.10.refs_9_
  26.0 2.0 %collective-permute-done.11 = bf16[4,14,16,128]{3,2,1,0:T(8,128)(2,1)S(1)} collective-permute-done((bf16[4,14,16,128]{3,2,1,0:T(8,128)(2,1)S(1)}, bf16[4,14,16,128]{3,2,1,0:T(8,128)(2,1)S(1)}, u32[]{:S(2)}, u32[]{:S(2)}) %collective-permute-start.11) | collective-permute-done | bytes 229408 | tf_op jit(solution)/shard_map/ppermute | solution.py:214
  28.1 0.3 shard_map.47.refs_7_
  28.4 2.1 %collective-permute-done.6 = bf16[5,6,16,128]{3,2,1,0:T(8,128)(2,1)S(1)} collective-permute-done((bf16[5,6,16,128]{3,2,1,0:T(8,128)(2,1)S(1)}, bf16[5,6,16,128]{3,2,1,0:T(8,128)(2,1)S(1)}, u32[]{:S(2)}, u32[]{:S(2)}) %collective-permute-start.6) | collective-permute-done | bytes 122912 | tf_op jit(solution)/shard_map/ppermute | solution.py:211
  30.6 1.8 %shard_map.48.refs_8_ = f32[2,6,128,128]{3,2,1,0:T(8,128)S(1)} custom-call(bf16[16,6,16,128]{3,2,1,0:T(8,128)(2,1)S(1)} %bitcast.20, bf16[7,6,16,128]{3,2,1,0:T(8,128)(2,1)S(1)} %collective-permute-done.refs_1_, bf16[5,6,16,128]{3,2,1,0:T(8,128)(2,1)S(1)} %collective-permute-done.4.refs_2_, bf16[7,6,16,128]{3,2,1,0:T(8,128)(2,1)S(1)} %collective-permute-done.5.refs_3_, ...), custom_call_target="tpu_custom_call" | custom-call | flops 1000000000 | bytes 4000000 | tf_op jit(solution)/shard_map/pallas_call | solution.py:138
  32.4 1.1 %shard_map.49.keep_ref = f32[2,6,128,128]{3,2,1,0:T(8,128)S(1)} custom-call(bf16[16,6,16,128]{3,2,1,0:T(8,128)(2,1)S(1)} %bitcast.21, bf16[7,6,16,128]{3,2,1,0:T(8,128)(2,1)S(1)} %collective-permute-done.refs_1_, bf16[5,6,16,128]{3,2,1,0:T(8,128)(2,1)S(1)} %collective-permute-done.4.refs_2_, bf16[7,6,16,128]{3,2,1,0:T(8,128)(2,1)S(1)} %collective-permute-done.5.refs_3_, ...), custom_call_target="tpu_custom_call" | custom-call | flops 1000000000 | bytes 4000000 | tf_op jit(solution)/shard_map/pallas_call | solution.py:138
  33.5 1.2 %collective-permute-done.12.came_ref = f32[2,6,128,128]{3,2,1,0:T(8,128)S(1)} collective-permute-done((f32[2,6,128,128]{3,2,1,0:T(8,128)S(1)}, f32[2,6,128,128]{3,2,1,0:T(8,128)S(1)}, u32[]{:S(2)}, u32[]{:S(2)}) %collective-permute-start.12) | collective-permute-done | bytes 786464 | tf_op jit(solution)/shard_map/ppermute | solution.py:211
  34.7 2.0 %shard_map.50 = bf16[2,12,64,256]{3,2,1,0:T(8,128)(2,1)} custom-call(f32[2,6,128,128]{3,2,1,0:T(8,128)S(1)} %shard_map.49.keep_ref, f32[2,6,128,128]{3,2,1,0:T(8,128)S(1)} %collective-permute-done.12.came_ref, bf16[27,64,128]{2,1,0:T(8,128)(2,1)S(1)} %copy-done.3), custom_call_target="tpu_custom_call" | custom-call | flops 1000000000 | bytes 3000000 | tf_op jit(solution)/shard_map/pallas_call | solution.py:192
  (25 shorter events, 0.4 us)
Async XLA Ops:
  0.0 1.1 %copy-start = (bf16[16,27,128]{2,0,1:T(8,128)(2,1)S(1)}, bf16[16,27,128]{2,0,1:T(8,128)(2,1)}, u32[]{:S(2)}) copy-start(bf16[16,27,128]{2,0,1:T(8,128)(2,1)} %param.5) | copy-start | bytes 331780
  0.0 1.0 %copy-start.1 = (bf16[16,16,6,128]{3,1,2,0:T(8,128)(2,1)S(1)}, bf16[16,16,6,128]{3,1,2,0:T(8,128)(2,1)}, u32[]{:S(2)}) copy-start(bf16[16,16,6,128]{3,1,2,0:T(8,128)(2,1)} %param.4) | copy-start | bytes 1179652
  1.1 9.5 %collective-permute-start.3 = (bf16[14,16,128]{2,1,0:T(8,128)(2,1)S(1)}, bf16[14,16,128]{2,1,0:T(8,128)(2,1)S(1)}, u32[]{:S(2)}, u32[]{:S(2)}) collective-permute-start(bf16[14,16,128]{2,1,0:T(8,128)(2,1)S(1)} %dynamic-slice_bitcast_fusion.2), channel_id=1, source_target_pairs={{0,12},{1,13},{2,14},{3,15},{4,8},{5,9},{6,10},{7,11},{8,4},{9,5},... | collective-permute-start | bytes 172040 | tf_op jit(solution)/shard_map/ppermute | solution.py:211
  6.2 5.6 %collective-permute-start.2 = (bf16[14,16,128]{2,1,0:T(8,128)(2,1)S(1)}, bf16[14,16,128]{2,1,0:T(8,128)(2,1)S(1)}, u32[]{:S(2)}, u32[]{:S(2)}) collective-permute-start(bf16[14,16,128]{2,1,0:T(8,128)(2,1)S(1)} %dynamic-slice_bitcast_fusion.2), channel_id=1, source_target_pairs={{0,8},{1,9},{2,10},{3,11},{4,12},{5,13},{6,14},{7,15},{8,0},{9,1},... | collective-permute-start | bytes 172040 | tf_op jit(solution)/shard_map/ppermute | solution.py:211
  6.2 5.8 %collective-permute-start.1 = (bf16[14,16,128]{2,1,0:T(8,128)(2,1)S(1)}, bf16[14,16,128]{2,1,0:T(8,128)(2,1)S(1)}, u32[]{:S(2)}, u32[]{:S(2)}) collective-permute-start(bf16[14,16,128]{2,1,0:T(8,128)(2,1)S(1)} %dynamic-slice_bitcast_fusion.2), channel_id=1, source_target_pairs={{0,4},{1,5},{2,6},{3,7},{4,0},{5,1},{6,2},{7,3},{8,12},{9,13},{10,... | collective-permute-start | bytes 172040 | tf_op jit(solution)/shard_map/ppermute | solution.py:211
  6.9 8.8 %collective-permute-start = (bf16[7,6,16,128]{3,2,1,0:T(8,128)(2,1)S(1)}, bf16[7,6,16,128]{3,2,1,0:T(8,128)(2,1)S(1)}, u32[]{:S(2)}, u32[]{:S(2)}) collective-permute-start(bf16[7,6,16,128]{3,2,1,0:T(8,128)(2,1)S(1)} %get-tuple-element.25), channel_id=1, source_target_pairs={{0,4},{1,5},{2,6},{3,7},{4,0},{5,1},{6,2},{7,3},{8,12},{9,13},{10,... | collective-permute-start | bytes 516104 | tf_op jit(solution)/shard_map/ppermute | solution.py:211
  8.3 11.1 %collective-permute-start.5 = (bf16[7,6,16,128]{3,2,1,0:T(8,128)(2,1)S(1)}, bf16[7,6,16,128]{3,2,1,0:T(8,128)(2,1)S(1)}, u32[]{:S(2)}, u32[]{:S(2)}) collective-permute-start(bf16[7,6,16,128]{3,2,1,0:T(8,128)(2,1)S(1)} %get-tuple-element.29), channel_id=1, source_target_pairs={{0,12},{1,13},{2,14},{3,15},{4,8},{5,9},{6,10},{7,11},{8,4},{9,5},... | collective-permute-start | bytes 516104 | tf_op jit(solution)/shard_map/ppermute | solution.py:211
  12.0 10.0 %collective-permute-start.9 = (bf16[4,14,16,128]{3,2,1,0:T(8,128)(2,1)S(1)}, bf16[4,14,16,128]{3,2,1,0:T(8,128)(2,1)S(1)}, u32[]{:S(2)}, u32[]{:S(2)}) collective-permute-start(bf16[4,14,16,128]{3,2,1,0:T(8,128)(2,1)S(1)} %get-tuple-element.36), channel_id=1, source_target_pairs={{0,16},{16,0},{1,17},{17,1},{2,18},{18,2},{3,19},{19,3},{4,20},{20... | collective-permute-start | bytes 688136 | tf_op jit(solution)/shard_map/ppermute | solution.py:214
  13.6 8.4 %collective-permute-start.10 = (bf16[4,14,16,128]{3,2,1,0:T(8,128)(2,1)S(1)}, bf16[4,14,16,128]{3,2,1,0:T(8,128)(2,1)S(1)}, u32[]{:S(2)}, u32[]{:S(2)}) collective-permute-start(bf16[4,14,16,128]{3,2,1,0:T(8,128)(2,1)S(1)} %get-tuple-element.36), channel_id=1, source_target_pairs={{0,2},{1,3},{2,0},{3,1},{4,6},{5,7},{6,4},{7,5},{8,10},{9,11},{10,... | collective-permute-start | bytes 688136 | tf_op jit(solution)/shard_map/ppermute | solution.py:211
  15.7 10.2 %collective-permute-start.7 = (bf16[2,5,6,16,128]{4,3,2,1,0:T(8,128)(2,1)S(1)}, bf16[2,5,6,16,128]{4,3,2,1,0:T(8,128)(2,1)S(1)}, u32[]{:S(2)}, u32[]{:S(2)}) collective-permute-start(bf16[2,5,6,16,128]{4,3,2,1,0:T(8,128)(2,1)S(1)} %pad_maximum_fusion.2), channel_id=1, source_target_pairs={{0,2},{1,3},{2,0},{3,1},{4,6},{5,7},{6,4},{7,5},{8,10},{9,11},{10,... | collective-permute-start | bytes 737288 | tf_op jit(solution)/shard_map/ppermute | solution.py:211
  17.7 10.8 %collective-permute-start.4 = (bf16[5,6,16,128]{3,2,1,0:T(8,128)(2,1)S(1)}, bf16[5,6,16,128]{3,2,1,0:T(8,128)(2,1)S(1)}, u32[]{:S(2)}, u32[]{:S(2)}) collective-permute-start(bf16[5,6,16,128]{3,2,1,0:T(8,128)(2,1)S(1)} %get-tuple-element.28), channel_id=1, source_target_pairs={{0,8},{1,9},{2,10},{3,11},{4,12},{5,13},{6,14},{7,15},{8,0},{9,1},... | collective-permute-start | bytes 368648 | tf_op jit(solution)/shard_map/ppermute | solution.py:211
  19.3 11.2 %collective-permute-start.6 = (bf16[5,6,16,128]{3,2,1,0:T(8,128)(2,1)S(1)}, bf16[5,6,16,128]{3,2,1,0:T(8,128)(2,1)S(1)}, u32[]{:S(2)}, u32[]{:S(2)}) collective-permute-start(bf16[5,6,16,128]{3,2,1,0:T(8,128)(2,1)S(1)} %get-tuple-element.31), channel_id=1, source_target_pairs={{0,10},{1,11},{2,8},{3,9},{4,14},{5,15},{6,12},{7,13},{8,2},{9,3},... | collective-permute-start | bytes 368648 | tf_op jit(solution)/shard_map/ppermute | solution.py:211
  22.0 6.0 %collective-permute-start.11 = (bf16[4,14,16,128]{3,2,1,0:T(8,128)(2,1)S(1)}, bf16[4,14,16,128]{3,2,1,0:T(8,128)(2,1)S(1)}, u32[]{:S(2)}, u32[]{:S(2)}) collective-permute-start(bf16[4,14,16,128]{3,2,1,0:T(8,128)(2,1)S(1)} %collective-permute-done.10), channel_id=1, source_target_pairs={{0,16},{16,0},{1,17},{17,1},{2,18},{18,2},{3,19},{19,3},{4,20},{20... | collective-permute-start | bytes 688136 | tf_op jit(solution)/shard_map/ppermute | solution.py:214
  22.1 8.5 %collective-permute-start.8 = (bf16[1,5,6,16,128]{4,3,2,1,0:T(8,128)(2,1)S(1)}, bf16[1,5,6,16,128]{4,3,2,1,0:T(8,128)(2,1)S(1)}, u32[]{:S(2)}, u32[]{:S(2)}) collective-permute-start(bf16[1,5,6,16,128]{4,3,2,1,0:T(8,128)(2,1)S(1)} %dynamic-slice_bitcast_fusion), channel_id=1, source_target_pairs={{0,2},{1,3},{2,0},{3,1},{4,6},{5,7},{6,4},{7,5},{8,10},{9,11},{10,... | collective-permute-start | bytes 368648 | tf_op jit(solution)/shard_map/ppermute | solution.py:211
  23.7 2.3 %copy-start.4 = (f32[128]{0:T(128)S(1)}, f32[128]{0:T(128)}, u32[]{:S(2)}) copy-start(f32[128]{0:T(128)} %param.6) | copy-start | bytes 1540
  28.1 2.5 %copy-start.2 = (bf16[16,16,6,128]{3,1,2,0:T(8,128)(2,1)S(1)}, bf16[16,16,6,128]{3,1,2,0:T(8,128)(2,1)}, u32[]{:S(2)}) copy-start(bf16[16,16,6,128]{3,1,2,0:T(8,128)(2,1)} %param.4) | copy-start | bytes 1179652
  32.3 2.4 %copy-start.3 = (bf16[27,64,128]{2,1,0:T(8,128)(2,1)S(1)}, bf16[27,64,128]{2,1,0:T(8,128)(2,1)}, u32[]{:S(2)}) copy-start(bf16[27,64,128]{2,1,0:T(8,128)(2,1)} %up_ref.1) | copy-start | bytes 1327108
  32.3 2.4 %collective-permute-start.12 = (f32[2,6,128,128]{3,2,1,0:T(8,128)S(1)}, f32[2,6,128,128]{3,2,1,0:T(8,128)S(1)}, u32[]{:S(2)}, u32[]{:S(2)}) collective-permute-start(f32[2,6,128,128]{3,2,1,0:T(8,128)S(1)} %shard_map.48.refs_8_), channel_id=1, source_target_pairs={{0,1},{1,0},{2,3},{3,2},{4,5},{5,4},{6,7},{7,6},{8,9},{9,8},{10,11... | collective-permute-start | bytes 2359304 | tf_op jit(solution)/shard_map/ppermute | solution.py:211

commit v5 on v4

--- a/solution.py
+++ b/solution.py
@@ -9,6 +9,7 @@
 
 TILE = 4
 VMEM = pl.BlockSpec(memory_space=pltpu.VMEM)
+PARTS = 3
 PARAMS = pltpu.CompilerParams(vmem_limit_bytes=16 * 2**20)
 
 
@@ -81,7 +82,7 @@
     cout = taps.shape[0] // 3
     lane = lax.broadcasted_iota(jnp.int32, (cout, wide_z), 1)
     zeros = jnp.zeros((len(parts) * chans, wide_z), taps.dtype)
-    by_kind = {"all": 0, "tile": tile_start(total), "chip": chip_start(total)}
+    by_kind = {"tile": tile_start(total), "chip": chip_start(total)}
     starts = [by_kind[kind] for kind in kinds] + [by_kind["chip"]] * steps
     rows = {(slot, y): zeros for slot in range(len(stores) + 2) for y in (-1, wide_y)}
     for slot in range(len(stores) + 2):
@@ -145,7 +146,7 @@
     )(*parts, taps, *more)
 
 
-def up_body(keep_ref, came_ref, up_ref, out_ref):
+def up_body(keep_ref, came_ref, up_ref, out_ref, made, sems):
     core = lax.axis_index("gx") % 2
     _, wide_y, cout, wide_z = keep_ref.shape
     cup = up_ref.shape[1]
@@ -162,38 +163,48 @@
     def later(value):
         return jnp.where(edge, 0.0, pltpu.roll(value, wide_z - 1, 1))
 
-    for odd in range(2):
-        if odd:
-            left = jnp.concatenate([up_ref[18:27].reshape(9 * cup, cout), up_ref[0:9].reshape(9 * cup, cout)], axis=1)
-            right = jnp.concatenate(hidden, axis=0)
-        else:
-            left = up_ref[9:18].reshape(9 * cup, cout)
-            right = hidden[0]
-        product = jnp.dot(left, right, preferred_element_type=jnp.float32)
-
-        def term(tap_y, tap_z, y):
-            at = (3 * tap_y + tap_z) * cup
-            return product[at : at + cup, y * wide_z : (y + 1) * wide_z]
-
+    rest = [jnp.concatenate([value[:, wide_z:], jnp.zeros((cout, wide_z), value.dtype)], axis=1) for value in hidden]
+
+    def taps(*firsts):
+        return jnp.concatenate([up_ref[first : first + 3].reshape(3 * cup, cout) for first in firsts], axis=1)
+
+    sides = (
+        (taps(12), hidden[:1], taps(15, 9), [hidden[0], rest[0]]),
+        (taps(21, 3), hidden, taps(24, 18, 6, 0), [hidden[0], rest[0], hidden[1], rest[1]]),
+    )
+    copies = []
+    for odd, (left, right, left_odd, right_odd) in enumerate(sides):
+        products = (
+            jnp.dot(left, jnp.concatenate(right, axis=0), preferred_element_type=jnp.float32),
+            jnp.dot(left_odd, jnp.concatenate(right_odd, axis=0), preferred_element_type=jnp.float32),
+        )
         lines = []
         for y in range(wide_y):
-            for par_y in range(2):
-                choices = [(1, y)] if par_y == 0 else [(2, y)] + ([(0, y + 1)] if y + 1 < wide_y else [])
-                even = sum(term(tap_y, 1, at) for tap_y, at in choices)
-                plain = sum(term(tap_y, 2, at) for tap_y, at in choices)
-                moved = sum(term(tap_y, 0, at) for tap_y, at in choices)
+            for product in products:
+                moved, even, plain = (
+                    product[tap * cup : (tap + 1) * cup, y * wide_z : (y + 1) * wide_z] for tap in range(3)
+                )
                 lines.append(jnp.concatenate([even, plain + later(moved)], axis=1).astype(jnp.bfloat16))
-        woven = jnp.dot(jnp.concatenate(lines, axis=0), weave, preferred_element_type=jnp.float32)
-        out_ref[odd] = woven.astype(jnp.bfloat16).reshape(2 * wide_y, cup, 2 * wide_z)
+        share = len(lines) // PARTS
+        for part in range(PARTS):
+            rows = slice(part * share, (part + 1) * share)
+            woven = jnp.dot(jnp.concatenate(lines[rows], axis=0), weave, preferred_element_type=jnp.float32)
+            made[odd, rows] = woven.astype(jnp.bfloat16).reshape(share, cup, 2 * wide_z)
+            copies.append(pltpu.make_async_copy(made.at[odd, rows], out_ref.at[odd, rows], sems.at[len(copies)]))
+            copies[-1].start()
+    for copy in copies:
+        copy.wait()
 
 
 def upsample(keep, came, up):
     _, wide_y, _, wide_z = keep.shape
+    shape = (2, 2 * wide_y, up.shape[1], 2 * wide_z)
     return pl.pallas_call(
         up_body,
-        out_shape=jax.ShapeDtypeStruct((2, 2 * wide_y, up.shape[1], 2 * wide_z), jnp.bfloat16),
+        out_shape=jax.ShapeDtypeStruct(shape, jnp.bfloat16),
         in_specs=[VMEM] * 3,
-        out_specs=VMEM,
+        out_specs=pl.BlockSpec(memory_space=pl.ANY),
+        scratch_shapes=[pltpu.VMEM(shape, jnp.bfloat16), pltpu.SemaphoreType.DMA((2 * PARTS,))],
         compiler_params=PARAMS,
         cost_estimate=pl.CostEstimate(flops=10**9, bytes_accessed=3 * 10**6, transcendentals=0),
     )(keep, came, up)
@@ -217,10 +228,10 @@
     steps = range(tiles)
 
     straight = {step for step in steps if step % 4 == 2}
-    counts = [5] + [count for step in steps[1:] for count in ([5, 5] if step in straight else [wide])]
+    counts = [5, 5] + [count for step in steps[1:] for count in ([5, 5] if step in straight else [wide])]
 
     def starts():
-        found = [chip_start(total, 2)]
+        found = [chip_start(total, 2), chip_start(total)]
         for step in steps[1:]:
             mask = TILE * step
             found += [chip_start(total, mask), chip_start(total, mask ^ 2)] if step in straight else [tile_start(total, step)]
@@ -230,9 +241,9 @@
     span = -(-27 // groups)
     held = lax.dynamic_slice_in_dim(weight, jnp.minimum(group * span, 27 - span), span, 0)
     held, *pieces = lax.optimization_barrier((held, *pieces))
-    far_own, *pieces = pieces
+    far_own, own, *pieces = pieces
     held = jnp.stack([held] + [swap(held, TILE * step) for step in steps[1:]], axis=0)
-    near, far, far_order = {0: vol}, [], []
+    near, far, far_order = {0: own}, [], []
     for step in steps[1:]:
         if step in straight:
             near[step] = swap(after(pieces.pop(0), held), TILE * step)
@@ -247,7 +258,7 @@
         cut = [lax.dynamic_slice_in_dim(near[step], partner, 5, 0) if step else far_own for step in chosen]
         far.append(swap(jnp.stack(cut, axis=0), 2))
         far_order.append(chosen)
-    kinds = tuple("all" if step == 0 else "chip" if step in straight else "tile" for step in steps)
+    kinds = tuple("chip" if step in straight or not step else "tile" for step in steps)
     near = [near[step] for step in steps]
     bias = jnp.broadcast_to(conv_bias[:, None], (weight.shape[2], vol.shape[3]))
     far[-2], bias = lax.optimization_barrier((far[-2], bias))

time: 36.8 us -> 36.6 us (level)
    unnamed x10 -> x8, local copies, waits for them, and re-layouts: 1.05 us -> 1.04 us
where the time goes in v5:
time: 36.6 us; the launch traced here: 36.4 us
  starting transfers between devices  18.8 us (51%)
  waiting for transfers between devices  11.3 us (31%)
  Pallas kernels  4.89 us (13%)
  local copies, waits for them, and re-layouts  1.15 us (3%)
    ppermute x11, starting transfers between devices, swap(): return lax.ppermute(block, 'gx', [(i, i ^ mask) for i in range(size)])  17.2 us
    ppermute x11, waiting for transfers between devices, swap(): return lax.ppermute(block, 'gx', [(i, i ^ mask) for i in range(size)])  9.33 us
    pallas_call x2, Pallas kernels, conv_call(): pl.pallas_call(functools.partial(body, total, kinds), out_shape=jax.Shape...  2.78 us
    ppermute x2, waiting for transfers between devices, cross(): return lax.ppermute(block, 'groups', [(i, i ^ mask) for i in range(groups)])  2 us
    pallas_call x1, Pallas kernels, upsample(): pl.pallas_call(up_body, out_shape=jax.ShapeDtypeStruct(shape, jnp.bfloat1...  1.76 us
    ppermute x2, starting transfers between devices, cross(): return lax.ppermute(block, 'groups', [(i, i ^ mask) for i in range(groups)])  1.6 us
    unnamed x8, local copies, waits for them, and re-layouts  1.04 us
  transfers between devices with their start and end apart: 13, of which 8 were waited for; matrix products, arithmetic and copies ran while one was open for 1% of the time, Pallas kernels for 4%

profile of v5, /device:TPU:0, one launch (start us, length us, event | category | flops | bytes accessed | tf_op | source)
XLA Modules:
  0.0 36.4 jit_solution(15752117753211036560)
XLA Ops:
  0.0 1.0 %copy-done.1 = bf16[16,16,6,128]{3,1,2,0:T(8,128)(2,1)S(1)} copy-done((bf16[16,16,6,128]{3,1,2,0:T(8,128)(2,1)S(1)}, bf16[16,16,6,128]{3,1,2,0:T(8,128)(2,1)}, u32[]{:S(2)}) %copy-start.1) | copy-done | bytes 393240
  1.1 5.1 %collective-permute-start.3 = (bf16[14,16,128]{2,1,0:T(8,128)(2,1)S(1)}, bf16[14,16,128]{2,1,0:T(8,128)(2,1)S(1)}, u32[]{:S(2)}, u32[]{:S(2)}) collective-permute-start(bf16[14,16,128]{2,1,0:T(8,128)(2,1)S(1)} %dynamic-slice_bitcast_fusion.2), channel_id=1, source_target_pairs={{0,12},{1,13},{2,14},{3,15},{4,8},{5,9},{6,10},{7,11},{8,4},{9,5},... | collective-permute-start | bytes 172040 | tf_op jit(solution)/shard_map/ppermute | solution.py:222
  6.2 0.6 %collective-permute-start.1 = (bf16[14,16,128]{2,1,0:T(8,128)(2,1)S(1)}, bf16[14,16,128]{2,1,0:T(8,128)(2,1)S(1)}, u32[]{:S(2)}, u32[]{:S(2)}) collective-permute-start(bf16[14,16,128]{2,1,0:T(8,128)(2,1)S(1)} %dynamic-slice_bitcast_fusion.2), channel_id=1, source_target_pairs={{0,4},{1,5},{2,6},{3,7},{4,0},{5,1},{6,2},{7,3},{8,12},{9,13},{10,... | collective-permute-start | bytes 172040 | tf_op jit(solution)/shard_map/ppermute | solution.py:222
  6.9 1.4 %collective-permute-start = (bf16[7,6,16,128]{3,2,1,0:T(8,128)(2,1)S(1)}, bf16[7,6,16,128]{3,2,1,0:T(8,128)(2,1)S(1)}, u32[]{:S(2)}, u32[]{:S(2)}) collective-permute-start(bf16[7,6,16,128]{3,2,1,0:T(8,128)(2,1)S(1)} %get-tuple-element.29), channel_id=1, source_target_pairs={{0,4},{1,5},{2,6},{3,7},{4,0},{5,1},{6,2},{7,3},{8,12},{9,13},{10,... | collective-permute-start | bytes 516104 | tf_op jit(solution)/shard_map/ppermute | solution.py:222
  8.3 2.4 %collective-permute-start.5 = (bf16[7,6,16,128]{3,2,1,0:T(8,128)(2,1)S(1)}, bf16[7,6,16,128]{3,2,1,0:T(8,128)(2,1)S(1)}, u32[]{:S(2)}, u32[]{:S(2)}) collective-permute-start(bf16[7,6,16,128]{3,2,1,0:T(8,128)(2,1)S(1)} %get-tuple-element.33), channel_id=1, source_target_pairs={{0,12},{1,13},{2,14},{3,15},{4,8},{5,9},{6,10},{7,11},{8,4},{9,5},... | collective-permute-start | bytes 516104 | tf_op jit(solution)/shard_map/ppermute | solution.py:222
  10.7 1.2 %collective-permute-done.2 = bf16[14,16,128]{2,1,0:T(8,128)(2,1)S(1)} collective-permute-done((bf16[14,16,128]{2,1,0:T(8,128)(2,1)S(1)}, bf16[14,16,128]{2,1,0:T(8,128)(2,1)S(1)}, u32[]{:S(2)}, u32[]{:S(2)}) %collective-permute-start.2) | collective-permute-done | bytes 57376 | tf_op jit(solution)/shard_map/ppermute | solution.py:222
  11.9 0.1 collective-permute-done.1
  12.0 1.6 %collective-permute-start.9 = (bf16[4,14,16,128]{3,2,1,0:T(8,128)(2,1)S(1)}, bf16[4,14,16,128]{3,2,1,0:T(8,128)(2,1)S(1)}, u32[]{:S(2)}, u32[]{:S(2)}) collective-permute-start(bf16[4,14,16,128]{3,2,1,0:T(8,128)(2,1)S(1)} %get-tuple-element.40), channel_id=1, source_target_pairs={{0,16},{16,0},{1,17},{17,1},{2,18},{18,2},{3,19},{19,3},{4,20},{20... | collective-permute-start | bytes 688136 | tf_op jit(solution)/shard_map/ppermute | solution.py:225
  13.6 1.5 %collective-permute-start.10 = (bf16[4,14,16,128]{3,2,1,0:T(8,128)(2,1)S(1)}, bf16[4,14,16,128]{3,2,1,0:T(8,128)(2,1)S(1)}, u32[]{:S(2)}, u32[]{:S(2)}) collective-permute-start(bf16[4,14,16,128]{3,2,1,0:T(8,128)(2,1)S(1)} %get-tuple-element.40), channel_id=1, source_target_pairs={{0,2},{1,3},{2,0},{3,1},{4,6},{5,7},{6,4},{7,5},{8,10},{9,11},{10,... | collective-permute-start | bytes 688136 | tf_op jit(solution)/shard_map/ppermute | solution.py:222
  15.1 0.6 %collective-permute-done.refs_1_ = bf16[7,6,16,128]{3,2,1,0:T(8,128)(2,1)S(1)} collective-permute-done((bf16[7,6,16,128]{3,2,1,0:T(8,128)(2,1)S(1)}, bf16[7,6,16,128]{3,2,1,0:T(8,128)(2,1)S(1)}, u32[]{:S(2)}, u32[]{:S(2)}) %collective-permute-start) | collective-permute-done | bytes 172064 | tf_op jit(solution)/shard_map/ppermute | solution.py:222
  15.7 1.9 %collective-permute-start.7 = (bf16[2,5,6,16,128]{4,3,2,1,0:T(8,128)(2,1)S(1)}, bf16[2,5,6,16,128]{4,3,2,1,0:T(8,128)(2,1)S(1)}, u32[]{:S(2)}, u32[]{:S(2)}) collective-permute-start(bf16[2,5,6,16,128]{4,3,2,1,0:T(8,128)(2,1)S(1)} %pad_maximum_fusion.2), channel_id=1, source_target_pairs={{0,2},{1,3},{2,0},{3,1},{4,6},{5,7},{6,4},{7,5},{8,10},{9,11},{10,... | collective-permute-start | bytes 737288 | tf_op jit(solution)/shard_map/ppermute | solution.py:222
  17.7 1.7 %collective-permute-start.4 = (bf16[5,6,16,128]{3,2,1,0:T(8,128)(2,1)S(1)}, bf16[5,6,16,128]{3,2,1,0:T(8,128)(2,1)S(1)}, u32[]{:S(2)}, u32[]{:S(2)}) collective-permute-start(bf16[5,6,16,128]{3,2,1,0:T(8,128)(2,1)S(1)} %get-tuple-element.32), channel_id=1, source_target_pairs={{0,8},{1,9},{2,10},{3,11},{4,12},{5,13},{6,14},{7,15},{8,0},{9,1},... | collective-permute-start | bytes 368648 | tf_op jit(solution)/shard_map/ppermute | solution.py:222
  19.3 0.8 %collective-permute-start.6 = (bf16[5,6,16,128]{3,2,1,0:T(8,128)(2,1)S(1)}, bf16[5,6,16,128]{3,2,1,0:T(8,128)(2,1)S(1)}, u32[]{:S(2)}, u32[]{:S(2)}) collective-permute-start(bf16[5,6,16,128]{3,2,1,0:T(8,128)(2,1)S(1)} %get-tuple-element.35), channel_id=1, source_target_pairs={{0,10},{1,11},{2,8},{3,9},{4,14},{5,15},{6,12},{7,13},{8,2},{9,3},... | collective-permute-start | bytes 368648 | tf_op jit(solution)/shard_map/ppermute | solution.py:222
  20.2 1.8 %collective-permute-done.10 = bf16[4,14,16,128]{3,2,1,0:T(8,128)(2,1)S(1)} collective-permute-done((bf16[4,14,16,128]{3,2,1,0:T(8,128)(2,1)S(1)}, bf16[4,14,16,128]{3,2,1,0:T(8,128)(2,1)S(1)}, u32[]{:S(2)}, u32[]{:S(2)}) %collective-permute-start.10) | collective-permute-done | bytes 229408 | tf_op jit(solution)/shard_map/ppermute | solution.py:222
  22.1 1.6 %collective-permute-start.8 = (bf16[1,5,6,16,128]{4,3,2,1,0:T(8,128)(2,1)S(1)}, bf16[1,5,6,16,128]{4,3,2,1,0:T(8,128)(2,1)S(1)}, u32[]{:S(2)}, u32[]{:S(2)}) collective-permute-start(bf16[1,5,6,16,128]{4,3,2,1,0:T(8,128)(2,1)S(1)} %dynamic-slice_bitcast_fusion), channel_id=1, source_target_pairs={{0,2},{1,3},{2,0},{3,1},{4,6},{5,7},{6,4},{7,5},{8,10},{9,11},{10,... | collective-permute-start | bytes 368648 | tf_op jit(solution)/shard_map/ppermute | solution.py:222
  23.7 2.2 %collective-permute-done.7.refs_5_ = bf16[2,5,6,16,128]{4,3,2,1,0:T(8,128)(2,1)S(1)} collective-permute-done((bf16[2,5,6,16,128]{4,3,2,1,0:T(8,128)(2,1)S(1)}, bf16[2,5,6,16,128]{4,3,2,1,0:T(8,128)(2,1)S(1)}, u32[]{:S(2)}, u32[]{:S(2)}) %collective-permute-start.7) | collective-permute-done | bytes 245792 | tf_op jit(solution)/shard_map/ppermute | solution.py:222
  26.0 0.1 broadcast_in_dim.10.refs_9_
  26.0 2.0 %collective-permute-done.11 = bf16[4,14,16,128]{3,2,1,0:T(8,128)(2,1)S(1)} collective-permute-done((bf16[4,14,16,128]{3,2,1,0:T(8,128)(2,1)S(1)}, bf16[4,14,16,128]{3,2,1,0:T(8,128)(2,1)S(1)}, u32[]{:S(2)}, u32[]{:S(2)}) %collective-permute-start.11) | collective-permute-done | bytes 229408 | tf_op jit(solution)/shard_map/ppermute | solution.py:225
  28.1 0.3 shard_map.47.refs_7_
  28.4 2.1 %collective-permute-done.6 = bf16[5,6,16,128]{3,2,1,0:T(8,128)(2,1)S(1)} collective-permute-done((bf16[5,6,16,128]{3,2,1,0:T(8,128)(2,1)S(1)}, bf16[5,6,16,128]{3,2,1,0:T(8,128)(2,1)S(1)}, u32[]{:S(2)}, u32[]{:S(2)}) %collective-permute-start.6) | collective-permute-done | bytes 122912 | tf_op jit(solution)/shard_map/ppermute | solution.py:222
  30.6 1.7 %shard_map.48.refs_8_ = f32[2,6,128,128]{3,2,1,0:T(8,128)S(1)} custom-call(bf16[5,6,16,128]{3,2,1,0:T(8,128)(2,1)S(1)} %get-tuple-element.28.refs_0_, bf16[7,6,16,128]{3,2,1,0:T(8,128)(2,1)S(1)} %collective-permute-done.refs_1_, bf16[5,6,16,128]{3,2,1,0:T(8,128)(2,1)S(1)} %collective-permute-done.4.refs_2_, ...), custom_call_target="tpu_custom_call" | custom-call | flops 1000000000 | bytes 4000000 | tf_op jit(solution)/shard_map/pallas_call | solution.py:139
  32.4 1.0 %shard_map.49.keep_ref = f32[2,6,128,128]{3,2,1,0:T(8,128)S(1)} custom-call(bf16[5,6,16,128]{3,2,1,0:T(8,128)(2,1)S(1)} %get-tuple-element.28.refs_0_, bf16[7,6,16,128]{3,2,1,0:T(8,128)(2,1)S(1)} %collective-permute-done.refs_1_, bf16[5,6,16,128]{3,2,1,0:T(8,128)(2,1)S(1)} %collective-permute-done.4.refs_2_, ...), custom_call_target="tpu_custom_call" | custom-call | flops 1000000000 | bytes 4000000 | tf_op jit(solution)/shard_map/pallas_call | solution.py:139
  33.5 1.2 %collective-permute-done.12.came_ref = f32[2,6,128,128]{3,2,1,0:T(8,128)S(1)} collective-permute-done((f32[2,6,128,128]{3,2,1,0:T(8,128)S(1)}, f32[2,6,128,128]{3,2,1,0:T(8,128)S(1)}, u32[]{:S(2)}, u32[]{:S(2)}) %collective-permute-start.12) | collective-permute-done | bytes 786464 | tf_op jit(solution)/shard_map/ppermute | solution.py:222
  34.7 1.8 %shard_map.50 = bf16[2,12,64,256]{3,2,1,0:T(8,128)(2,1)} custom-call(f32[2,6,128,128]{3,2,1,0:T(8,128)S(1)} %shard_map.49.keep_ref, f32[2,6,128,128]{3,2,1,0:T(8,128)S(1)} %collective-permute-done.12.came_ref, bf16[27,64,128]{2,1,0:T(8,128)(2,1)S(1)} %copy-done.2), custom_call_target="tpu_custom_call" | custom-call | flops 1000000000 | bytes 3000000 | tf_op jit(solution)/shard_map/pallas_call | solution.py:202
  (23 shorter events, 0.4 us)
Async XLA Ops:
  0.0 1.1 %copy-start = (bf16[16,27,128]{2,0,1:T(8,128)(2,1)S(1)}, bf16[16,27,128]{2,0,1:T(8,128)(2,1)}, u32[]{:S(2)}) copy-start(bf16[16,27,128]{2,0,1:T(8,128)(2,1)} %param.5) | copy-start | bytes 331780
  0.0 1.0 %copy-start.1 = (bf16[16,16,6,128]{3,1,2,0:T(8,128)(2,1)S(1)}, bf16[16,16,6,128]{3,1,2,0:T(8,128)(2,1)}, u32[]{:S(2)}) copy-start(bf16[16,16,6,128]{3,1,2,0:T(8,128)(2,1)} %param.4) | copy-start | bytes 1179652
  1.1 9.5 %collective-permute-start.3 = (bf16[14,16,128]{2,1,0:T(8,128)(2,1)S(1)}, bf16[14,16,128]{2,1,0:T(8,128)(2,1)S(1)}, u32[]{:S(2)}, u32[]{:S(2)}) collective-permute-start(bf16[14,16,128]{2,1,0:T(8,128)(2,1)S(1)} %dynamic-slice_bitcast_fusion.2), channel_id=1, source_target_pairs={{0,12},{1,13},{2,14},{3,15},{4,8},{5,9},{6,10},{7,11},{8,4},{9,5},... | collective-permute-start | bytes 172040 | tf_op jit(solution)/shard_map/ppermute | solution.py:222
  6.2 5.6 %collective-permute-start.2 = (bf16[14,16,128]{2,1,0:T(8,128)(2,1)S(1)}, bf16[14,16,128]{2,1,0:T(8,128)(2,1)S(1)}, u32[]{:S(2)}, u32[]{:S(2)}) collective-permute-start(bf16[14,16,128]{2,1,0:T(8,128)(2,1)S(1)} %dynamic-slice_bitcast_fusion.2), channel_id=1, source_target_pairs={{0,8},{1,9},{2,10},{3,11},{4,12},{5,13},{6,14},{7,15},{8,0},{9,1},... | collective-permute-start | bytes 172040 | tf_op jit(solution)/shard_map/ppermute | solution.py:222
  6.2 5.8 %collective-permute-start.1 = (bf16[14,16,128]{2,1,0:T(8,128)(2,1)S(1)}, bf16[14,16,128]{2,1,0:T(8,128)(2,1)S(1)}, u32[]{:S(2)}, u32[]{:S(2)}) collective-permute-start(bf16[14,16,128]{2,1,0:T(8,128)(2,1)S(1)} %dynamic-slice_bitcast_fusion.2), channel_id=1, source_target_pairs={{0,4},{1,5},{2,6},{3,7},{4,0},{5,1},{6,2},{7,3},{8,12},{9,13},{10,... | collective-permute-start | bytes 172040 | tf_op jit(solution)/shard_map/ppermute | solution.py:222
  6.9 8.8 %collective-permute-start = (bf16[7,6,16,128]{3,2,1,0:T(8,128)(2,1)S(1)}, bf16[7,6,16,128]{3,2,1,0:T(8,128)(2,1)S(1)}, u32[]{:S(2)}, u32[]{:S(2)}) collective-permute-start(bf16[7,6,16,128]{3,2,1,0:T(8,128)(2,1)S(1)} %get-tuple-element.29), channel_id=1, source_target_pairs={{0,4},{1,5},{2,6},{3,7},{4,0},{5,1},{6,2},{7,3},{8,12},{9,13},{10,... | collective-permute-start | bytes 516104 | tf_op jit(solution)/shard_map/ppermute | solution.py:222
  8.3 11.1 %collective-permute-start.5 = (bf16[7,6,16,128]{3,2,1,0:T(8,128)(2,1)S(1)}, bf16[7,6,16,128]{3,2,1,0:T(8,128)(2,1)S(1)}, u32[]{:S(2)}, u32[]{:S(2)}) collective-permute-start(bf16[7,6,16,128]{3,2,1,0:T(8,128)(2,1)S(1)} %get-tuple-element.33), channel_id=1, source_target_pairs={{0,12},{1,13},{2,14},{3,15},{4,8},{5,9},{6,10},{7,11},{8,4},{9,5},... | collective-permute-start | bytes 516104 | tf_op jit(solution)/shard_map/ppermute | solution.py:222
  12.0 10.0 %collective-permute-start.9 = (bf16[4,14,16,128]{3,2,1,0:T(8,128)(2,1)S(1)}, bf16[4,14,16,128]{3,2,1,0:T(8,128)(2,1)S(1)}, u32[]{:S(2)}, u32[]{:S(2)}) collective-permute-start(bf16[4,14,16,128]{3,2,1,0:T(8,128)(2,1)S(1)} %get-tuple-element.40), channel_id=1, source_target_pairs={{0,16},{16,0},{1,17},{17,1},{2,18},{18,2},{3,19},{19,3},{4,20},{20... | collective-permute-start | bytes 688136 | tf_op jit(solution)/shard_map/ppermute | solution.py:225
  13.6 8.4 %collective-permute-start.10 = (bf16[4,14,16,128]{3,2,1,0:T(8,128)(2,1)S(1)}, bf16[4,14,16,128]{3,2,1,0:T(8,128)(2,1)S(1)}, u32[]{:S(2)}, u32[]{:S(2)}) collective-permute-start(bf16[4,14,16,128]{3,2,1,0:T(8,128)(2,1)S(1)} %get-tuple-element.40), channel_id=1, source_target_pairs={{0,2},{1,3},{2,0},{3,1},{4,6},{5,7},{6,4},{7,5},{8,10},{9,11},{10,... | collective-permute-start | bytes 688136 | tf_op jit(solution)/shard_map/ppermute | solution.py:222
  15.7 10.2 %collective-permute-start.7 = (bf16[2,5,6,16,128]{4,3,2,1,0:T(8,128)(2,1)S(1)}, bf16[2,5,6,16,128]{4,3,2,1,0:T(8,128)(2,1)S(1)}, u32[]{:S(2)}, u32[]{:S(2)}) collective-permute-start(bf16[2,5,6,16,128]{4,3,2,1,0:T(8,128)(2,1)S(1)} %pad_maximum_fusion.2), channel_id=1, source_target_pairs={{0,2},{1,3},{2,0},{3,1},{4,6},{5,7},{6,4},{7,5},{8,10},{9,11},{10,... | collective-permute-start | bytes 737288 | tf_op jit(solution)/shard_map/ppermute | solution.py:222
  17.7 10.8 %collective-permute-start.4 = (bf16[5,6,16,128]{3,2,1,0:T(8,128)(2,1)S(1)}, bf16[5,6,16,128]{3,2,1,0:T(8,128)(2,1)S(1)}, u32[]{:S(2)}, u32[]{:S(2)}) collective-permute-start(bf16[5,6,16,128]{3,2,1,0:T(8,128)(2,1)S(1)} %get-tuple-element.32), channel_id=1, source_target_pairs={{0,8},{1,9},{2,10},{3,11},{4,12},{5,13},{6,14},{7,15},{8,0},{9,1},... | collective-permute-start | bytes 368648 | tf_op jit(solution)/shard_map/ppermute | solution.py:222
  19.3 11.2 %collective-permute-start.6 = (bf16[5,6,16,128]{3,2,1,0:T(8,128)(2,1)S(1)}, bf16[5,6,16,128]{3,2,1,0:T(8,128)(2,1)S(1)}, u32[]{:S(2)}, u32[]{:S(2)}) collective-permute-start(bf16[5,6,16,128]{3,2,1,0:T(8,128)(2,1)S(1)} %get-tuple-element.35), channel_id=1, source_target_pairs={{0,10},{1,11},{2,8},{3,9},{4,14},{5,15},{6,12},{7,13},{8,2},{9,3},... | collective-permute-start | bytes 368648 | tf_op jit(solution)/shard_map/ppermute | solution.py:222
  22.0 6.0 %collective-permute-start.11 = (bf16[4,14,16,128]{3,2,1,0:T(8,128)(2,1)S(1)}, bf16[4,14,16,128]{3,2,1,0:T(8,128)(2,1)S(1)}, u32[]{:S(2)}, u32[]{:S(2)}) collective-permute-start(bf16[4,14,16,128]{3,2,1,0:T(8,128)(2,1)S(1)} %collective-permute-done.10), channel_id=1, source_target_pairs={{0,16},{16,0},{1,17},{17,1},{2,18},{18,2},{3,19},{19,3},{4,20},{20... | collective-permute-start | bytes 688136 | tf_op jit(solution)/shard_map/ppermute | solution.py:225
  22.1 8.5 %collective-permute-start.8 = (bf16[1,5,6,16,128]{4,3,2,1,0:T(8,128)(2,1)S(1)}, bf16[1,5,6,16,128]{4,3,2,1,0:T(8,128)(2,1)S(1)}, u32[]{:S(2)}, u32[]{:S(2)}) collective-permute-start(bf16[1,5,6,16,128]{4,3,2,1,0:T(8,128)(2,1)S(1)} %dynamic-slice_bitcast_fusion), channel_id=1, source_target_pairs={{0,2},{1,3},{2,0},{3,1},{4,6},{5,7},{6,4},{7,5},{8,10},{9,11},{10,... | collective-permute-start | bytes 368648 | tf_op jit(solution)/shard_map/ppermute | solution.py:222
  23.7 2.3 %copy-start.3 = (f32[128]{0:T(128)S(1)}, f32[128]{0:T(128)}, u32[]{:S(2)}) copy-start(f32[128]{0:T(128)} %param.6) | copy-start | bytes 1540
  32.3 2.4 %copy-start.2 = (bf16[27,64,128]{2,1,0:T(8,128)(2,1)S(1)}, bf16[27,64,128]{2,1,0:T(8,128)(2,1)}, u32[]{:S(2)}) copy-start(bf16[27,64,128]{2,1,0:T(8,128)(2,1)} %up_ref.1) | copy-start | bytes 1327108
  32.3 2.4 %collective-permute-start.12 = (f32[2,6,128,128]{3,2,1,0:T(8,128)S(1)}, f32[2,6,128,128]{3,2,1,0:T(8,128)S(1)}, u32[]{:S(2)}, u32[]{:S(2)}) collective-permute-start(f32[2,6,128,128]{3,2,1,0:T(8,128)S(1)} %shard_map.48.refs_8_), channel_id=1, source_target_pairs={{0,1},{1,0},{2,3},{3,2},{4,5},{5,4},{6,7},{7,6},{8,9},{9,8},{10,11... | collective-permute-start | bytes 2359304 | tf_op jit(solution)/shard_map/ppermute | solution.py:222

commit v6 on v5

--- a/solution.py
+++ b/solution.py
@@ -48,7 +48,7 @@
     )(vol)
 
 
-def taps_body(near_order, far_order, span, *refs):
+def taps_body(orders, span, *refs):
     weights, out_ref = refs[:-1], refs[-1]
     group = lax.axis_index("groups")
     cout = out_ref.shape[0] // 3
@@ -57,16 +57,16 @@
         for tap in range(tap_z, 27, 3):
             part = tap // span
             start = min(part * span, 27 - span)
-            for weight, order in zip(weights, (near_order, far_order)):
+            for weight, order in zip(weights, orders):
                 pieces += [weight[group ^ part, place, tap - start] for place in order]
         out_ref[tap_z * cout : (tap_z + 1) * cout] = jnp.concatenate(pieces, axis=0).T
 
 
-def taps_of(near_order, far_order, span, weights):
+def taps_of(orders, span, weights):
     cout, chans = weights[0].shape[-1], weights[0].shape[-2]
-    columns = 9 * chans * (len(near_order) + len(far_order))
+    columns = 9 * chans * sum(len(order) for order in orders)
     return pl.pallas_call(
-        functools.partial(taps_body, near_order, far_order, span),
+        functools.partial(taps_body, orders, span),
         out_shape=jax.ShapeDtypeStruct((3 * cout, columns), jnp.bfloat16),
         in_specs=[VMEM] * len(weights),
         out_specs=VMEM,
@@ -78,12 +78,13 @@
 def conv_planes(total, kinds, refs, taps, first, stores):
     steps = len(kinds)
     parts = [*refs[:steps], *(ref.at[at] for ref in refs[steps:] for at in range(ref.shape[0]))]
+    kinds = [*kinds, *["chip"] * (len(parts) - steps)]
     _, wide_y, chans, wide_z = parts[0].shape
     cout = taps.shape[0] // 3
     lane = lax.broadcasted_iota(jnp.int32, (cout, wide_z), 1)
     zeros = jnp.zeros((len(parts) * chans, wide_z), taps.dtype)
     by_kind = {"tile": tile_start(total), "chip": chip_start(total)}
-    starts = [by_kind[kind] for kind in kinds] + [by_kind["chip"]] * steps
+    starts = [by_kind[kind] for kind in kinds]
     rows = {(slot, y): zeros for slot in range(len(stores) + 2) for y in (-1, wide_y)}
     for slot in range(len(stores) + 2):
         at = first - 1 + slot
@@ -106,43 +107,57 @@
                 store(pair + side, part[cout : 2 * cout] + low + high)
 
 
-def send_body(total, kinds, *refs):
+def early_body(total, kinds, *refs):
     *parts, taps, out_ref = refs
     core = lax.axis_index("gx") % 2
 
-    def lower(y, value):
-        out_ref[core, y] = value
-
-    def upper(y, value):
-        out_ref[1 - core, y] = value
-
-    conv_planes(total, kinds, parts, taps, chip_first() + 1 - core, (lower, upper))
+    def store_at(at):
+        def store(y, value):
+            out_ref[at, y] = value
+
+        return store
+
+    conv_planes(total, kinds, parts, taps, chip_first() + 1 - core, (store_at(core), store_at(1 - core)))
+    conv_planes(total, kinds, parts, taps, chip_first() + 2 * core, (store_at(2),))
+
+
+def send_body(total, kinds, *refs):
+    *parts, taps, sums_ref, out_ref = refs
+    core = lax.axis_index("gx") % 2
+
+    def store_at(at):
+        def store(y, value):
+            out_ref[at, y] = sums_ref[at, y] + value
+
+        return store
+
+    conv_planes(total, kinds, parts, taps, chip_first() + 1 - core, (store_at(core), store_at(1 - core)))
 
 
 def keep_body(total, kinds, *refs):
-    *parts, taps, shared_ref, bias_ref, out_ref = refs
+    *parts, taps, sums_ref, shared_ref, bias_ref, out_ref = refs
     core = lax.axis_index("gx") % 2
     bias = bias_ref[...]
     plane = chip_first() + 2 * core
     inside = plane < total
 
     def store(y, value):
-        out_ref[core, y] = jnp.where(inside, value + bias, -jnp.inf)
+        out_ref[core, y] = jnp.where(inside, sums_ref[2, y] + value + bias, -jnp.inf)
         out_ref[1 - core, y] = shared_ref[0, y] + bias
 
     conv_planes(total, kinds, parts, taps, plane, (store,))
 
 
-def conv_call(body, total, kinds, parts, taps, *more):
+def conv_call(body, planes, total, kinds, parts, taps, *more):
     _, wide_y, _, wide_z = parts[0].shape
     cout = taps.shape[0] // 3
     return pl.pallas_call(
         functools.partial(body, total, kinds),
-        out_shape=jax.ShapeDtypeStruct((2, wide_y, cout, wide_z), jnp.float32),
+        out_shape=jax.ShapeDtypeStruct((planes, wide_y, cout, wide_z), jnp.float32),
         in_specs=[VMEM] * (len(parts) + 1 + len(more)),
         out_specs=VMEM,
         compiler_params=PARAMS,
-        cost_estimate=pl.CostEstimate(flops=10**9, bytes_accessed=4 * 10**6, transcendentals=0),
+        cost_estimate=pl.CostEstimate(flops=10**7, bytes_accessed=10**5, transcendentals=0),
     )(*parts, taps, *more)
 
 
@@ -258,15 +273,19 @@
         cut = [lax.dynamic_slice_in_dim(near[step], partner, 5, 0) if step else far_own for step in chosen]
         far.append(swap(jnp.stack(cut, axis=0), 2))
         far_order.append(chosen)
-    kinds = tuple("chip" if step in straight or not step else "tile" for step in steps)
-    near = [near[step] for step in steps]
     bias = jnp.broadcast_to(conv_bias[:, None], (weight.shape[2], vol.shape[3]))
     far[-2], bias = lax.optimization_barrier((far[-2], bias))
-    taps = taps_of(tuple(steps), tuple(step for chosen in far_order for step in chosen), span, columns)
-    parts = near + far
-    shared = conv_call(send_body, total, kinds, parts, taps)
+    first = [step for step in steps if step not in straight]
+    last = [step for step in steps if step in straight]
+    taps = taps_of([tuple(first)], span, columns[:1])
+    kinds = tuple("tile" if step else "chip" for step in first)
+    sums = conv_call(early_body, 3, total, kinds, [near[step] for step in first], taps)
+    taps = taps_of([tuple(last), tuple(step for chosen in far_order for step in chosen)], span, columns)
+    kinds = ("chip",) * len(last)
+    parts = [near[step] for step in last] + far
+    shared = conv_call(send_body, 2, total, kinds, parts, taps, sums)
     came = swap(shared, 1)
-    keep = conv_call(keep_body, total, kinds, parts, taps, shared, bias)
+    keep = conv_call(keep_body, 2, total, kinds, parts, taps, sums, shared, bias)
     out = upsample(keep, came, tconv_weight)
     return jnp.transpose(out, (0, 2, 1, 3))
 

time: 36.6 us -> 36.1 us (0.986)
  waiting for transfers between devices: 11.3 us -> 10.3 us
  Pallas kernels: 4.89 us -> 5.42 us
    ppermute x11, waiting for transfers between devices: 9.33 us -> 8.28 us  [swap(): return lax.ppermute(block, 'gx', [(i, i ^ mask) for i in range(size)])]
    pallas_call x2 -> x3, Pallas kernels: 2.78 us -> 3.21 us  [conv_call(): pl.pallas_call(functools.partial(body, total, kinds), out_shape=jax.Shape...]
  transfers between devices with their start and end apart: 13 -> 13, of which waited for: 8 -> 9; matrix products, arithmetic and copies ran while one was open for 1% -> 1% of each run, Pallas kernels for 4% -> 7%
where the time goes in v6:
time: 36.1 us; the launch traced here: 35.9 us
  starting transfers between devices  18.8 us (52%)
  waiting for transfers between devices  10.3 us (29%)
  Pallas kernels  5.42 us (15%)
  local copies, waits for them, and re-layouts  1.15 us (3%)
    ppermute x11, starting transfers between devices, swap(): return lax.ppermute(block, 'gx', [(i, i ^ mask) for i in range(size)])  17.2 us
    ppermute x11, waiting for transfers between devices, swap(): return lax.ppermute(block, 'gx', [(i, i ^ mask) for i in range(size)])  8.28 us
    pallas_call x3, Pallas kernels, conv_call(): pl.pallas_call(functools.partial(body, total, kinds), out_shape=jax.Shape...  3.21 us
    ppermute x2, waiting for transfers between devices, cross(): return lax.ppermute(block, 'groups', [(i, i ^ mask) for i in range(groups)])  2 us
    pallas_call x1, Pallas kernels, upsample(): pl.pallas_call(up_body, out_shape=jax.ShapeDtypeStruct(shape, jnp.bfloat1...  1.77 us
    ppermute x2, starting transfers between devices, cross(): return lax.ppermute(block, 'groups', [(i, i ^ mask) for i in range(groups)])  1.6 us
    unnamed x8, local copies, waits for them, and re-layouts  1.05 us
  transfers between devices with their start and end apart: 13, of which 9 were waited for; matrix products, arithmetic and copies ran while one was open for 1% of the time, Pallas kernels for 7%

profile of v6, /device:TPU:0, one launch (start us, length us, event | category | flops | bytes accessed | tf_op | source)
XLA Modules:
  0.0 35.9 jit_solution(10559640393761448828)
XLA Ops:
  0.0 1.0 %copy-done.1 = bf16[16,16,6,128]{3,1,2,0:T(8,128)(2,1)S(1)} copy-done((bf16[16,16,6,128]{3,1,2,0:T(8,128)(2,1)S(1)}, bf16[16,16,6,128]{3,1,2,0:T(8,128)(2,1)}, u32[]{:S(2)}) %copy-start.1) | copy-done | bytes 393240
  1.1 5.1 %collective-permute-start.2 = (bf16[14,16,128]{2,1,0:T(8,128)(2,1)S(1)}, bf16[14,16,128]{2,1,0:T(8,128)(2,1)S(1)}, u32[]{:S(2)}, u32[]{:S(2)}) collective-permute-start(bf16[14,16,128]{2,1,0:T(8,128)(2,1)S(1)} %dynamic-slice_bitcast_fusion.2), channel_id=1, source_target_pairs={{0,12},{1,13},{2,14},{3,15},{4,8},{5,9},{6,10},{7,11},{8,4},{9,5},... | collective-permute-start | bytes 172040 | tf_op jit(solution)/shard_map/ppermute | solution.py:237
  6.2 0.6 %collective-permute-start = (bf16[14,16,128]{2,1,0:T(8,128)(2,1)S(1)}, bf16[14,16,128]{2,1,0:T(8,128)(2,1)S(1)}, u32[]{:S(2)}, u32[]{:S(2)}) collective-permute-start(bf16[14,16,128]{2,1,0:T(8,128)(2,1)S(1)} %dynamic-slice_bitcast_fusion.2), channel_id=1, source_target_pairs={{0,4},{1,5},{2,6},{3,7},{4,0},{5,1},{6,2},{7,3},{8,12},{9,13},{10,... | collective-permute-start | bytes 172040 | tf_op jit(solution)/shard_map/ppermute | solution.py:237
  6.9 1.4 %collective-permute-start.5 = (bf16[7,6,16,128]{3,2,1,0:T(8,128)(2,1)S(1)}, bf16[7,6,16,128]{3,2,1,0:T(8,128)(2,1)S(1)}, u32[]{:S(2)}, u32[]{:S(2)}) collective-permute-start(bf16[7,6,16,128]{3,2,1,0:T(8,128)(2,1)S(1)} %get-tuple-element.34), channel_id=1, source_target_pairs={{0,4},{1,5},{2,6},{3,7},{4,0},{5,1},{6,2},{7,3},{8,12},{9,13},{10,... | collective-permute-start | bytes 516104 | tf_op jit(solution)/shard_map/ppermute | solution.py:237
  8.3 2.4 %collective-permute-start.7 = (bf16[7,6,16,128]{3,2,1,0:T(8,128)(2,1)S(1)}, bf16[7,6,16,128]{3,2,1,0:T(8,128)(2,1)S(1)}, u32[]{:S(2)}, u32[]{:S(2)}) collective-permute-start(bf16[7,6,16,128]{3,2,1,0:T(8,128)(2,1)S(1)} %get-tuple-element.36), channel_id=1, source_target_pairs={{0,12},{1,13},{2,14},{3,15},{4,8},{5,9},{6,10},{7,11},{8,4},{9,5},... | collective-permute-start | bytes 516104 | tf_op jit(solution)/shard_map/ppermute | solution.py:237
  10.7 1.2 %collective-permute-done.1 = bf16[14,16,128]{2,1,0:T(8,128)(2,1)S(1)} collective-permute-done((bf16[14,16,128]{2,1,0:T(8,128)(2,1)S(1)}, bf16[14,16,128]{2,1,0:T(8,128)(2,1)S(1)}, u32[]{:S(2)}, u32[]{:S(2)}) %collective-permute-start.1) | collective-permute-done | bytes 57376 | tf_op jit(solution)/shard_map/ppermute | solution.py:237
  12.0 1.6 %collective-permute-start.9 = (bf16[4,14,16,128]{3,2,1,0:T(8,128)(2,1)S(1)}, bf16[4,14,16,128]{3,2,1,0:T(8,128)(2,1)S(1)}, u32[]{:S(2)}, u32[]{:S(2)}) collective-permute-start(bf16[4,14,16,128]{3,2,1,0:T(8,128)(2,1)S(1)} %get-tuple-element.40), channel_id=1, source_target_pairs={{0,16},{16,0},{1,17},{17,1},{2,18},{18,2},{3,19},{19,3},{4,20},{20... | collective-permute-start | bytes 688136 | tf_op jit(solution)/shard_map/ppermute | solution.py:240
  13.6 1.5 %collective-permute-start.10 = (bf16[4,14,16,128]{3,2,1,0:T(8,128)(2,1)S(1)}, bf16[4,14,16,128]{3,2,1,0:T(8,128)(2,1)S(1)}, u32[]{:S(2)}, u32[]{:S(2)}) collective-permute-start(bf16[4,14,16,128]{3,2,1,0:T(8,128)(2,1)S(1)} %get-tuple-element.40), channel_id=1, source_target_pairs={{0,2},{1,3},{2,0},{3,1},{4,6},{5,7},{6,4},{7,5},{8,10},{9,11},{10,... | collective-permute-start | bytes 688136 | tf_op jit(solution)/shard_map/ppermute | solution.py:237
  15.1 0.6 %collective-permute-done.5.refs_1_ = bf16[7,6,16,128]{3,2,1,0:T(8,128)(2,1)S(1)} collective-permute-done((bf16[7,6,16,128]{3,2,1,0:T(8,128)(2,1)S(1)}, bf16[7,6,16,128]{3,2,1,0:T(8,128)(2,1)S(1)}, u32[]{:S(2)}, u32[]{:S(2)}) %collective-permute-start.5) | collective-permute-done | bytes 172064 | tf_op jit(solution)/shard_map/ppermute | solution.py:237
  15.7 1.9 %collective-permute-start.6 = (bf16[2,5,6,16,128]{4,3,2,1,0:T(8,128)(2,1)S(1)}, bf16[2,5,6,16,128]{4,3,2,1,0:T(8,128)(2,1)S(1)}, u32[]{:S(2)}, u32[]{:S(2)}) collective-permute-start(bf16[2,5,6,16,128]{4,3,2,1,0:T(8,128)(2,1)S(1)} %pad_maximum_fusion.2), channel_id=1, source_target_pairs={{0,2},{1,3},{2,0},{3,1},{4,6},{5,7},{6,4},{7,5},{8,10},{9,11},{10,... | collective-permute-start | bytes 737288 | tf_op jit(solution)/shard_map/ppermute | solution.py:237
  17.7 1.7 %collective-permute-start.3 = (bf16[5,6,16,128]{3,2,1,0:T(8,128)(2,1)S(1)}, bf16[5,6,16,128]{3,2,1,0:T(8,128)(2,1)S(1)}, u32[]{:S(2)}, u32[]{:S(2)}) collective-permute-start(bf16[5,6,16,128]{3,2,1,0:T(8,128)(2,1)S(1)} %get-tuple-element.30), channel_id=1, source_target_pairs={{0,8},{1,9},{2,10},{3,11},{4,12},{5,13},{6,14},{7,15},{8,0},{9,1},... | collective-permute-start | bytes 368648 | tf_op jit(solution)/shard_map/ppermute | solution.py:237
  19.3 0.8 %collective-permute-start.4 = (bf16[5,6,16,128]{3,2,1,0:T(8,128)(2,1)S(1)}, bf16[5,6,16,128]{3,2,1,0:T(8,128)(2,1)S(1)}, u32[]{:S(2)}, u32[]{:S(2)}) collective-permute-start(bf16[5,6,16,128]{3,2,1,0:T(8,128)(2,1)S(1)} %get-tuple-element.32), channel_id=1, source_target_pairs={{0,10},{1,11},{2,8},{3,9},{4,14},{5,15},{6,12},{7,13},{8,2},{9,3},... | collective-permute-start | bytes 368648 | tf_op jit(solution)/shard_map/ppermute | solution.py:237
  20.2 1.8 %collective-permute-done.10 = bf16[4,14,16,128]{3,2,1,0:T(8,128)(2,1)S(1)} collective-permute-done((bf16[4,14,16,128]{3,2,1,0:T(8,128)(2,1)S(1)}, bf16[4,14,16,128]{3,2,1,0:T(8,128)(2,1)S(1)}, u32[]{:S(2)}, u32[]{:S(2)}) %collective-permute-start.10) | collective-permute-done | bytes 229408 | tf_op jit(solution)/shard_map/ppermute | solution.py:237
  22.1 1.6 %collective-permute-start.8 = (bf16[1,5,6,16,128]{4,3,2,1,0:T(8,128)(2,1)S(1)}, bf16[1,5,6,16,128]{4,3,2,1,0:T(8,128)(2,1)S(1)}, u32[]{:S(2)}, u32[]{:S(2)}) collective-permute-start(bf16[1,5,6,16,128]{4,3,2,1,0:T(8,128)(2,1)S(1)} %dynamic-slice_bitcast_fusion), channel_id=1, source_target_pairs={{0,2},{1,3},{2,0},{3,1},{4,6},{5,7},{6,4},{7,5},{8,10},{9,11},{10,... | collective-permute-start | bytes 368648 | tf_op jit(solution)/shard_map/ppermute | solution.py:237
  23.7 0.2 shard_map.48.refs_3_
  23.9 1.2 %shard_map.49.refs_5_ = f32[3,6,128,128]{3,2,1,0:T(8,128)S(1)} custom-call(bf16[5,6,16,128]{3,2,1,0:T(8,128)(2,1)S(1)} %get-tuple-element.37.refs_0_, bf16[7,6,16,128]{3,2,1,0:T(8,128)(2,1)S(1)} %collective-permute-done.5.refs_1_, bf16[7,6,16,128]{3,2,1,0:T(8,128)(2,1)S(1)} %collective-permute-done.7.refs_2_, bf16[384,432]{1,0:T(8,128)(2,1)S(1)} %shard_map.48.refs_3_), custom_call_target="tpu_custom_call" | custom-call | flops 10000000 | bytes 100000 | tf_op jit(solution)/shard_map/pallas_call | solution.py:154
  25.2 0.8 %collective-permute-done.6.refs_2_ = bf16[2,5,6,16,128]{4,3,2,1,0:T(8,128)(2,1)S(1)} collective-permute-done((bf16[2,5,6,16,128]{4,3,2,1,0:T(8,128)(2,1)S(1)}, bf16[2,5,6,16,128]{4,3,2,1,0:T(8,128)(2,1)S(1)}, u32[]{:S(2)}, u32[]{:S(2)}) %collective-permute-start.6) | collective-permute-done | bytes 245792 | tf_op jit(solution)/shard_map/ppermute | solution.py:237
  26.0 2.0 %collective-permute-done.11 = bf16[4,14,16,128]{3,2,1,0:T(8,128)(2,1)S(1)} collective-permute-done((bf16[4,14,16,128]{3,2,1,0:T(8,128)(2,1)S(1)}, bf16[4,14,16,128]{3,2,1,0:T(8,128)(2,1)S(1)}, u32[]{:S(2)}, u32[]{:S(2)}) %collective-permute-start.11) | collective-permute-done | bytes 229408 | tf_op jit(solution)/shard_map/ppermute | solution.py:240
  28.1 0.2 shard_map.47.refs_4_
  28.4 2.1 %collective-permute-done.4 = bf16[5,6,16,128]{3,2,1,0:T(8,128)(2,1)S(1)} collective-permute-done((bf16[5,6,16,128]{3,2,1,0:T(8,128)(2,1)S(1)}, bf16[5,6,16,128]{3,2,1,0:T(8,128)(2,1)S(1)}, u32[]{:S(2)}, u32[]{:S(2)}) %collective-permute-start.4) | collective-permute-done | bytes 122912 | tf_op jit(solution)/shard_map/ppermute | solution.py:237
  30.6 1.2 %shard_map.50.refs_6_ = f32[2,6,128,128]{3,2,1,0:T(8,128)S(1)} custom-call(bf16[5,6,16,128]{3,2,1,0:T(8,128)(2,1)S(1)} %collective-permute-done.3.refs_0_, bf16[1,5,6,16,128]{4,3,2,1,0:T(8,128)(2,1)S(1)} %bitcast.19, bf16[2,5,6,16,128]{4,3,2,1,0:T(8,128)(2,1)S(1)} %collective-permute-done.6.refs_2_, ...), custom_call_target="tpu_custom_call" | custom-call | flops 10000000 | bytes 100000 | tf_op jit(solution)/shard_map/pallas_call | solution.py:154
  31.9 0.8 %shard_map.51.keep_ref = f32[2,6,128,128]{3,2,1,0:T(8,128)S(1)} custom-call(bf16[5,6,16,128]{3,2,1,0:T(8,128)(2,1)S(1)} %collective-permute-done.3.refs_0_, bf16[1,5,6,16,128]{4,3,2,1,0:T(8,128)(2,1)S(1)} %bitcast.20, bf16[2,5,6,16,128]{4,3,2,1,0:T(8,128)(2,1)S(1)} %collective-permute-done.6.refs_2_, ...), custom_call_target="tpu_custom_call" | custom-call | flops 10000000 | bytes 100000 | tf_op jit(solution)/shard_map/pallas_call | solution.py:154
  32.7 1.5 %collective-permute-done.12.came_ref = f32[2,6,128,128]{3,2,1,0:T(8,128)S(1)} collective-permute-done((f32[2,6,128,128]{3,2,1,0:T(8,128)S(1)}, f32[2,6,128,128]{3,2,1,0:T(8,128)S(1)}, u32[]{:S(2)}, u32[]{:S(2)}) %collective-permute-start.12) | collective-permute-done | bytes 786464 | tf_op jit(solution)/shard_map/ppermute | solution.py:237
  34.2 1.8 %shard_map.52 = bf16[2,12,64,256]{3,2,1,0:T(8,128)(2,1)} custom-call(f32[2,6,128,128]{3,2,1,0:T(8,128)S(1)} %shard_map.51.keep_ref, f32[2,6,128,128]{3,2,1,0:T(8,128)S(1)} %collective-permute-done.12.came_ref, bf16[27,64,128]{2,1,0:T(8,128)(2,1)S(1)} %copy-done.2), custom_call_target="tpu_custom_call" | custom-call | flops 1000000000 | bytes 3000000 | tf_op jit(solution)/shard_map/pallas_call | solution.py:217
  (25 shorter events, 0.7 us)
Async XLA Ops:
  0.0 1.1 %copy-start = (bf16[16,27,128]{2,0,1:T(8,128)(2,1)S(1)}, bf16[16,27,128]{2,0,1:T(8,128)(2,1)}, u32[]{:S(2)}) copy-start(bf16[16,27,128]{2,0,1:T(8,128)(2,1)} %param.5) | copy-start | bytes 331780
  0.0 1.0 %copy-start.1 = (bf16[16,16,6,128]{3,1,2,0:T(8,128)(2,1)S(1)}, bf16[16,16,6,128]{3,1,2,0:T(8,128)(2,1)}, u32[]{:S(2)}) copy-start(bf16[16,16,6,128]{3,1,2,0:T(8,128)(2,1)} %param.4) | copy-start | bytes 1179652
  1.1 9.5 %collective-permute-start.2 = (bf16[14,16,128]{2,1,0:T(8,128)(2,1)S(1)}, bf16[14,16,128]{2,1,0:T(8,128)(2,1)S(1)}, u32[]{:S(2)}, u32[]{:S(2)}) collective-permute-start(bf16[14,16,128]{2,1,0:T(8,128)(2,1)S(1)} %dynamic-slice_bitcast_fusion.2), channel_id=1, source_target_pairs={{0,12},{1,13},{2,14},{3,15},{4,8},{5,9},{6,10},{7,11},{8,4},{9,5},... | collective-permute-start | bytes 172040 | tf_op jit(solution)/shard_map/ppermute | solution.py:237
  6.2 5.6 %collective-permute-start.1 = (bf16[14,16,128]{2,1,0:T(8,128)(2,1)S(1)}, bf16[14,16,128]{2,1,0:T(8,128)(2,1)S(1)}, u32[]{:S(2)}, u32[]{:S(2)}) collective-permute-start(bf16[14,16,128]{2,1,0:T(8,128)(2,1)S(1)} %dynamic-slice_bitcast_fusion.2), channel_id=1, source_target_pairs={{0,8},{1,9},{2,10},{3,11},{4,12},{5,13},{6,14},{7,15},{8,0},{9,1},... | collective-permute-start | bytes 172040 | tf_op jit(solution)/shard_map/ppermute | solution.py:237
  6.2 5.8 %collective-permute-start = (bf16[14,16,128]{2,1,0:T(8,128)(2,1)S(1)}, bf16[14,16,128]{2,1,0:T(8,128)(2,1)S(1)}, u32[]{:S(2)}, u32[]{:S(2)}) collective-permute-start(bf16[14,16,128]{2,1,0:T(8,128)(2,1)S(1)} %dynamic-slice_bitcast_fusion.2), channel_id=1, source_target_pairs={{0,4},{1,5},{2,6},{3,7},{4,0},{5,1},{6,2},{7,3},{8,12},{9,13},{10,... | collective-permute-start | bytes 172040 | tf_op jit(solution)/shard_map/ppermute | solution.py:237
  6.9 8.8 %collective-permute-start.5 = (bf16[7,6,16,128]{3,2,1,0:T(8,128)(2,1)S(1)}, bf16[7,6,16,128]{3,2,1,0:T(8,128)(2,1)S(1)}, u32[]{:S(2)}, u32[]{:S(2)}) collective-permute-start(bf16[7,6,16,128]{3,2,1,0:T(8,128)(2,1)S(1)} %get-tuple-element.34), channel_id=1, source_target_pairs={{0,4},{1,5},{2,6},{3,7},{4,0},{5,1},{6,2},{7,3},{8,12},{9,13},{10,... | collective-permute-start | bytes 516104 | tf_op jit(solution)/shard_map/ppermute | solution.py:237
  8.3 11.1 %collective-permute-start.7 = (bf16[7,6,16,128]{3,2,1,0:T(8,128)(2,1)S(1)}, bf16[7,6,16,128]{3,2,1,0:T(8,128)(2,1)S(1)}, u32[]{:S(2)}, u32[]{:S(2)}) collective-permute-start(bf16[7,6,16,128]{3,2,1,0:T(8,128)(2,1)S(1)} %get-tuple-element.36), channel_id=1, source_target_pairs={{0,12},{1,13},{2,14},{3,15},{4,8},{5,9},{6,10},{7,11},{8,4},{9,5},... | collective-permute-start | bytes 516104 | tf_op jit(solution)/shard_map/ppermute | solution.py:237
  12.0 10.0 %collective-permute-start.9 = (bf16[4,14,16,128]{3,2,1,0:T(8,128)(2,1)S(1)}, bf16[4,14,16,128]{3,2,1,0:T(8,128)(2,1)S(1)}, u32[]{:S(2)}, u32[]{:S(2)}) collective-permute-start(bf16[4,14,16,128]{3,2,1,0:T(8,128)(2,1)S(1)} %get-tuple-element.40), channel_id=1, source_target_pairs={{0,16},{16,0},{1,17},{17,1},{2,18},{18,2},{3,19},{19,3},{4,20},{20... | collective-permute-start | bytes 688136 | tf_op jit(solution)/shard_map/ppermute | solution.py:240
  13.6 8.4 %collective-permute-start.10 = (bf16[4,14,16,128]{3,2,1,0:T(8,128)(2,1)S(1)}, bf16[4,14,16,128]{3,2,1,0:T(8,128)(2,1)S(1)}, u32[]{:S(2)}, u32[]{:S(2)}) collective-permute-start(bf16[4,14,16,128]{3,2,1,0:T(8,128)(2,1)S(1)} %get-tuple-element.40), channel_id=1, source_target_pairs={{0,2},{1,3},{2,0},{3,1},{4,6},{5,7},{6,4},{7,5},{8,10},{9,11},{10,... | collective-permute-start | bytes 688136 | tf_op jit(solution)/shard_map/ppermute | solution.py:237
  15.7 10.2 %collective-permute-start.6 = (bf16[2,5,6,16,128]{4,3,2,1,0:T(8,128)(2,1)S(1)}, bf16[2,5,6,16,128]{4,3,2,1,0:T(8,128)(2,1)S(1)}, u32[]{:S(2)}, u32[]{:S(2)}) collective-permute-start(bf16[2,5,6,16,128]{4,3,2,1,0:T(8,128)(2,1)S(1)} %pad_maximum_fusion.2), channel_id=1, source_target_pairs={{0,2},{1,3},{2,0},{3,1},{4,6},{5,7},{6,4},{7,5},{8,10},{9,11},{10,... | collective-permute-start | bytes 737288 | tf_op jit(solution)/shard_map/ppermute | solution.py:237
  17.7 10.8 %collective-permute-start.3 = (bf16[5,6,16,128]{3,2,1,0:T(8,128)(2,1)S(1)}, bf16[5,6,16,128]{3,2,1,0:T(8,128)(2,1)S(1)}, u32[]{:S(2)}, u32[]{:S(2)}) collective-permute-start(bf16[5,6,16,128]{3,2,1,0:T(8,128)(2,1)S(1)} %get-tuple-element.30), channel_id=1, source_target_pairs={{0,8},{1,9},{2,10},{3,11},{4,12},{5,13},{6,14},{7,15},{8,0},{9,1},... | collective-permute-start | bytes 368648 | tf_op jit(solution)/shard_map/ppermute | solution.py:237
  19.3 11.2 %collective-permute-start.4 = (bf16[5,6,16,128]{3,2,1,0:T(8,128)(2,1)S(1)}, bf16[5,6,16,128]{3,2,1,0:T(8,128)(2,1)S(1)}, u32[]{:S(2)}, u32[]{:S(2)}) collective-permute-start(bf16[5,6,16,128]{3,2,1,0:T(8,128)(2,1)S(1)} %get-tuple-element.32), channel_id=1, source_target_pairs={{0,10},{1,11},{2,8},{3,9},{4,14},{5,15},{6,12},{7,13},{8,2},{9,3},... | collective-permute-start | bytes 368648 | tf_op jit(solution)/shard_map/ppermute | solution.py:237
  22.0 6.0 %collective-permute-start.11 = (bf16[4,14,16,128]{3,2,1,0:T(8,128)(2,1)S(1)}, bf16[4,14,16,128]{3,2,1,0:T(8,128)(2,1)S(1)}, u32[]{:S(2)}, u32[]{:S(2)}) collective-permute-start(bf16[4,14,16,128]{3,2,1,0:T(8,128)(2,1)S(1)} %collective-permute-done.10), channel_id=1, source_target_pairs={{0,16},{16,0},{1,17},{17,1},{2,18},{18,2},{3,19},{19,3},{4,20},{20... | collective-permute-start | bytes 688136 | tf_op jit(solution)/shard_map/ppermute | solution.py:240
  22.1 8.5 %collective-permute-start.8 = (bf16[1,5,6,16,128]{4,3,2,1,0:T(8,128)(2,1)S(1)}, bf16[1,5,6,16,128]{4,3,2,1,0:T(8,128)(2,1)S(1)}, u32[]{:S(2)}, u32[]{:S(2)}) collective-permute-start(bf16[1,5,6,16,128]{4,3,2,1,0:T(8,128)(2,1)S(1)} %dynamic-slice_bitcast_fusion), channel_id=1, source_target_pairs={{0,2},{1,3},{2,0},{3,1},{4,6},{5,7},{6,4},{7,5},{8,10},{9,11},{10,... | collective-permute-start | bytes 368648 | tf_op jit(solution)/shard_map/ppermute | solution.py:237
  23.9 2.0 %copy-start.3 = (f32[128]{0:T(128)S(1)}, f32[128]{0:T(128)}, u32[]{:S(2)}) copy-start(f32[128]{0:T(128)} %param.6) | copy-start | bytes 1540
  31.8 2.4 %copy-start.2 = (bf16[27,64,128]{2,1,0:T(8,128)(2,1)S(1)}, bf16[27,64,128]{2,1,0:T(8,128)(2,1)}, u32[]{:S(2)}) copy-start(bf16[27,64,128]{2,1,0:T(8,128)(2,1)} %up_ref.1) | copy-start | bytes 1327108
  31.8 2.4 %collective-permute-start.12 = (f32[2,6,128,128]{3,2,1,0:T(8,128)S(1)}, f32[2,6,128,128]{3,2,1,0:T(8,128)S(1)}, u32[]{:S(2)}, u32[]{:S(2)}) collective-permute-start(f32[2,6,128,128]{3,2,1,0:T(8,128)S(1)} %shard_map.50.refs_6_), channel_id=1, source_target_pairs={{0,1},{1,0},{2,3},{3,2},{4,5},{5,4},{6,7},{7,6},{8,9},{9,8},{10,11... | collective-permute-start | bytes 2359304 | tf_op jit(solution)/shard_map/ppermute | solution.py:237

commit v7 on v6

--- a/solution.py
+++ b/solution.py
@@ -262,7 +262,7 @@
     for step in steps[1:]:
         if step in straight:
             near[step] = swap(after(pieces.pop(0), held), TILE * step)
-            far.append(swap(after(pieces.pop(0), held), TILE * step ^ 2)[None])
+            far.append(swap(pieces.pop(0), TILE * step ^ 2)[None])
             far_order.append([step])
         else:
             near[step] = swap(pieces.pop(0), TILE * step)

time: 36.1 us -> 35.4 us (0.981)
  waiting for transfers between devices: 10.3 us -> 9.6 us
    ppermute x2, waiting for transfers between devices: 2 us -> 1.39 us  [cross(): return lax.ppermute(block, 'groups', [(i, i ^ mask) for i in range(groups)])]
  transfers between devices with their start and end apart: 13 -> 13, of which waited for: 9 -> 8; matrix products, arithmetic and copies ran while one was open for 1% -> 1% of each run, Pallas kernels for 7% -> 7%
where the time goes in v7:
time: 35.4 us; the launch traced here: 35.3 us
  starting transfers between devices  18.8 us (53%)
  waiting for transfers between devices  9.6 us (27%)
  Pallas kernels  5.41 us (15%)
  local copies, waits for them, and re-layouts  1.15 us (3%)
    ppermute x11, starting transfers between devices, swap(): return lax.ppermute(block, 'gx', [(i, i ^ mask) for i in range(size)])  17.2 us
    ppermute x11, waiting for transfers between devices, swap(): return lax.ppermute(block, 'gx', [(i, i ^ mask) for i in range(size)])  8.22 us
    pallas_call x3, Pallas kernels, conv_call(): pl.pallas_call(functools.partial(body, total, kinds), out_shape=jax.Shape...  3.21 us
    pallas_call x1, Pallas kernels, upsample(): pl.pallas_call(up_body, out_shape=jax.ShapeDtypeStruct(shape, jnp.bfloat1...  1.77 us
    ppermute x2, starting transfers between devices, cross(): return lax.ppermute(block, 'groups', [(i, i ^ mask) for i in range(groups)])  1.57 us
    ppermute x2, waiting for transfers between devices, cross(): return lax.ppermute(block, 'groups', [(i, i ^ mask) for i in range(groups)])  1.39 us
    unnamed x8, local copies, waits for them, and re-layouts  1.05 us
  transfers between devices with their start and end apart: 13, of which 8 were waited for; matrix products, arithmetic and copies ran while one was open for 1% of the time, Pallas kernels for 7%

profile of v7, /device:TPU:0, one launch (start us, length us, event | category | flops | bytes accessed | tf_op | source)
XLA Modules:
  0.0 35.3 jit_solution(15069812626532555006)
XLA Ops:
  0.0 1.0 %copy-done.1 = bf16[16,16,6,128]{3,1,2,0:T(8,128)(2,1)S(1)} copy-done((bf16[16,16,6,128]{3,1,2,0:T(8,128)(2,1)S(1)}, bf16[16,16,6,128]{3,1,2,0:T(8,128)(2,1)}, u32[]{:S(2)}) %copy-start.1) | copy-done | bytes 393240
  1.1 5.1 %collective-permute-start.2 = (bf16[14,16,128]{2,1,0:T(8,128)(2,1)S(1)}, bf16[14,16,128]{2,1,0:T(8,128)(2,1)S(1)}, u32[]{:S(2)}, u32[]{:S(2)}) collective-permute-start(bf16[14,16,128]{2,1,0:T(8,128)(2,1)S(1)} %dynamic-slice_bitcast_fusion.2), channel_id=1, source_target_pairs={{0,12},{1,13},{2,14},{3,15},{4,8},{5,9},{6,10},{7,11},{8,4},{9,5},... | collective-permute-start | bytes 172040 | tf_op jit(solution)/shard_map/ppermute | solution.py:237
  6.2 0.6 %collective-permute-start = (bf16[14,16,128]{2,1,0:T(8,128)(2,1)S(1)}, bf16[14,16,128]{2,1,0:T(8,128)(2,1)S(1)}, u32[]{:S(2)}, u32[]{:S(2)}) collective-permute-start(bf16[14,16,128]{2,1,0:T(8,128)(2,1)S(1)} %dynamic-slice_bitcast_fusion.2), channel_id=1, source_target_pairs={{0,4},{1,5},{2,6},{3,7},{4,0},{5,1},{6,2},{7,3},{8,12},{9,13},{10,... | collective-permute-start | bytes 172040 | tf_op jit(solution)/shard_map/ppermute | solution.py:237
  6.9 1.4 %collective-permute-start.5 = (bf16[7,6,16,128]{3,2,1,0:T(8,128)(2,1)S(1)}, bf16[7,6,16,128]{3,2,1,0:T(8,128)(2,1)S(1)}, u32[]{:S(2)}, u32[]{:S(2)}) collective-permute-start(bf16[7,6,16,128]{3,2,1,0:T(8,128)(2,1)S(1)} %get-tuple-element.32), channel_id=1, source_target_pairs={{0,4},{1,5},{2,6},{3,7},{4,0},{5,1},{6,2},{7,3},{8,12},{9,13},{10,... | collective-permute-start | bytes 516104 | tf_op jit(solution)/shard_map/ppermute | solution.py:237
  8.3 2.4 %collective-permute-start.7 = (bf16[7,6,16,128]{3,2,1,0:T(8,128)(2,1)S(1)}, bf16[7,6,16,128]{3,2,1,0:T(8,128)(2,1)S(1)}, u32[]{:S(2)}, u32[]{:S(2)}) collective-permute-start(bf16[7,6,16,128]{3,2,1,0:T(8,128)(2,1)S(1)} %get-tuple-element.34), channel_id=1, source_target_pairs={{0,12},{1,13},{2,14},{3,15},{4,8},{5,9},{6,10},{7,11},{8,4},{9,5},... | collective-permute-start | bytes 516104 | tf_op jit(solution)/shard_map/ppermute | solution.py:237
  10.7 1.2 %collective-permute-done.1 = bf16[14,16,128]{2,1,0:T(8,128)(2,1)S(1)} collective-permute-done((bf16[14,16,128]{2,1,0:T(8,128)(2,1)S(1)}, bf16[14,16,128]{2,1,0:T(8,128)(2,1)S(1)}, u32[]{:S(2)}, u32[]{:S(2)}) %collective-permute-start.1) | collective-permute-done | bytes 57376 | tf_op jit(solution)/shard_map/ppermute | solution.py:237
  12.0 1.6 %collective-permute-start.9 = (bf16[4,14,16,128]{3,2,1,0:T(8,128)(2,1)S(1)}, bf16[4,14,16,128]{3,2,1,0:T(8,128)(2,1)S(1)}, u32[]{:S(2)}, u32[]{:S(2)}) collective-permute-start(bf16[4,14,16,128]{3,2,1,0:T(8,128)(2,1)S(1)} %get-tuple-element.38), channel_id=1, source_target_pairs={{0,16},{16,0},{1,17},{17,1},{2,18},{18,2},{3,19},{19,3},{4,20},{20... | collective-permute-start | bytes 688136 | tf_op jit(solution)/shard_map/ppermute | solution.py:240
  13.6 1.5 %collective-permute-start.10 = (bf16[4,14,16,128]{3,2,1,0:T(8,128)(2,1)S(1)}, bf16[4,14,16,128]{3,2,1,0:T(8,128)(2,1)S(1)}, u32[]{:S(2)}, u32[]{:S(2)}) collective-permute-start(bf16[4,14,16,128]{3,2,1,0:T(8,128)(2,1)S(1)} %get-tuple-element.38), channel_id=1, source_target_pairs={{0,2},{1,3},{2,0},{3,1},{4,6},{5,7},{6,4},{7,5},{8,10},{9,11},{10,... | collective-permute-start | bytes 688136 | tf_op jit(solution)/shard_map/ppermute | solution.py:237
  15.1 0.6 %collective-permute-done.5.refs_1_ = bf16[7,6,16,128]{3,2,1,0:T(8,128)(2,1)S(1)} collective-permute-done((bf16[7,6,16,128]{3,2,1,0:T(8,128)(2,1)S(1)}, bf16[7,6,16,128]{3,2,1,0:T(8,128)(2,1)S(1)}, u32[]{:S(2)}, u32[]{:S(2)}) %collective-permute-start.5) | collective-permute-done | bytes 172064 | tf_op jit(solution)/shard_map/ppermute | solution.py:237
  15.7 1.9 %collective-permute-start.6 = (bf16[2,5,6,16,128]{4,3,2,1,0:T(8,128)(2,1)S(1)}, bf16[2,5,6,16,128]{4,3,2,1,0:T(8,128)(2,1)S(1)}, u32[]{:S(2)}, u32[]{:S(2)}) collective-permute-start(bf16[2,5,6,16,128]{4,3,2,1,0:T(8,128)(2,1)S(1)} %pad_maximum_fusion.2), channel_id=1, source_target_pairs={{0,2},{1,3},{2,0},{3,1},{4,6},{5,7},{6,4},{7,5},{8,10},{9,11},{10,... | collective-permute-start | bytes 737288 | tf_op jit(solution)/shard_map/ppermute | solution.py:237
  17.7 1.6 %collective-permute-start.4 = (bf16[5,6,16,128]{3,2,1,0:T(8,128)(2,1)S(1)}, bf16[5,6,16,128]{3,2,1,0:T(8,128)(2,1)S(1)}, u32[]{:S(2)}, u32[]{:S(2)}) collective-permute-start(bf16[5,6,16,128]{3,2,1,0:T(8,128)(2,1)S(1)} %get-tuple-element.30), channel_id=1, source_target_pairs={{0,10},{1,11},{2,8},{3,9},{4,14},{5,15},{6,12},{7,13},{8,2},{9,3},... | collective-permute-start | bytes 368648 | tf_op jit(solution)/shard_map/ppermute | solution.py:237
  19.3 0.9 %collective-permute-start.3 = (bf16[5,6,16,128]{3,2,1,0:T(8,128)(2,1)S(1)}, bf16[5,6,16,128]{3,2,1,0:T(8,128)(2,1)S(1)}, u32[]{:S(2)}, u32[]{:S(2)}) collective-permute-start(bf16[5,6,16,128]{3,2,1,0:T(8,128)(2,1)S(1)} %get-tuple-element.29), channel_id=1, source_target_pairs={{0,8},{1,9},{2,10},{3,11},{4,12},{5,13},{6,14},{7,15},{8,0},{9,1},... | collective-permute-start | bytes 368648 | tf_op jit(solution)/shard_map/ppermute | solution.py:237
  20.2 3.1 %collective-permute-done.10 = bf16[4,14,16,128]{3,2,1,0:T(8,128)(2,1)S(1)} collective-permute-done((bf16[4,14,16,128]{3,2,1,0:T(8,128)(2,1)S(1)}, bf16[4,14,16,128]{3,2,1,0:T(8,128)(2,1)S(1)}, u32[]{:S(2)}, u32[]{:S(2)}) %collective-permute-start.10) | collective-permute-done | bytes 229408 | tf_op jit(solution)/shard_map/ppermute | solution.py:237
  23.4 1.7 %collective-permute-start.8 = (bf16[1,5,6,16,128]{4,3,2,1,0:T(8,128)(2,1)S(1)}, bf16[1,5,6,16,128]{4,3,2,1,0:T(8,128)(2,1)S(1)}, u32[]{:S(2)}, u32[]{:S(2)}) collective-permute-start(bf16[1,5,6,16,128]{4,3,2,1,0:T(8,128)(2,1)S(1)} %dynamic-slice_bitcast_fusion), channel_id=1, source_target_pairs={{0,2},{1,3},{2,0},{3,1},{4,6},{5,7},{6,4},{7,5},{8,10},{9,11},{10,... | collective-permute-start | bytes 368648 | tf_op jit(solution)/shard_map/ppermute | solution.py:237
  25.1 0.2 shard_map.48.refs_3_
  25.2 1.2 %shard_map.49.refs_5_ = f32[3,6,128,128]{3,2,1,0:T(8,128)S(1)} custom-call(bf16[5,6,16,128]{3,2,1,0:T(8,128)(2,1)S(1)} %get-tuple-element.35.refs_0_, bf16[7,6,16,128]{3,2,1,0:T(8,128)(2,1)S(1)} %collective-permute-done.5.refs_1_, bf16[7,6,16,128]{3,2,1,0:T(8,128)(2,1)S(1)} %collective-permute-done.7.refs_2_, bf16[384,432]{1,0:T(8,128)(2,1)S(1)} %shard_map.48.refs_3_), custom_call_target="tpu_custom_call" | custom-call | flops 10000000 | bytes 100000 | tf_op jit(solution)/shard_map/pallas_call | solution.py:154
  26.5 1.4 %collective-permute-done.6.refs_2_ = bf16[2,5,6,16,128]{4,3,2,1,0:T(8,128)(2,1)S(1)} collective-permute-done((bf16[2,5,6,16,128]{4,3,2,1,0:T(8,128)(2,1)S(1)}, bf16[2,5,6,16,128]{4,3,2,1,0:T(8,128)(2,1)S(1)}, u32[]{:S(2)}, u32[]{:S(2)}) %collective-permute-start.6) | collective-permute-done | bytes 245792 | tf_op jit(solution)/shard_map/ppermute | solution.py:237
  28.0 1.4 %collective-permute-done.11 = bf16[4,14,16,128]{3,2,1,0:T(8,128)(2,1)S(1)} collective-permute-done((bf16[4,14,16,128]{3,2,1,0:T(8,128)(2,1)S(1)}, bf16[4,14,16,128]{3,2,1,0:T(8,128)(2,1)S(1)}, u32[]{:S(2)}, u32[]{:S(2)}) %collective-permute-start.11) | collective-permute-done | bytes 229408 | tf_op jit(solution)/shard_map/ppermute | solution.py:240
  29.4 0.2 shard_map.47.refs_4_
  29.6 0.3 collective-permute-done.8.refs_3_
  29.9 1.2 %shard_map.50.refs_6_ = f32[2,6,128,128]{3,2,1,0:T(8,128)S(1)} custom-call(bf16[5,6,16,128]{3,2,1,0:T(8,128)(2,1)S(1)} %collective-permute-done.3.refs_0_, bf16[1,5,6,16,128]{4,3,2,1,0:T(8,128)(2,1)S(1)} %bitcast.19, bf16[2,5,6,16,128]{4,3,2,1,0:T(8,128)(2,1)S(1)} %collective-permute-done.6.refs_2_, ...), custom_call_target="tpu_custom_call" | custom-call | flops 10000000 | bytes 100000 | tf_op jit(solution)/shard_map/pallas_call | solution.py:154
  31.2 0.8 %shard_map.51.keep_ref = f32[2,6,128,128]{3,2,1,0:T(8,128)S(1)} custom-call(bf16[5,6,16,128]{3,2,1,0:T(8,128)(2,1)S(1)} %collective-permute-done.3.refs_0_, bf16[1,5,6,16,128]{4,3,2,1,0:T(8,128)(2,1)S(1)} %bitcast.20, bf16[2,5,6,16,128]{4,3,2,1,0:T(8,128)(2,1)S(1)} %collective-permute-done.6.refs_2_, ...), custom_call_target="tpu_custom_call" | custom-call | flops 10000000 | bytes 100000 | tf_op jit(solution)/shard_map/pallas_call | solution.py:154
  32.0 1.5 %collective-permute-done.12.came_ref = f32[2,6,128,128]{3,2,1,0:T(8,128)S(1)} collective-permute-done((f32[2,6,128,128]{3,2,1,0:T(8,128)S(1)}, f32[2,6,128,128]{3,2,1,0:T(8,128)S(1)}, u32[]{:S(2)}, u32[]{:S(2)}) %collective-permute-start.12) | collective-permute-done | bytes 786464 | tf_op jit(solution)/shard_map/ppermute | solution.py:237
  33.5 1.8 %shard_map.52 = bf16[2,12,64,256]{3,2,1,0:T(8,128)(2,1)} custom-call(f32[2,6,128,128]{3,2,1,0:T(8,128)S(1)} %shard_map.51.keep_ref, f32[2,6,128,128]{3,2,1,0:T(8,128)S(1)} %collective-permute-done.12.came_ref, bf16[27,64,128]{2,1,0:T(8,128)(2,1)S(1)} %copy-done.2), custom_call_target="tpu_custom_call" | custom-call | flops 1000000000 | bytes 3000000 | tf_op jit(solution)/shard_map/pallas_call | solution.py:217
  (25 shorter events, 0.5 us)
Async XLA Ops:
  0.0 1.1 %copy-start = (bf16[16,27,128]{2,0,1:T(8,128)(2,1)S(1)}, bf16[16,27,128]{2,0,1:T(8,128)(2,1)}, u32[]{:S(2)}) copy-start(bf16[16,27,128]{2,0,1:T(8,128)(2,1)} %param.5) | copy-start | bytes 331780
  0.0 1.0 %copy-start.1 = (bf16[16,16,6,128]{3,1,2,0:T(8,128)(2,1)S(1)}, bf16[16,16,6,128]{3,1,2,0:T(8,128)(2,1)}, u32[]{:S(2)}) copy-start(bf16[16,16,6,128]{3,1,2,0:T(8,128)(2,1)} %param.4) | copy-start | bytes 1179652
  1.1 9.5 %collective-permute-start.2 = (bf16[14,16,128]{2,1,0:T(8,128)(2,1)S(1)}, bf16[14,16,128]{2,1,0:T(8,128)(2,1)S(1)}, u32[]{:S(2)}, u32[]{:S(2)}) collective-permute-start(bf16[14,16,128]{2,1,0:T(8,128)(2,1)S(1)} %dynamic-slice_bitcast_fusion.2), channel_id=1, source_target_pairs={{0,12},{1,13},{2,14},{3,15},{4,8},{5,9},{6,10},{7,11},{8,4},{9,5},... | collective-permute-start | bytes 172040 | tf_op jit(solution)/shard_map/ppermute | solution.py:237
  6.2 5.6 %collective-permute-start.1 = (bf16[14,16,128]{2,1,0:T(8,128)(2,1)S(1)}, bf16[14,16,128]{2,1,0:T(8,128)(2,1)S(1)}, u32[]{:S(2)}, u32[]{:S(2)}) collective-permute-start(bf16[14,16,128]{2,1,0:T(8,128)(2,1)S(1)} %dynamic-slice_bitcast_fusion.2), channel_id=1, source_target_pairs={{0,8},{1,9},{2,10},{3,11},{4,12},{5,13},{6,14},{7,15},{8,0},{9,1},... | collective-permute-start | bytes 172040 | tf_op jit(solution)/shard_map/ppermute | solution.py:237
  6.2 5.8 %collective-permute-start = (bf16[14,16,128]{2,1,0:T(8,128)(2,1)S(1)}, bf16[14,16,128]{2,1,0:T(8,128)(2,1)S(1)}, u32[]{:S(2)}, u32[]{:S(2)}) collective-permute-start(bf16[14,16,128]{2,1,0:T(8,128)(2,1)S(1)} %dynamic-slice_bitcast_fusion.2), channel_id=1, source_target_pairs={{0,4},{1,5},{2,6},{3,7},{4,0},{5,1},{6,2},{7,3},{8,12},{9,13},{10,... | collective-permute-start | bytes 172040 | tf_op jit(solution)/shard_map/ppermute | solution.py:237
  6.9 8.8 %collective-permute-start.5 = (bf16[7,6,16,128]{3,2,1,0:T(8,128)(2,1)S(1)}, bf16[7,6,16,128]{3,2,1,0:T(8,128)(2,1)S(1)}, u32[]{:S(2)}, u32[]{:S(2)}) collective-permute-start(bf16[7,6,16,128]{3,2,1,0:T(8,128)(2,1)S(1)} %get-tuple-element.32), channel_id=1, source_target_pairs={{0,4},{1,5},{2,6},{3,7},{4,0},{5,1},{6,2},{7,3},{8,12},{9,13},{10,... | collective-permute-start | bytes 516104 | tf_op jit(solution)/shard_map/ppermute | solution.py:237
  8.3 11.0 %collective-permute-start.7 = (bf16[7,6,16,128]{3,2,1,0:T(8,128)(2,1)S(1)}, bf16[7,6,16,128]{3,2,1,0:T(8,128)(2,1)S(1)}, u32[]{:S(2)}, u32[]{:S(2)}) collective-permute-start(bf16[7,6,16,128]{3,2,1,0:T(8,128)(2,1)S(1)} %get-tuple-element.34), channel_id=1, source_target_pairs={{0,12},{1,13},{2,14},{3,15},{4,8},{5,9},{6,10},{7,11},{8,4},{9,5},... | collective-permute-start | bytes 516104 | tf_op jit(solution)/shard_map/ppermute | solution.py:237
  12.0 11.3 %collective-permute-start.9 = (bf16[4,14,16,128]{3,2,1,0:T(8,128)(2,1)S(1)}, bf16[4,14,16,128]{3,2,1,0:T(8,128)(2,1)S(1)}, u32[]{:S(2)}, u32[]{:S(2)}) collective-permute-start(bf16[4,14,16,128]{3,2,1,0:T(8,128)(2,1)S(1)} %get-tuple-element.38), channel_id=1, source_target_pairs={{0,16},{16,0},{1,17},{17,1},{2,18},{18,2},{3,19},{19,3},{4,20},{20... | collective-permute-start | bytes 688136 | tf_op jit(solution)/shard_map/ppermute | solution.py:240
  13.6 9.7 %collective-permute-start.10 = (bf16[4,14,16,128]{3,2,1,0:T(8,128)(2,1)S(1)}, bf16[4,14,16,128]{3,2,1,0:T(8,128)(2,1)S(1)}, u32[]{:S(2)}, u32[]{:S(2)}) collective-permute-start(bf16[4,14,16,128]{3,2,1,0:T(8,128)(2,1)S(1)} %get-tuple-element.38), channel_id=1, source_target_pairs={{0,2},{1,3},{2,0},{3,1},{4,6},{5,7},{6,4},{7,5},{8,10},{9,11},{10,... | collective-permute-start | bytes 688136 | tf_op jit(solution)/shard_map/ppermute | solution.py:237
  15.7 12.2 %collective-permute-start.6 = (bf16[2,5,6,16,128]{4,3,2,1,0:T(8,128)(2,1)S(1)}, bf16[2,5,6,16,128]{4,3,2,1,0:T(8,128)(2,1)S(1)}, u32[]{:S(2)}, u32[]{:S(2)}) collective-permute-start(bf16[2,5,6,16,128]{4,3,2,1,0:T(8,128)(2,1)S(1)} %pad_maximum_fusion.2), channel_id=1, source_target_pairs={{0,2},{1,3},{2,0},{3,1},{4,6},{5,7},{6,4},{7,5},{8,10},{9,11},{10,... | collective-permute-start | bytes 737288 | tf_op jit(solution)/shard_map/ppermute | solution.py:237
  17.7 11.9 %collective-permute-start.4 = (bf16[5,6,16,128]{3,2,1,0:T(8,128)(2,1)S(1)}, bf16[5,6,16,128]{3,2,1,0:T(8,128)(2,1)S(1)}, u32[]{:S(2)}, u32[]{:S(2)}) collective-permute-start(bf16[5,6,16,128]{3,2,1,0:T(8,128)(2,1)S(1)} %get-tuple-element.30), channel_id=1, source_target_pairs={{0,10},{1,11},{2,8},{3,9},{4,14},{5,15},{6,12},{7,13},{8,2},{9,3},... | collective-permute-start | bytes 368648 | tf_op jit(solution)/shard_map/ppermute | solution.py:237
  19.3 10.3 %collective-permute-start.3 = (bf16[5,6,16,128]{3,2,1,0:T(8,128)(2,1)S(1)}, bf16[5,6,16,128]{3,2,1,0:T(8,128)(2,1)S(1)}, u32[]{:S(2)}, u32[]{:S(2)}) collective-permute-start(bf16[5,6,16,128]{3,2,1,0:T(8,128)(2,1)S(1)} %get-tuple-element.29), channel_id=1, source_target_pairs={{0,8},{1,9},{2,10},{3,11},{4,12},{5,13},{6,14},{7,15},{8,0},{9,1},... | collective-permute-start | bytes 368648 | tf_op jit(solution)/shard_map/ppermute | solution.py:237
  23.3 6.0 %collective-permute-start.11 = (bf16[4,14,16,128]{3,2,1,0:T(8,128)(2,1)S(1)}, bf16[4,14,16,128]{3,2,1,0:T(8,128)(2,1)S(1)}, u32[]{:S(2)}, u32[]{:S(2)}) collective-permute-start(bf16[4,14,16,128]{3,2,1,0:T(8,128)(2,1)S(1)} %collective-permute-done.10), channel_id=1, source_target_pairs={{0,16},{16,0},{1,17},{17,1},{2,18},{18,2},{3,19},{19,3},{4,20},{20... | collective-permute-start | bytes 688136 | tf_op jit(solution)/shard_map/ppermute | solution.py:240
  23.4 6.6 %collective-permute-start.8 = (bf16[1,5,6,16,128]{4,3,2,1,0:T(8,128)(2,1)S(1)}, bf16[1,5,6,16,128]{4,3,2,1,0:T(8,128)(2,1)S(1)}, u32[]{:S(2)}, u32[]{:S(2)}) collective-permute-start(bf16[1,5,6,16,128]{4,3,2,1,0:T(8,128)(2,1)S(1)} %dynamic-slice_bitcast_fusion), channel_id=1, source_target_pairs={{0,2},{1,3},{2,0},{3,1},{4,6},{5,7},{6,4},{7,5},{8,10},{9,11},{10,... | collective-permute-start | bytes 368648 | tf_op jit(solution)/shard_map/ppermute | solution.py:237
  25.2 2.7 %copy-start.3 = (f32[128]{0:T(128)S(1)}, f32[128]{0:T(128)}, u32[]{:S(2)}) copy-start(f32[128]{0:T(128)} %param.6) | copy-start | bytes 1540
  31.1 2.4 %copy-start.2 = (bf16[27,64,128]{2,1,0:T(8,128)(2,1)S(1)}, bf16[27,64,128]{2,1,0:T(8,128)(2,1)}, u32[]{:S(2)}) copy-start(bf16[27,64,128]{2,1,0:T(8,128)(2,1)} %up_ref.1) | copy-start | bytes 1327108
  31.2 2.4 %collective-permute-start.12 = (f32[2,6,128,128]{3,2,1,0:T(8,128)S(1)}, f32[2,6,128,128]{3,2,1,0:T(8,128)S(1)}, u32[]{:S(2)}, u32[]{:S(2)}) collective-permute-start(f32[2,6,128,128]{3,2,1,0:T(8,128)S(1)} %shard_map.50.refs_6_), channel_id=1, source_target_pairs={{0,1},{1,0},{2,3},{3,2},{4,5},{5,4},{6,7},{7,6},{8,9},{9,8},{10,11... | collective-permute-start | bytes 2359304 | tf_op jit(solution)/shard_map/ppermute | solution.py:237

commit v8 on v7

--- a/solution.py
+++ b/solution.py
@@ -157,7 +157,7 @@
         in_specs=[VMEM] * (len(parts) + 1 + len(more)),
         out_specs=VMEM,
         compiler_params=PARAMS,
-        cost_estimate=pl.CostEstimate(flops=10**7, bytes_accessed=10**5, transcendentals=0),
+        cost_estimate=pl.CostEstimate(flops=10**6, bytes_accessed=10**4, transcendentals=0),
     )(*parts, taps, *more)
 
 

time: 35.4 us -> 35.4 us (level)
  no operation moved by 1% of the time
where the time goes in v8:
time: 35.4 us; the launch traced here: 35.3 us
  starting transfers between devices  18.8 us (53%)
  waiting for transfers between devices  9.6 us (27%)
  Pallas kernels  5.41 us (15%)
  local copies, waits for them, and re-layouts  1.15 us (3%)
    ppermute x11, starting transfers between devices, swap(): return lax.ppermute(block, 'gx', [(i, i ^ mask) for i in range(size)])  17.2 us
    ppermute x11, waiting for transfers between devices, swap(): return lax.ppermute(block, 'gx', [(i, i ^ mask) for i in range(size)])  8.22 us
    pallas_call x3, Pallas kernels, conv_call(): pl.pallas_call(functools.partial(body, total, kinds), out_shape=jax.Shape...  3.21 us
    pallas_call x1, Pallas kernels, upsample(): pl.pallas_call(up_body, out_shape=jax.ShapeDtypeStruct(shape, jnp.bfloat1...  1.77 us
    ppermute x2, starting transfers between devices, cross(): return lax.ppermute(block, 'groups', [(i, i ^ mask) for i in range(groups)])  1.57 us
    ppermute x2, waiting for transfers between devices, cross(): return lax.ppermute(block, 'groups', [(i, i ^ mask) for i in range(groups)])  1.39 us
    unnamed x8, local copies, waits for them, and re-layouts  1.05 us
  transfers between devices with their start and end apart: 13, of which 8 were waited for; matrix products, arithmetic and copies ran while one was open for 1% of the time, Pallas kernels for 7%

profile of v8, /device:TPU:0, one launch (start us, length us, event | category | flops | bytes accessed | tf_op | source)
XLA Modules:
  0.0 35.3 jit_solution(15069812626532555006)
XLA Ops:
  0.0 1.0 %copy-done.1 = bf16[16,16,6,128]{3,1,2,0:T(8,128)(2,1)S(1)} copy-done((bf16[16,16,6,128]{3,1,2,0:T(8,128)(2,1)S(1)}, bf16[16,16,6,128]{3,1,2,0:T(8,128)(2,1)}, u32[]{:S(2)}) %copy-start.1) | copy-done | bytes 393240
  1.1 5.1 %collective-permute-start.2 = (bf16[14,16,128]{2,1,0:T(8,128)(2,1)S(1)}, bf16[14,16,128]{2,1,0:T(8,128)(2,1)S(1)}, u32[]{:S(2)}, u32[]{:S(2)}) collective-permute-start(bf16[14,16,128]{2,1,0:T(8,128)(2,1)S(1)} %dynamic-slice_bitcast_fusion.2), channel_id=1, source_target_pairs={{0,12},{1,13},{2,14},{3,15},{4,8},{5,9},{6,10},{7,11},{8,4},{9,5},... | collective-permute-start | bytes 172040 | tf_op jit(solution)/shard_map/ppermute | solution.py:237
  6.2 0.6 %collective-permute-start = (bf16[14,16,128]{2,1,0:T(8,128)(2,1)S(1)}, bf16[14,16,128]{2,1,0:T(8,128)(2,1)S(1)}, u32[]{:S(2)}, u32[]{:S(2)}) collective-permute-start(bf16[14,16,128]{2,1,0:T(8,128)(2,1)S(1)} %dynamic-slice_bitcast_fusion.2), channel_id=1, source_target_pairs={{0,4},{1,5},{2,6},{3,7},{4,0},{5,1},{6,2},{7,3},{8,12},{9,13},{10,... | collective-permute-start | bytes 172040 | tf_op jit(solution)/shard_map/ppermute | solution.py:237
  6.9 1.4 %collective-permute-start.5 = (bf16[7,6,16,128]{3,2,1,0:T(8,128)(2,1)S(1)}, bf16[7,6,16,128]{3,2,1,0:T(8,128)(2,1)S(1)}, u32[]{:S(2)}, u32[]{:S(2)}) collective-permute-start(bf16[7,6,16,128]{3,2,1,0:T(8,128)(2,1)S(1)} %get-tuple-element.32), channel_id=1, source_target_pairs={{0,4},{1,5},{2,6},{3,7},{4,0},{5,1},{6,2},{7,3},{8,12},{9,13},{10,... | collective-permute-start | bytes 516104 | tf_op jit(solution)/shard_map/ppermute | solution.py:237
  8.3 2.4 %collective-permute-start.7 = (bf16[7,6,16,128]{3,2,1,0:T(8,128)(2,1)S(1)}, bf16[7,6,16,128]{3,2,1,0:T(8,128)(2,1)S(1)}, u32[]{:S(2)}, u32[]{:S(2)}) collective-permute-start(bf16[7,6,16,128]{3,2,1,0:T(8,128)(2,1)S(1)} %get-tuple-element.34), channel_id=1, source_target_pairs={{0,12},{1,13},{2,14},{3,15},{4,8},{5,9},{6,10},{7,11},{8,4},{9,5},... | collective-permute-start | bytes 516104 | tf_op jit(solution)/shard_map/ppermute | solution.py:237
  10.7 1.2 %collective-permute-done.1 = bf16[14,16,128]{2,1,0:T(8,128)(2,1)S(1)} collective-permute-done((bf16[14,16,128]{2,1,0:T(8,128)(2,1)S(1)}, bf16[14,16,128]{2,1,0:T(8,128)(2,1)S(1)}, u32[]{:S(2)}, u32[]{:S(2)}) %collective-permute-start.1) | collective-permute-done | bytes 57376 | tf_op jit(solution)/shard_map/ppermute | solution.py:237
  12.0 1.6 %collective-permute-start.9 = (bf16[4,14,16,128]{3,2,1,0:T(8,128)(2,1)S(1)}, bf16[4,14,16,128]{3,2,1,0:T(8,128)(2,1)S(1)}, u32[]{:S(2)}, u32[]{:S(2)}) collective-permute-start(bf16[4,14,16,128]{3,2,1,0:T(8,128)(2,1)S(1)} %get-tuple-element.38), channel_id=1, source_target_pairs={{0,16},{16,0},{1,17},{17,1},{2,18},{18,2},{3,19},{19,3},{4,20},{20... | collective-permute-start | bytes 688136 | tf_op jit(solution)/shard_map/ppermute | solution.py:240
  13.6 1.5 %collective-permute-start.10 = (bf16[4,14,16,128]{3,2,1,0:T(8,128)(2,1)S(1)}, bf16[4,14,16,128]{3,2,1,0:T(8,128)(2,1)S(1)}, u32[]{:S(2)}, u32[]{:S(2)}) collective-permute-start(bf16[4,14,16,128]{3,2,1,0:T(8,128)(2,1)S(1)} %get-tuple-element.38), channel_id=1, source_target_pairs={{0,2},{1,3},{2,0},{3,1},{4,6},{5,7},{6,4},{7,5},{8,10},{9,11},{10,... | collective-permute-start | bytes 688136 | tf_op jit(solution)/shard_map/ppermute | solution.py:237
  15.1 0.6 %collective-permute-done.5.refs_1_ = bf16[7,6,16,128]{3,2,1,0:T(8,128)(2,1)S(1)} collective-permute-done((bf16[7,6,16,128]{3,2,1,0:T(8,128)(2,1)S(1)}, bf16[7,6,16,128]{3,2,1,0:T(8,128)(2,1)S(1)}, u32[]{:S(2)}, u32[]{:S(2)}) %collective-permute-start.5) | collective-permute-done | bytes 172064 | tf_op jit(solution)/shard_map/ppermute | solution.py:237
  15.7 1.9 %collective-permute-start.6 = (bf16[2,5,6,16,128]{4,3,2,1,0:T(8,128)(2,1)S(1)}, bf16[2,5,6,16,128]{4,3,2,1,0:T(8,128)(2,1)S(1)}, u32[]{:S(2)}, u32[]{:S(2)}) collective-permute-start(bf16[2,5,6,16,128]{4,3,2,1,0:T(8,128)(2,1)S(1)} %pad_maximum_fusion.2), channel_id=1, source_target_pairs={{0,2},{1,3},{2,0},{3,1},{4,6},{5,7},{6,4},{7,5},{8,10},{9,11},{10,... | collective-permute-start | bytes 737288 | tf_op jit(solution)/shard_map/ppermute | solution.py:237
  17.7 1.6 %collective-permute-start.4 = (bf16[5,6,16,128]{3,2,1,0:T(8,128)(2,1)S(1)}, bf16[5,6,16,128]{3,2,1,0:T(8,128)(2,1)S(1)}, u32[]{:S(2)}, u32[]{:S(2)}) collective-permute-start(bf16[5,6,16,128]{3,2,1,0:T(8,128)(2,1)S(1)} %get-tuple-element.30), channel_id=1, source_target_pairs={{0,10},{1,11},{2,8},{3,9},{4,14},{5,15},{6,12},{7,13},{8,2},{9,3},... | collective-permute-start | bytes 368648 | tf_op jit(solution)/shard_map/ppermute | solution.py:237
  19.3 0.9 %collective-permute-start.3 = (bf16[5,6,16,128]{3,2,1,0:T(8,128)(2,1)S(1)}, bf16[5,6,16,128]{3,2,1,0:T(8,128)(2,1)S(1)}, u32[]{:S(2)}, u32[]{:S(2)}) collective-permute-start(bf16[5,6,16,128]{3,2,1,0:T(8,128)(2,1)S(1)} %get-tuple-element.29), channel_id=1, source_target_pairs={{0,8},{1,9},{2,10},{3,11},{4,12},{5,13},{6,14},{7,15},{8,0},{9,1},... | collective-permute-start | bytes 368648 | tf_op jit(solution)/shard_map/ppermute | solution.py:237
  20.2 3.1 %collective-permute-done.10 = bf16[4,14,16,128]{3,2,1,0:T(8,128)(2,1)S(1)} collective-permute-done((bf16[4,14,16,128]{3,2,1,0:T(8,128)(2,1)S(1)}, bf16[4,14,16,128]{3,2,1,0:T(8,128)(2,1)S(1)}, u32[]{:S(2)}, u32[]{:S(2)}) %collective-permute-start.10) | collective-permute-done | bytes 229408 | tf_op jit(solution)/shard_map/ppermute | solution.py:237
  23.4 1.7 %collective-permute-start.8 = (bf16[1,5,6,16,128]{4,3,2,1,0:T(8,128)(2,1)S(1)}, bf16[1,5,6,16,128]{4,3,2,1,0:T(8,128)(2,1)S(1)}, u32[]{:S(2)}, u32[]{:S(2)}) collective-permute-start(bf16[1,5,6,16,128]{4,3,2,1,0:T(8,128)(2,1)S(1)} %dynamic-slice_bitcast_fusion), channel_id=1, source_target_pairs={{0,2},{1,3},{2,0},{3,1},{4,6},{5,7},{6,4},{7,5},{8,10},{9,11},{10,... | collective-permute-start | bytes 368648 | tf_op jit(solution)/shard_map/ppermute | solution.py:237
  25.1 0.2 shard_map.48.refs_3_
  25.2 1.2 %shard_map.49.refs_5_ = f32[3,6,128,128]{3,2,1,0:T(8,128)S(1)} custom-call(bf16[5,6,16,128]{3,2,1,0:T(8,128)(2,1)S(1)} %get-tuple-element.35.refs_0_, bf16[7,6,16,128]{3,2,1,0:T(8,128)(2,1)S(1)} %collective-permute-done.5.refs_1_, bf16[7,6,16,128]{3,2,1,0:T(8,128)(2,1)S(1)} %collective-permute-done.7.refs_2_, bf16[384,432]{1,0:T(8,128)(2,1)S(1)} %shard_map.48.refs_3_), custom_call_target="tpu_custom_call" | custom-call | flops 1000000 | bytes 10000 | tf_op jit(solution)/shard_map/pallas_call | solution.py:154
  26.5 1.4 %collective-permute-done.6.refs_2_ = bf16[2,5,6,16,128]{4,3,2,1,0:T(8,128)(2,1)S(1)} collective-permute-done((bf16[2,5,6,16,128]{4,3,2,1,0:T(8,128)(2,1)S(1)}, bf16[2,5,6,16,128]{4,3,2,1,0:T(8,128)(2,1)S(1)}, u32[]{:S(2)}, u32[]{:S(2)}) %collective-permute-start.6) | collective-permute-done | bytes 245792 | tf_op jit(solution)/shard_map/ppermute | solution.py:237
  28.0 1.4 %collective-permute-done.11 = bf16[4,14,16,128]{3,2,1,0:T(8,128)(2,1)S(1)} collective-permute-done((bf16[4,14,16,128]{3,2,1,0:T(8,128)(2,1)S(1)}, bf16[4,14,16,128]{3,2,1,0:T(8,128)(2,1)S(1)}, u32[]{:S(2)}, u32[]{:S(2)}) %collective-permute-start.11) | collective-permute-done | bytes 229408 | tf_op jit(solution)/shard_map/ppermute | solution.py:240
  29.4 0.2 shard_map.47.refs_4_
  29.6 0.3 collective-permute-done.8.refs_3_
  29.9 1.2 %shard_map.50.refs_6_ = f32[2,6,128,128]{3,2,1,0:T(8,128)S(1)} custom-call(bf16[5,6,16,128]{3,2,1,0:T(8,128)(2,1)S(1)} %collective-permute-done.3.refs_0_, bf16[1,5,6,16,128]{4,3,2,1,0:T(8,128)(2,1)S(1)} %bitcast.19, bf16[2,5,6,16,128]{4,3,2,1,0:T(8,128)(2,1)S(1)} %collective-permute-done.6.refs_2_, ...), custom_call_target="tpu_custom_call" | custom-call | flops 1000000 | bytes 10000 | tf_op jit(solution)/shard_map/pallas_call | solution.py:154
  31.2 0.8 %shard_map.51.keep_ref = f32[2,6,128,128]{3,2,1,0:T(8,128)S(1)} custom-call(bf16[5,6,16,128]{3,2,1,0:T(8,128)(2,1)S(1)} %collective-permute-done.3.refs_0_, bf16[1,5,6,16,128]{4,3,2,1,0:T(8,128)(2,1)S(1)} %bitcast.20, bf16[2,5,6,16,128]{4,3,2,1,0:T(8,128)(2,1)S(1)} %collective-permute-done.6.refs_2_, ...), custom_call_target="tpu_custom_call" | custom-call | flops 1000000 | bytes 10000 | tf_op jit(solution)/shard_map/pallas_call | solution.py:154
  32.0 1.5 %collective-permute-done.12.came_ref = f32[2,6,128,128]{3,2,1,0:T(8,128)S(1)} collective-permute-done((f32[2,6,128,128]{3,2,1,0:T(8,128)S(1)}, f32[2,6,128,128]{3,2,1,0:T(8,128)S(1)}, u32[]{:S(2)}, u32[]{:S(2)}) %collective-permute-start.12) | collective-permute-done | bytes 786464 | tf_op jit(solution)/shard_map/ppermute | solution.py:237
  33.5 1.8 %shard_map.52 = bf16[2,12,64,256]{3,2,1,0:T(8,128)(2,1)} custom-call(f32[2,6,128,128]{3,2,1,0:T(8,128)S(1)} %shard_map.51.keep_ref, f32[2,6,128,128]{3,2,1,0:T(8,128)S(1)} %collective-permute-done.12.came_ref, bf16[27,64,128]{2,1,0:T(8,128)(2,1)S(1)} %copy-done.2), custom_call_target="tpu_custom_call" | custom-call | flops 1000000000 | bytes 3000000 | tf_op jit(solution)/shard_map/pallas_call | solution.py:217
  (25 shorter events, 0.5 us)
Async XLA Ops:
  0.0 1.1 %copy-start = (bf16[16,27,128]{2,0,1:T(8,128)(2,1)S(1)}, bf16[16,27,128]{2,0,1:T(8,128)(2,1)}, u32[]{:S(2)}) copy-start(bf16[16,27,128]{2,0,1:T(8,128)(2,1)} %param.5) | copy-start | bytes 331780
  0.0 1.0 %copy-start.1 = (bf16[16,16,6,128]{3,1,2,0:T(8,128)(2,1)S(1)}, bf16[16,16,6,128]{3,1,2,0:T(8,128)(2,1)}, u32[]{:S(2)}) copy-start(bf16[16,16,6,128]{3,1,2,0:T(8,128)(2,1)} %param.4) | copy-start | bytes 1179652
  1.1 9.5 %collective-permute-start.2 = (bf16[14,16,128]{2,1,0:T(8,128)(2,1)S(1)}, bf16[14,16,128]{2,1,0:T(8,128)(2,1)S(1)}, u32[]{:S(2)}, u32[]{:S(2)}) collective-permute-start(bf16[14,16,128]{2,1,0:T(8,128)(2,1)S(1)} %dynamic-slice_bitcast_fusion.2), channel_id=1, source_target_pairs={{0,12},{1,13},{2,14},{3,15},{4,8},{5,9},{6,10},{7,11},{8,4},{9,5},... | collective-permute-start | bytes 172040 | tf_op jit(solution)/shard_map/ppermute | solution.py:237
  6.2 5.6 %collective-permute-start.1 = (bf16[14,16,128]{2,1,0:T(8,128)(2,1)S(1)}, bf16[14,16,128]{2,1,0:T(8,128)(2,1)S(1)}, u32[]{:S(2)}, u32[]{:S(2)}) collective-permute-start(bf16[14,16,128]{2,1,0:T(8,128)(2,1)S(1)} %dynamic-slice_bitcast_fusion.2), channel_id=1, source_target_pairs={{0,8},{1,9},{2,10},{3,11},{4,12},{5,13},{6,14},{7,15},{8,0},{9,1},... | collective-permute-start | bytes 172040 | tf_op jit(solution)/shard_map/ppermute | solution.py:237
  6.2 5.8 %collective-permute-start = (bf16[14,16,128]{2,1,0:T(8,128)(2,1)S(1)}, bf16[14,16,128]{2,1,0:T(8,128)(2,1)S(1)}, u32[]{:S(2)}, u32[]{:S(2)}) collective-permute-start(bf16[14,16,128]{2,1,0:T(8,128)(2,1)S(1)} %dynamic-slice_bitcast_fusion.2), channel_id=1, source_target_pairs={{0,4},{1,5},{2,6},{3,7},{4,0},{5,1},{6,2},{7,3},{8,12},{9,13},{10,... | collective-permute-start | bytes 172040 | tf_op jit(solution)/shard_map/ppermute | solution.py:237
  6.9 8.8 %collective-permute-start.5 = (bf16[7,6,16,128]{3,2,1,0:T(8,128)(2,1)S(1)}, bf16[7,6,16,128]{3,2,1,0:T(8,128)(2,1)S(1)}, u32[]{:S(2)}, u32[]{:S(2)}) collective-permute-start(bf16[7,6,16,128]{3,2,1,0:T(8,128)(2,1)S(1)} %get-tuple-element.32), channel_id=1, source_target_pairs={{0,4},{1,5},{2,6},{3,7},{4,0},{5,1},{6,2},{7,3},{8,12},{9,13},{10,... | collective-permute-start | bytes 516104 | tf_op jit(solution)/shard_map/ppermute | solution.py:237
  8.3 11.0 %collective-permute-start.7 = (bf16[7,6,16,128]{3,2,1,0:T(8,128)(2,1)S(1)}, bf16[7,6,16,128]{3,2,1,0:T(8,128)(2,1)S(1)}, u32[]{:S(2)}, u32[]{:S(2)}) collective-permute-start(bf16[7,6,16,128]{3,2,1,0:T(8,128)(2,1)S(1)} %get-tuple-element.34), channel_id=1, source_target_pairs={{0,12},{1,13},{2,14},{3,15},{4,8},{5,9},{6,10},{7,11},{8,4},{9,5},... | collective-permute-start | bytes 516104 | tf_op jit(solution)/shard_map/ppermute | solution.py:237
  12.0 11.3 %collective-permute-start.9 = (bf16[4,14,16,128]{3,2,1,0:T(8,128)(2,1)S(1)}, bf16[4,14,16,128]{3,2,1,0:T(8,128)(2,1)S(1)}, u32[]{:S(2)}, u32[]{:S(2)}) collective-permute-start(bf16[4,14,16,128]{3,2,1,0:T(8,128)(2,1)S(1)} %get-tuple-element.38), channel_id=1, source_target_pairs={{0,16},{16,0},{1,17},{17,1},{2,18},{18,2},{3,19},{19,3},{4,20},{20... | collective-permute-start | bytes 688136 | tf_op jit(solution)/shard_map/ppermute | solution.py:240
  13.6 9.7 %collective-permute-start.10 = (bf16[4,14,16,128]{3,2,1,0:T(8,128)(2,1)S(1)}, bf16[4,14,16,128]{3,2,1,0:T(8,128)(2,1)S(1)}, u32[]{:S(2)}, u32[]{:S(2)}) collective-permute-start(bf16[4,14,16,128]{3,2,1,0:T(8,128)(2,1)S(1)} %get-tuple-element.38), channel_id=1, source_target_pairs={{0,2},{1,3},{2,0},{3,1},{4,6},{5,7},{6,4},{7,5},{8,10},{9,11},{10,... | collective-permute-start | bytes 688136 | tf_op jit(solution)/shard_map/ppermute | solution.py:237
  15.7 12.2 %collective-permute-start.6 = (bf16[2,5,6,16,128]{4,3,2,1,0:T(8,128)(2,1)S(1)}, bf16[2,5,6,16,128]{4,3,2,1,0:T(8,128)(2,1)S(1)}, u32[]{:S(2)}, u32[]{:S(2)}) collective-permute-start(bf16[2,5,6,16,128]{4,3,2,1,0:T(8,128)(2,1)S(1)} %pad_maximum_fusion.2), channel_id=1, source_target_pairs={{0,2},{1,3},{2,0},{3,1},{4,6},{5,7},{6,4},{7,5},{8,10},{9,11},{10,... | collective-permute-start | bytes 737288 | tf_op jit(solution)/shard_map/ppermute | solution.py:237
  17.7 11.9 %collective-permute-start.4 = (bf16[5,6,16,128]{3,2,1,0:T(8,128)(2,1)S(1)}, bf16[5,6,16,128]{3,2,1,0:T(8,128)(2,1)S(1)}, u32[]{:S(2)}, u32[]{:S(2)}) collective-permute-start(bf16[5,6,16,128]{3,2,1,0:T(8,128)(2,1)S(1)} %get-tuple-element.30), channel_id=1, source_target_pairs={{0,10},{1,11},{2,8},{3,9},{4,14},{5,15},{6,12},{7,13},{8,2},{9,3},... | collective-permute-start | bytes 368648 | tf_op jit(solution)/shard_map/ppermute | solution.py:237
  19.3 10.3 %collective-permute-start.3 = (bf16[5,6,16,128]{3,2,1,0:T(8,128)(2,1)S(1)}, bf16[5,6,16,128]{3,2,1,0:T(8,128)(2,1)S(1)}, u32[]{:S(2)}, u32[]{:S(2)}) collective-permute-start(bf16[5,6,16,128]{3,2,1,0:T(8,128)(2,1)S(1)} %get-tuple-element.29), channel_id=1, source_target_pairs={{0,8},{1,9},{2,10},{3,11},{4,12},{5,13},{6,14},{7,15},{8,0},{9,1},... | collective-permute-start | bytes 368648 | tf_op jit(solution)/shard_map/ppermute | solution.py:237
  23.3 6.0 %collective-permute-start.11 = (bf16[4,14,16,128]{3,2,1,0:T(8,128)(2,1)S(1)}, bf16[4,14,16,128]{3,2,1,0:T(8,128)(2,1)S(1)}, u32[]{:S(2)}, u32[]{:S(2)}) collective-permute-start(bf16[4,14,16,128]{3,2,1,0:T(8,128)(2,1)S(1)} %collective-permute-done.10), channel_id=1, source_target_pairs={{0,16},{16,0},{1,17},{17,1},{2,18},{18,2},{3,19},{19,3},{4,20},{20... | collective-permute-start | bytes 688136 | tf_op jit(solution)/shard_map/ppermute | solution.py:240
  23.4 6.6 %collective-permute-start.8 = (bf16[1,5,6,16,128]{4,3,2,1,0:T(8,128)(2,1)S(1)}, bf16[1,5,6,16,128]{4,3,2,1,0:T(8,128)(2,1)S(1)}, u32[]{:S(2)}, u32[]{:S(2)}) collective-permute-start(bf16[1,5,6,16,128]{4,3,2,1,0:T(8,128)(2,1)S(1)} %dynamic-slice_bitcast_fusion), channel_id=1, source_target_pairs={{0,2},{1,3},{2,0},{3,1},{4,6},{5,7},{6,4},{7,5},{8,10},{9,11},{10,... | collective-permute-start | bytes 368648 | tf_op jit(solution)/shard_map/ppermute | solution.py:237
  25.2 2.7 %copy-start.3 = (f32[128]{0:T(128)S(1)}, f32[128]{0:T(128)}, u32[]{:S(2)}) copy-start(f32[128]{0:T(128)} %param.6) | copy-start | bytes 1540
  31.1 2.4 %copy-start.2 = (bf16[27,64,128]{2,1,0:T(8,128)(2,1)S(1)}, bf16[27,64,128]{2,1,0:T(8,128)(2,1)}, u32[]{:S(2)}) copy-start(bf16[27,64,128]{2,1,0:T(8,128)(2,1)} %up_ref.1) | copy-start | bytes 1327108
  31.2 2.4 %collective-permute-start.12 = (f32[2,6,128,128]{3,2,1,0:T(8,128)S(1)}, f32[2,6,128,128]{3,2,1,0:T(8,128)S(1)}, u32[]{:S(2)}, u32[]{:S(2)}) collective-permute-start(f32[2,6,128,128]{3,2,1,0:T(8,128)S(1)} %shard_map.50.refs_6_), channel_id=1, source_target_pairs={{0,1},{1,0},{2,3},{3,2},{4,5},{5,4},{6,7},{7,6},{8,9},{9,8},{10,11... | collective-permute-start | bytes 2359304 | tf_op jit(solution)/shard_map/ppermute | solution.py:237
